TPU v7x, 32 devices: a whole 2x2x4 slice. The times are simulated.
32 devices in a mesh: dp: 4 (over y, x), seq: 8 (over z, core).
Axes of the slice: x: 2, y: 2, z: 4, core: 2. Of those that a mesh axis runs over, the one named last changes fastest.
Arguments:
- video: bfloat16 [4, 8, 16, 160, 256], P('dp', 'seq'), may hold values from -6 to 6
- cotangent: bfloat16 [4, 8, 16, 160, 256], P('dp', 'seq'), may hold values from -6 to 6
- spatial_weight: bfloat16 [3, 3, 256, 256], replicated, may hold values from -0.125 to 0.125
- temporal_weight: bfloat16 [3, 256, 256], replicated, may hold values from -0.21875 to 0.21875
Outputs:
- video_grad: bfloat16 [4, 8, 16, 160, 256], P('dp', 'seq')
- spatial_grad: float32 [2304, 256], P('seq')
- temporal_grad: float32 [768, 256], P('seq')
All inputs are finite; a program needn't handle non-finite values.
Results may differ from a plain program's by a relative error of at most 0.0054.
Values may be sent and summed in bfloat16 or wider, within the bound.
No kernel may reach another device: no remote copies, remote signals or barrier semaphores. Data moves between devices by JAX's collectives and lax.ppermute only.
A program may use at most 128 MiB of HBM per device.

v0:
```python
import jax
import jax.numpy as jnp
from jax import lax
from jax.sharding import PartitionSpec as P


def reduce_grads(partial_sum):
    whole = lax.psum(partial_sum, "dp")
    return lax.psum_scatter(whole, "seq", scatter_dimension=0, tiled=True)


def shards(video, cotangent, spatial_weight, temporal_weight):
    height, width, chans = (video.shape[2], video.shape[3], video.shape[4])
    positions = height * width
    frame = video[0, 0]
    padded = jnp.pad(frame, ((1, 1), (1, 1), (0, 0)))
    hidden = jnp.zeros((height, width, chans), jnp.float32)
    for a in range(3):
        for b in range(3):
            hidden = hidden + jnp.einsum(
                "hwc,cd->hwd",
                padded[a : a + height, b : b + width],
                spatial_weight[a, b],
                preferred_element_type=jnp.float32,
            )
    hidden_low = hidden.astype(jnp.bfloat16)
    grad_flat = cotangent[0, 0].reshape(1, positions, chans)
    hidden_flat = hidden_low.reshape(1, positions, chans)
    total_count = lax.axis_size("dp") * video.shape[0] * lax.axis_size("seq") * positions
    scale = 1.0 / jnp.sqrt(jnp.float32(total_count))
    grad_rows, hidden_rows = (
        lax.all_to_all(grad_flat, "seq", split_axis=1, concat_axis=0, tiled=True),
        lax.all_to_all(hidden_flat, "seq", split_axis=1, concat_axis=0, tiled=True),
    )
    frames = grad_rows.shape[0]
    hid32 = hidden_rows.astype(jnp.float32)
    sig = jax.nn.sigmoid(hid32)
    act = (hid32 * sig).astype(jnp.bfloat16)
    grad_pad = jnp.pad(grad_rows, ((0, 2), (0, 0), (0, 0)))
    act_grad = jnp.zeros(hid32.shape, jnp.float32)
    taps = []
    for k in range(3):
        act_grad = act_grad + jnp.einsum(
            "tqd,cd->tqc",
            grad_pad[k : k + frames],
            temporal_weight[k],
            preferred_element_type=jnp.float32,
        )
        taps.append(
            jnp.einsum(
                "tqc,tqd->cd", act[: frames - k], grad_rows[k:], preferred_element_type=jnp.float32
            )
        )
    temporal_part = jnp.concatenate(taps, axis=0)
    grad_rows_h = (act_grad * sig * (1.0 + hid32 * (1.0 - sig))).astype(jnp.bfloat16)
    back_flat = lax.all_to_all(grad_rows_h, "seq", split_axis=0, concat_axis=1, tiled=True)
    hidden_grad = back_flat.reshape(height, width, chans)
    temporal_grad = reduce_grads(temporal_part) * scale
    grad_pad2 = jnp.pad(hidden_grad, ((1, 1), (1, 1), (0, 0)))
    back = jnp.zeros((height, width, chans), jnp.float32)
    parts = []
    for a in range(3):
        for b in range(3):
            back = back + jnp.einsum(
                "hwd,cd->hwc",
                grad_pad2[2 - a : 2 - a + height, 2 - b : 2 - b + width],
                spatial_weight[a, b],
                preferred_element_type=jnp.float32,
            )
            parts.append(
                jnp.einsum(
                    "hwc,hwd->cd",
                    padded[a : a + height, b : b + width],
                    hidden_grad,
                    preferred_element_type=jnp.float32,
                )
            )
    spatial_grad = reduce_grads(jnp.concatenate(parts, axis=0)) * scale
    video_grad = back.astype(jnp.bfloat16).reshape(video.shape)
    return (video_grad, spatial_grad, temporal_grad)


def solution(mesh):
    placed = (P("dp", "seq", None, None, None), P("dp", "seq", None, None, None), P(), P())
    return jax.shard_map(
        shards,
        mesh=mesh,
        in_specs=placed,
        out_specs=(P("dp", "seq", None, None, None), P("seq", None), P("seq", None)),
        check_vma=False,
    )
```

profile of v0, /device:TPU:0, one launch (start us, length us, event | category | flops | bytes accessed | tf_op | source)
XLA Modules:
  0.0 268.2 jit_solution(10674403140662033116)
XLA Ops:
  7.2 4.1 %copy.19 = bf16[1,2560,256]{2,0,1:T(2,128)(2,1)S(1)} copy(bf16[1,2560,256]{2,1,0:T(8,128)(2,1)} %bitcast.209) | data formatting | bytes 2621440 | tf_op jit(solution)/shard_map/reshape;squeeze | solution.py:27
  11.8 14.1 %reduce.1 = bf16[2560,256]{1,0:T(8,128)(2,1)} reduce(bf16[2560,1,256]{2,1,0:T(2,128)(2,1)S(1)} %bitcast.204, bf16[]{:T(256)} %broadcast.12), dimensions={1}, to_apply=%bitcast.159.reduce_sub_computation | reduce | bytes 2621442
  25.9 4.2 %reshape.59 = bf16[8,2,40960]{2,1,0:T(2,128)(2,1)} reshape(bf16[2560,256]{1,0:T(8,128)(2,1)} %reduce.1) | data formatting | bytes 2621440
  30.1 6.5 %all-to-all-start = ((bf16[8,2,40960]{2,1,0:T(2,128)(2,1)}), bf16[8,2,40960]{2,1,0:T(2,128)(2,1)}, u32[]{:S(2)}, u32[]{:S(2)}) async-start(bf16[8,2,40960]{2,1,0:T(2,128)(2,1)} %reshape.59), calls=%async_computation | async-start | bytes 2621440 | tf_op jit(solution)/shard_map/all_to_all | solution.py:32
  40.6 2.2 add_convert_fusion.1
  42.9 16.0 %copy.18 = bf16[1,2560,256]{2,0,1:T(2,128)(2,1)} copy(bf16[1,2560,256]{2,1,0:T(8,128)(2,1)S(1)} %bitcast.206) | data formatting | bytes 2621440 | tf_op jit(solution)/shard_map/reshape | solution.py:28
  58.8 14.1 %reduce = bf16[2560,256]{1,0:T(8,128)(2,1)S(1)} reduce(bf16[2560,1,256]{2,1,0:T(2,128)(2,1)} %bitcast.205, bf16[]{:T(256)} %broadcast.12), dimensions={1}, to_apply=%bitcast.158.reduce_sub_computation | reduce | bytes 2621442
  74.2 5.1 %all-to-all-start.1 = ((bf16[8,2,40960]{2,1,0:T(2,128)(2,1)}), bf16[8,2,40960]{2,1,0:T(2,128)(2,1)}, u32[]{:S(2)}, u32[]{:S(2)}) async-start(bf16[8,2,40960]{2,1,0:T(2,128)(2,1)} %reshape.57), calls=%async_computation.1 | async-start | bytes 2621440 | tf_op jit(solution)/shard_map/all_to_all | solution.py:33
  79.3 6.0 %reshape.60 = bf16[2560,1,256]{2,1,0:T(2,128)(2,1)} reshape(bf16[8,2,40960]{2,1,0:T(2,128)(2,1)} %all-to-all-done) | data formatting | bytes 2621440
  89.4 2.0 fusion.95
  91.4 20.2 %all-to-all-done.1 = bf16[8,2,40960]{2,1,0:T(2,128)(2,1)} async-done(((bf16[8,2,40960]{2,1,0:T(2,128)(2,1)}), bf16[8,2,40960]{2,1,0:T(2,128)(2,1)}, u32[]{:S(2)}, u32[]{:S(2)}) %all-to-all-start.1) | async-done | bytes 1310752 | tf_op jit(solution)/shard_map/all_to_all | solution.py:33
  111.6 6.1 %reshape.58 = bf16[2560,1,256]{2,1,0:T(2,128)(2,1)} reshape(bf16[8,2,40960]{2,1,0:T(2,128)(2,1)} %all-to-all-done.1) | data formatting | bytes 2621440
  117.7 2.1 copy.13
  121.7 2.3 multiply_convert_fusion.1
  124.0 3.6 %all-to-all-start.2 = ((bf16[8,320,256]{2,1,0:T(8,128)(2,1)}), bf16[8,320,256]{2,1,0:T(8,128)(2,1)S(1)}, u32[]{:S(2)}, u32[]{:S(2)}) async-start(bf16[8,320,256]{2,1,0:T(8,128)(2,1)} %multiply_convert_fusion.1), calls=%async_computation.2 | async-start | bytes 2621440 | tf_op jit(solution)/shard_map/all_to_all | solution.py:56
  127.6 4.1 %slice.165 = bf16[1,2240,256]{2,0,1:T(2,128)(2,1)S(1)} slice(bf16[1,2560,256]{2,0,1:T(2,128)(2,1)} %bitcast.195), slice={[0:1], [320:2560], [0:256]} | slice | bytes 2293760 | tf_op jit(solution)/shard_map/slice | solution.py:51
  131.7 2.1 slice.166
  139.9 24.0 %all-to-all-done.2 = bf16[8,320,256]{2,1,0:T(8,128)(2,1)S(1)} async-done(((bf16[8,320,256]{2,1,0:T(8,128)(2,1)}), bf16[8,320,256]{2,1,0:T(8,128)(2,1)S(1)}, u32[]{:S(2)}, u32[]{:S(2)}) %all-to-all-start.2) | async-done | bytes 1310752 | tf_op jit(solution)/shard_map/all_to_all | solution.py:56
  184.6 2.1 fusion.4
  188.6 2.1 fusion.8
  190.8 2.1 fusion.82
  192.8 18.9 %reduce-scatter.3.cloned.1.call-done = f32[288,256]{1,0:T(8,128)} async-done(((f32[2304,256]{1,0:T(8,128)}), f32[288,256]{1,0:T(8,128)}) %reduce-scatter.3.cloned.1.call-update) | async-done | bytes 294928 | tf_op jit(solution)/shard_map/reduce_scatter | solution.py:9
  211.7 9.3 %fusion = bf16[1,1,16,160,256]{4,3,2,1,0:T(8,128)(2,1)} fusion(f32[16,160,256]{2,1,0:T(8,128)} %fusion.2, f32[16,160,256]{2,1,0:T(8,128)} %fusion.4, f32[16,160,256]{2,1,0:T(8,128)} %fusion.6, f32[16,160,256]{2,1,0:T(8,128)} %fusion.82, f32[16,160,256]{2,1,0:T(8,128)} %fusion.8, f32[16,160,256]{2,1,0:T(8,128)} %fusion.10, f32[16,160,256]{2,1,0:T(8,128)} %fusion.14, ...), kind=kOutput, calls=%fused_computation.5 | convolution fusion | flops 341442560 | bytes 23724032 | tf_op jit(solution)/shard_map/hwd,cd->hwc/dot_general | solution.py:64
  221.0 37.5 %all-reduce.6.cloned.1.call-done = (f32[288,256]{1,0:T(8,128)}, f32[96,256]{1,0:T(8,128)}) async-done(((f32[288,256]{1,0:T(8,128)}, f32[96,256]{1,0:T(8,128)}), (f32[288,256]{1,0:T(8,128)}, f32[96,256]{1,0:T(8,128)})) %all-reduce.6.cloned.1.call-update) | async-done | bytes 393232 | tf_op jit(solution)/shard_map/psum | solution.py:8
  (65 shorter events, 43.7 us)
Async XLA Ops:
  30.1 6.5 %copy-start = (bf16[1,1,16,160,256]{4,3,2,1,0:T(8,128)(2,1)S(1)}, bf16[1,1,16,160,256]{4,3,2,1,0:T(8,128)(2,1)}, u32[]{:S(2)}) copy-start(bf16[1,1,16,160,256]{4,3,2,1,0:T(8,128)(2,1)} %param.4) | copy-start | bytes 3932164
  30.1 6.5 %copy-start.6 = (bf16[3,3,256,256]{3,2,1,0:T(8,128)(2,1)S(1)}, bf16[3,3,256,256]{3,2,1,0:T(8,128)(2,1)}, u32[]{:S(2)}) copy-start(bf16[3,3,256,256]{3,2,1,0:T(8,128)(2,1)} %param.6) | copy-start | bytes 3538948
  30.1 44.1 %all-to-all-start = ((bf16[8,2,40960]{2,1,0:T(2,128)(2,1)}), bf16[8,2,40960]{2,1,0:T(2,128)(2,1)}, u32[]{:S(2)}, u32[]{:S(2)}) async-start(bf16[8,2,40960]{2,1,0:T(2,128)(2,1)} %reshape.59), calls=%async_computation | async-start | bytes 2621440 | tf_op jit(solution)/shard_map/all_to_all | solution.py:32
  74.2 37.4 %all-to-all-start.1 = ((bf16[8,2,40960]{2,1,0:T(2,128)(2,1)}), bf16[8,2,40960]{2,1,0:T(2,128)(2,1)}, u32[]{:S(2)}, u32[]{:S(2)}) async-start(bf16[8,2,40960]{2,1,0:T(2,128)(2,1)} %reshape.57), calls=%async_computation.1 | async-start | bytes 2621440 | tf_op jit(solution)/shard_map/all_to_all | solution.py:33
  85.3 2.0 copy-start.10
  87.3 32.4 %copy-start.2 = (bf16[1,2560,256]{2,1,0:T(8,128)(2,1)}, bf16[1,2560,256]{2,1,0:T(8,128)(2,1)S(1)}, u32[]{:S(2)}) copy-start(bf16[1,2560,256]{2,1,0:T(8,128)(2,1)S(1)} %copy.12) | copy-start | bytes 3932164
  117.7 3.6 %copy-start.8 = (f32[8,320,256]{2,1,0:T(8,128)S(1)}, f32[8,320,256]{2,1,0:T(8,128)}, u32[]{:S(2)}) copy-start(f32[8,320,256]{2,1,0:T(8,128)} %fusion.93) | copy-start | bytes 7864324
  117.7 4.0 %copy-start.9 = (f32[8,320,256]{2,1,0:T(8,128)S(1)}, f32[8,320,256]{2,1,0:T(8,128)}, u32[]{:S(2)}) copy-start(f32[8,320,256]{2,1,0:T(8,128)} %fusion.95) | copy-start | bytes 7864324
  119.8 1.6 copy-start.4
  124.0 39.9 %all-to-all-start.2 = ((bf16[8,320,256]{2,1,0:T(8,128)(2,1)}), bf16[8,320,256]{2,1,0:T(8,128)(2,1)S(1)}, u32[]{:S(2)}, u32[]{:S(2)}) async-start(bf16[8,320,256]{2,1,0:T(8,128)(2,1)} %multiply_convert_fusion.1), calls=%async_computation.2 | async-start | bytes 2621440 | tf_op jit(solution)/shard_map/all_to_all | solution.py:56
  127.5 65.3 %reduce-scatter.5.cloned.1.call-start = ((), (), s32[]{:S(2)}) async-start(), calls=%async_computation.6 | async-start | bytes 884736 | tf_op jit(solution)/shard_map/reduce_scatter | solution.py:9
  127.6 4.1 %copy-start.1 = (bf16[2560,1,256]{2,1,0:T(2,128)(2,1)S(1)}, bf16[2560,1,256]{2,1,0:T(2,128)(2,1)}, u32[]{:S(2)}) copy-start(bf16[2560,1,256]{2,1,0:T(2,128)(2,1)} %reshape.60) | copy-start | bytes 3932164
  134.1 1.7 copy-start.5
  137.0 1.3 copy-start.3
  139.8 71.8 %reduce-scatter.3.cloned.1.call-start = ((), (), s32[]{:S(2)}) async-start(), calls=%async_computation.5 | async-start | bytes 2654208 | tf_op jit(solution)/shard_map/reduce_scatter | solution.py:9
  175.2 1.3 copy-start.7
  175.2 83.3 %all-reduce.6.cloned.1.call-start = ((), (), s32[]{:S(2)}) async-start(), calls=%async_computation.7 | async-start | bytes 786432 | tf_op jit(solution)/shard_map/psum | solution.py:8
Sparse Core Ops, SparseCore 0:
  140.0 34.0 reduce-scatter.4
  176.5 35.1 reduce-scatter.2
  214.9 43.4 all-reduce.5
where the time goes:
time: 269 us; the launch traced here: 268 us
  waiting for transfers between devices  101 us (38%)
  local copies, waits for them, and re-layouts  54 us (20%)
  matrix products  51.1 us (19%)
  other arithmetic  33.2 us (12%)
  starting transfers between devices  15.5 us (6%)
  between operations  13.9 us (5%)
    psum x1, waiting for transfers between devices, reduce_grads(): whole = lax.psum(partial_sum, 'dp')  37.5 us
    unnamed x2, other arithmetic  28.3 us
    unnamed x31, local copies, waits for them, and re-layouts  27.7 us
    dot_general x9, matrix products, shards(): jnp.einsum('hwd,cd->hwc', grad_pad2[2 - a:2 - a + height, 2 - b:2 - b + w...  25.7 us
    all_to_all x1, waiting for transfers between devices, shards(): lax.all_to_all(grad_rows_h, 'seq', split_axis=0, concat_axis=1, tiled=True)  24 us
    all_to_all x1, waiting for transfers between devices, shards(): lax.all_to_all(hidden_flat, 'seq', split_axis=1, concat_axis=0, tiled=True)  20.2 us
    reduce_scatter x2, waiting for transfers between devices, reduce_grads(): return lax.psum_scatter(whole, 'seq', scatter_dimension=0, tiled=True)  18.9 us
    reshape x1, local copies, waits for them, and re-layouts, shards(): hidden_flat = hidden_low.reshape(1, positions, chans)  16 us
  transfers between devices with their start and end apart: 6, of which 4 were waited for; matrix products, arithmetic and copies ran while one was open for 36% of the time, Pallas kernels for 0%

commit v1 on v0

v1 whole, which is shorter than its diff:
```python
import functools

import jax
import jax.numpy as jnp
from jax import lax
from jax.experimental import pallas as pl
from jax.experimental.pallas import tpu as pltpu
from jax.sharding import PartitionSpec as P

BF16, F32 = jnp.bfloat16, jnp.float32
VM = pl.BlockSpec(memory_space=pltpu.VMEM)
SM = pl.BlockSpec(memory_space=pltpu.SMEM)


def dot(a, b):
    return jnp.dot(a, b, preferred_element_type=F32)


def dot_rt(a, b):
    return lax.dot_general(a, b, (((1,), (1,)), ((), ())), preferred_element_type=F32)


def dot_lt(a, b):
    return lax.dot_general(a, b, (((0,), (0,)), ((), ())), preferred_element_type=F32)


def call(kernel, name, outs, smem, flops, *args, scratch=()):
    nbytes = sum(a.size * a.dtype.itemsize for a in (*args, *outs))
    return pl.pallas_call(
        kernel,
        out_shape=outs,
        in_specs=[SM] * smem + [VM] * (len(args) - smem),
        out_specs=[VM] * len(outs),
        scratch_shapes=[pltpu.VMEM(shape, dtype) for shape, dtype in scratch],
        compiler_params=pltpu.CompilerParams(vmem_limit_bytes=40 * 2**20),
        cost_estimate=pl.CostEstimate(flops=flops, bytes_accessed=nbytes, transcendentals=0),
        name=name,
    )(*args)


def tile(i, size):
    return pl.ds(pl.multiple_of(i * size, size), size)


def side_shifts(rows, width):
    n, chans = rows.shape
    wide = rows.astype(F32)
    column = lax.rem(lax.broadcasted_iota(jnp.int32, (n, chans), 0), width)
    left = jnp.where(column == 0, 0.0, pltpu.roll(wide, 1, 0))
    right = jnp.where(column == width - 1, 0.0, pltpu.roll(wide, n - 1, 0))
    return left.astype(BF16), right.astype(BF16)


def put_cat(cat, where, first, mid, last):
    chans = mid.shape[1]
    cat[where, :chans] = first
    cat[where, chans : 2 * chans] = mid
    cat[where, 2 * chans :] = last


def silu_parts(v):
    v = v.astype(F32)
    sig = 1.0 / (1.0 + jnp.exp(-v))
    return (v * sig).astype(BF16), sig * (1.0 + v * (1.0 - sig))


def conv_rows(cat, weight, out, rows, step, width):
    def body(i, carry):
        start = i * step
        acc = dot(cat[pl.ds(pl.multiple_of(start, width), step)], weight[0])
        for a in (1, 2):
            acc += dot(cat[pl.ds(pl.multiple_of(start + a * width, width), step)], weight[a])
        out[pl.ds(pl.multiple_of(start, width), step)] = acc.astype(BF16)
        return carry

    lax.fori_loop(0, rows // step, body, 0)


def hidden_kernel(width, video, weight, hidden, cat):
    rows = video.shape[0]
    chans3 = cat.shape[1]
    cat[:width] = jnp.zeros((width, chans3), BF16)
    cat[rows + width :] = jnp.zeros((width, chans3), BF16)

    def build(i, carry):
        mid = video[tile(i, 2 * width)]
        left, right = side_shifts(mid, width)
        put_cat(cat, pl.ds(pl.multiple_of(i * 2 * width + width, width), 2 * width), left, mid, right)
        return carry

    lax.fori_loop(0, rows // (2 * width), build, 0)
    conv_rows(cat, weight, hidden, rows, rows // 2, width)


def add_taps(total, video, cat, first, last, base, height, width):
    chans = video.shape[1]
    for a in range(3):
        low, high = max(first, 1 - a), min(last, height + 1 - a)
        rows = video[(low + a - 1 - base) * width : (high + a - 1 - base) * width]
        part = dot_lt(rows, cat[(low - first) * width : (high - first) * width])
        for b in range(3):
            total[3 * a + b] += part[:, b * chans : (b + 1) * chans]


def local_kernel(height, width, core, video, hidden, cot, mate, tw, rest, spatial, temporal, act, cat):
    rows, chans = video.shape
    half = rows // 2
    step = 2 * width
    even = core[0] == 0
    tap1 = jnp.where(even, tw[1], jnp.zeros_like(tw[1]))

    def top(i, carry):
        act[tile(i, step)] = silu_parts(hidden[tile(i, step)])[0]
        return carry

    def bottom(i, carry):
        here = pl.ds(pl.multiple_of(half + i * step, width), step)
        act_rows, slope = silu_parts(hidden[here])
        act[here] = act_rows
        grad = dot_rt(cot[here], tw[0]) + dot_rt(mate[here], tap1)
        rest[tile(i, step)] = grad
        mid = (grad * slope).astype(BF16)
        left, right = side_shifts(mid, width)
        put_cat(cat, tile(i, step), right, mid, left)
        return carry

    lax.fori_loop(0, half // step, top, 0)
    lax.fori_loop(0, half // step, bottom, 0)
    spatial[...] = jnp.zeros_like(spatial)
    add_taps(spatial, video, cat, height // 2, height, 0, height, width)
    temporal[0] = dot_lt(act[...], cot[...])
    temporal[1] = jnp.where(even, dot_lt(act[...], mate[...]), 0.0)


def halo_kernel(
    height, width, core, video, hidden, cot, mate, near, far, above, sw, tw, spatial, temporal,
    hidden_grad, spatial_out, temporal_out, act, cat, wide, total, other,
):
    rows, chans = video.shape
    half = rows // 2
    step = 2 * width
    even = core[0] == 0
    zero = jnp.zeros_like(tw[1])
    tap1_even = jnp.where(even, tw[1], zero)
    tap1_odd = jnp.where(even, zero, tw[1])

    def own(i, carry):
        here = tile(i, step)
        act_rows, slope = silu_parts(hidden[here])
        act[here] = act_rows
        grad = dot_rt(cot[here], tw[0]) + dot_rt(mate[here], tap1_even)
        grad += dot_rt(near[here], tw[1]) + dot_rt(far[here], tw[2])
        mid = (grad * slope).astype(BF16)
        hidden_grad[here] = mid
        left, right = side_shifts(mid, width)
        put_cat(cat, here, right, mid, left)
        return carry

    lax.fori_loop(0, half // step, own, 0)
    total[...] = spatial[...]
    add_taps(total, video, cat, 0, height // 2, 0, height, width)
    temporal_out[:chans] = temporal[0].astype(BF16)
    tap1 = temporal[1] + dot_lt(act[...], near[...])
    tap2 = dot_lt(act[...], far[...])

    blocks = above.shape[0] // width

    def build(i, carry):
        here = tile(i, width)
        mid = above[here]
        left, right = side_shifts(mid, width)
        put_cat(wide, here, left, mid, right)
        return carry

    lax.fori_loop(0, blocks, build, 0)
    wide[blocks * width :] = jnp.zeros((width, wide.shape[1]), BF16)
    conv_rows(wide, sw, other, half, half, width)

    def remote(i, carry):
        here = tile(i, step)
        there = pl.ds(pl.multiple_of(half + i * step, width), step)
        act_rows, slope = silu_parts(other[here])
        act[here] = act_rows
        grad = dot_rt(cot[there], tw[2]) + dot_rt(mate[there], tap1_odd)
        mid = (grad * slope).astype(BF16)
        left, right = side_shifts(mid, width)
        put_cat(cat, here, right, mid, left)
        return carry

    lax.fori_loop(0, half // step, remote, 0)
    add_taps(total, above, cat, height // 2, height, height // 2 - 1, height, width)
    tap2 += dot_lt(act[...], cot[half:])
    tap1 += jnp.where(even, 0.0, dot_lt(act[...], mate[half:]))
    temporal_out[chans : 2 * chans] = tap1.astype(BF16)
    temporal_out[2 * chans :] = tap2.astype(BF16)
    for tap in range(9):
        spatial_out[tap * chans : (tap + 1) * chans] = total[tap].astype(BF16)


def back_kernel(width, top, hidden, rest, near, far, tw, sw, out, cat):
    half = top.shape[0]
    step = 2 * width
    chans3 = cat.shape[1]
    cat[:width] = jnp.zeros((width, chans3), BF16)
    cat[2 * half + width :] = jnp.zeros((width, chans3), BF16)

    def first(i, carry):
        mid = top[tile(i, step)]
        left, right = side_shifts(mid, width)
        put_cat(cat, pl.ds(pl.multiple_of(width + i * step, width), step), right, mid, left)
        return carry

    def second(i, carry):
        here = tile(i, step)
        slope = silu_parts(hidden[pl.ds(pl.multiple_of(half + i * step, width), step)])[1]
        grad = rest[here] + dot_rt(near[here], tw[1]) + dot_rt(far[here], tw[2])
        mid = (grad * slope).astype(BF16)
        left, right = side_shifts(mid, width)
        put_cat(cat, pl.ds(pl.multiple_of(half + width + i * step, width), step), right, mid, left)
        return carry

    lax.fori_loop(0, half // step, first, 0)
    lax.fori_loop(0, half // step, second, 0)
    conv_rows(cat, sw, out, 2 * half, half, width)


def peer(index, k, size):
    return index ^ k if size & (size - 1) == 0 else (index + k) % size


def reduce_grads(spatial, temporal):
    dp, seq = lax.axis_size("dp"), lax.axis_size("seq")
    levels = seq // 2
    chans = spatial.shape[1]
    q, s = lax.axis_index("dp"), lax.axis_index("seq")
    core, level = s % 2, s // 2
    parts = [g.reshape(levels, 2, dp, -1, chans) for g in (spatial, temporal)]
    split = parts[0].shape[3]
    both = jnp.concatenate(parts, axis=3)
    pick = functools.partial(lax.dynamic_index_in_dim, keepdims=False)
    swapped = lax.ppermute(pick(both, 1 - core, 1), "seq", [(i, i ^ 1) for i in range(seq)])
    mine = (pick(both, core, 1).astype(F32) + swapped.astype(F32)).astype(BF16)
    got = [
        lax.ppermute(pick(mine, peer(q, k, dp), 1), "dp", [(i, peer(i, k, dp)) for i in range(dp)])
        for k in range(1, dp)
    ]
    held = sum((g.astype(F32) for g in got), pick(mine, q, 1).astype(F32)).astype(BF16)
    got = [
        lax.ppermute(
            pick(held, peer(level, k, levels), 0),
            "seq",
            [(i, 2 * peer(i // 2, k, levels) + i % 2) for i in range(seq)],
        )
        for k in range(1, levels)
    ]
    final = sum((g.astype(F32) for g in got), pick(held, level, 0).astype(F32))
    small = final.astype(BF16)
    whole = jnp.zeros((dp, *small.shape), BF16)
    whole = lax.dynamic_update_index_in_dim(whole, small, q, 0)
    for k in range(1, dp):
        part = lax.ppermute(small, "dp", [(peer(i, k, dp), i) for i in range(dp)])
        whole = lax.dynamic_update_index_in_dim(whole, part, peer(q, k, dp), 0)
    whole = whole.astype(F32)
    return whole[:, :split].reshape(-1, chans), whole[:, split:].reshape(-1, chans)


def shards(video, cotangent, spatial_weight, temporal_weight):
    height, width, chans = (video.shape[2], video.shape[3], video.shape[4])
    rows = height * width
    half = rows // 2
    seq = lax.axis_size("seq")
    total_count = lax.axis_size("dp") * video.shape[0] * seq * rows
    scale = 1.0 / jnp.sqrt(jnp.float32(total_count))
    core = (lax.axis_index("seq") % 2).astype(jnp.int32).reshape(1)
    x = video.reshape(rows, chans)
    cot = cotangent.reshape(rows, chans)
    sw = spatial_weight.reshape(3, 3 * chans, chans)
    sw_back = jnp.transpose(spatial_weight[::-1], (0, 1, 3, 2)).reshape(3, 3 * chans, chans)
    down = [(i + 2, i) for i in range(seq - 2)]
    up = [(i, i + 2) for i in range(seq - 2)]
    across = [(i, i + 1) for i in range(0, seq, 2)]
    far_top = lax.ppermute(cot[:half], "seq", down)
    above = lax.ppermute(x[half - width :], "seq", up)
    mate = lax.ppermute(cot, "seq", [(i, i ^ 1) for i in range(seq)])
    far_bottom = lax.ppermute(cot[half:], "seq", down)
    near_top = lax.ppermute(far_top, "seq", across)
    near_bottom = lax.ppermute(far_bottom, "seq", across)

    def array(n, dtype, columns=chans):
        return jax.ShapeDtypeStruct((n, columns), dtype)

    mac = rows * chans * chans
    (hidden,) = call(
        functools.partial(hidden_kernel, width), "hidden", [array(rows, BF16)], 0, 18 * mac, x, sw,
        scratch=[((rows + 2 * width, 3 * chans), BF16)],
    )
    taps9 = jax.ShapeDtypeStruct((9, chans, chans), F32)
    taps2 = jax.ShapeDtypeStruct((2, chans, chans), F32)
    rest, spatial, temporal = call(
        functools.partial(local_kernel, height, width), "local", [array(half, F32), taps9, taps2], 1, 15 * mac,
        core, x, hidden, cot, mate, temporal_weight,
        scratch=[((rows, chans), BF16), ((half, 3 * chans), BF16)],
    )
    top, spatial, temporal = call(
        functools.partial(halo_kernel, height, width), "halo",
        [array(half, BF16), array(9 * chans, BF16), array(3 * chans, BF16)], 1, 38 * mac,
        core, x, hidden, cot, mate, near_top, far_top, above, sw, temporal_weight, spatial, temporal,
        scratch=[
            ((half, chans), BF16), ((half, 3 * chans), BF16), ((half + 2 * width, 3 * chans), BF16),
            (taps9.shape, F32), ((half, chans), BF16),
        ],
    )
    spatial, temporal = reduce_grads(spatial, temporal)
    (back,) = call(
        functools.partial(back_kernel, width), "back", [array(rows, BF16)], 0, 20 * mac,
        top, hidden, rest, near_bottom, far_bottom, temporal_weight, sw_back,
        scratch=[((rows + 2 * width, 3 * chans), BF16)],
    )
    return (back.reshape(video.shape), spatial * scale, temporal * scale)


def solution(mesh):
    placed = (P("dp", "seq", None, None, None), P("dp", "seq", None, None, None), P(), P())
    return jax.shard_map(
        shards,
        mesh=mesh,
        in_specs=placed,
        out_specs=(P("dp", "seq", None, None, None), P("seq", None), P("seq", None)),
        check_vma=False,
    )
```

time: 269 us -> 104 us (0.39)
  waiting for transfers between devices: 101 us -> 29.5 us
  matrix products: 51.1 us -> 0 us
  local copies, waits for them, and re-layouts: 54 us -> 11.1 us
  Pallas kernels: 0 us -> 30.5 us
  other arithmetic: 33.2 us -> 6.62 us
  between operations: 13.9 us -> 0.9 us
  starting transfers between devices: 15.5 us -> 25 us
    dot_general x33 -> x0, matrix products: 51.1 us -> none  [the longest x9 25.7 us: shards(): jnp.einsum('hwd,cd->hwc', grad_pad2[2 - a:2 - a + height, 2 - b:2 - b + w...]
    all_to_all x3 -> x0, waiting for transfers between devices: 44.2 us -> none  [the longest x1 24 us: shards(): lax.all_to_all(grad_rows_h, 'seq', split_axis=0, concat_axis=1, tiled=True)]
    psum x1 -> x0, waiting for transfers between devices: 37.5 us -> none  [reduce_grads(): whole = lax.psum(partial_sum, 'dp')]
    pallas_call x0 -> x4, Pallas kernels: none -> 30.5 us  [call(): pl.pallas_call(kernel, out_shape=outs, in_specs=[SM] * smem + [VM] * (len...]
    ppermute x0 -> x16, waiting for transfers between devices: none -> 29.5 us  [the longest x1 12.5 us: shards(): far_top = lax.ppermute(cot[:half], 'seq', down)]
    unnamed x2 -> x0, other arithmetic: 28.3 us -> none
    ppermute x0 -> x16, starting transfers between devices: none -> 25 us  [the longest x1 5.24 us: shards(): above = lax.ppermute(x[half - width:], 'seq', up)]
    unnamed x31 -> x26, local copies, waits for them, and re-layouts: 27.7 us -> 3.38 us
  transfers between devices with their start and end apart: 6 -> 16, of which waited for: 4 -> 7; matrix products, arithmetic and copies ran while one was open for 36% -> 11% of each run, Pallas kernels for 0% -> 18%
where the time goes in v1:
time: 104 us
  Pallas kernels  30.5 us (29%)
  waiting for transfers between devices  29.5 us (28%)
  starting transfers between devices  25 us (24%)
  local copies, waits for them, and re-layouts  11.1 us (11%)
  other arithmetic  6.62 us (6%)
    pallas_call x4, Pallas kernels, call(): pl.pallas_call(kernel, out_shape=outs, in_specs=[SM] * smem + [VM] * (len...  30.5 us
    ppermute x1, waiting for transfers between devices, shards(): far_top = lax.ppermute(cot[:half], 'seq', down)  12.5 us
    ppermute x1, waiting for transfers between devices, shards(): far_bottom = lax.ppermute(cot[half:], 'seq', down)  9.68 us
    ppermute x1, starting transfers between devices, shards(): above = lax.ppermute(x[half - width:], 'seq', up)  5.24 us
    ppermute x3, waiting for transfers between devices, reduce_grads(): part = lax.ppermute(small, 'dp', [(peer(i, k, dp), i) for i in range(dp)])  4.47 us
    ppermute x3, starting transfers between devices, reduce_grads(): lax.ppermute(pick(held, peer(level, k, levels), 0), 'seq', [(i, 2 * peer(...  4.39 us
    ppermute x3, starting transfers between devices, reduce_grads(): part = lax.ppermute(small, 'dp', [(peer(i, k, dp), i) for i in range(dp)])  3.57 us
    ppermute x3, starting transfers between devices, reduce_grads(): lax.ppermute(pick(mine, peer(q, k, dp), 1), 'dp', [(i, peer(i, k, dp)) fo...  3.55 us
  transfers between devices with their start and end apart: 16, of which 7 were waited for; matrix products, arithmetic and copies ran while one was open for 11% of the time, Pallas kernels for 18%

profile of v1, /device:TPU:0, one launch (start us, length us, event | category | flops | bytes accessed | tf_op | source)
XLA Modules:
  0.0 103.6 jit_solution(17975451948945849339)
XLA Ops:
  1.2 2.2 %fusion.12 = (bf16[1,1,8,160,256]{4,3,2,1,0:T(8,128)(2,1)}, bf16[1,1,8,160,256]{4,3,2,1,0:T(8,128)(2,1)S(1)}) fusion(bf16[1,1,16,160,256]{4,3,2,1,0:T(8,128)(2,1)} %param.5), kind=kLoop, calls=%fused_computation.31 | loop fusion | bytes 2621440 | tf_op jit(solution)/shard_map/slice | solution.py:285
  3.4 1.4 %collective-permute-start.1 = (bf16[1280,256]{1,0:T(8,128)(2,1)S(1)}, bf16[1280,256]{1,0:T(8,128)(2,1)}, u32[]{:S(2)}, u32[]{:S(2)}) collective-permute-start(bf16[1280,256]{1,0:T(8,128)(2,1)S(1)} %bitcast.62), channel_id=1, source_target_pairs={{2,0},{3,1},{4,2},{5,3},{6,4},{7,5},{10,8},{11,9},{12,10},{13,11},... | collective-permute-start | bytes 1966088 | tf_op jit(solution)/shard_map/ppermute | solution.py:282
  5.7 5.2 %collective-permute-start.3 = (bf16[1440,256]{1,0:T(8,128)(2,1)}, bf16[1440,256]{1,0:T(8,128)(2,1)S(1)}, u32[]{:S(2)}, u32[]{:S(2)}) collective-permute-start(bf16[1440,256]{1,0:T(8,128)(2,1)} %bitcast.5), channel_id=1, source_target_pairs={{0,2},{1,3},{2,4},{3,5},{4,6},{5,7},{8,10},{9,11},{10,12},{11,13},... | collective-permute-start | bytes 2211848 | tf_op jit(solution)/shard_map/ppermute | solution.py:283
  11.0 12.5 %collective-permute-done.1.far = bf16[1280,256]{1,0:T(8,128)(2,1)} collective-permute-done((bf16[1280,256]{1,0:T(8,128)(2,1)S(1)}, bf16[1280,256]{1,0:T(8,128)(2,1)}, u32[]{:S(2)}, u32[]{:S(2)}) %collective-permute-start.1) | collective-permute-done | bytes 655392 | tf_op jit(solution)/shard_map/ppermute | solution.py:282
  23.5 2.6 %collective-permute-start.2 = (bf16[1280,256]{1,0:T(8,128)(2,1)}, bf16[1280,256]{1,0:T(8,128)(2,1)}, u32[]{:S(2)}, u32[]{:S(2)}) collective-permute-start(bf16[1280,256]{1,0:T(8,128)(2,1)} %collective-permute-done.1.far), channel_id=1, source_target_pairs={{0,1},{2,3},{4,5},{6,7},{8,9},{10,11},{12,13},{14,15},{16,17},{18,... | collective-permute-start | bytes 1966088 | tf_op jit(solution)/shard_map/ppermute | solution.py:286
  26.1 4.6 %hidden.1 = bf16[2560,256]{1,0:T(8,128)(2,1)S(1)} custom-call(bf16[2560,256]{1,0:T(8,128)(2,1)S(1)} %bitcast.59, bf16[3,768,256]{2,1,0:T(8,128)(2,1)S(1)} %bitcast.56), custom_call_target="tpu_custom_call" | custom-call | flops 3019898880 | bytes 3801088 | tf_op jit(solution)/shard_map/hidden/pallas_call | solution.py:29
  30.7 6.3 %local.1 = (f32[1280,256]{1,0:T(8,128)S(1)}, f32[9,256,256]{2,1,0:T(8,128)S(1)}, f32[2,256,256]{2,1,0:T(8,128)S(1)}) custom-call(s32[1]{0:T(128)} %bitcast.core, bf16[2560,256]{1,0:T(8,128)(2,1)S(1)} %bitcast.60, bf16[2560,256]{1,0:T(8,128)(2,1)S(1)} %hidden.1, bf16[2560,256]{1,0:T(8,128)(2,1)S(1)} %bitcast.54, bf16[2560,256]{1,0:T(8,128)(2,1)} %collective-permute-done.mate, ...), custom_call_target="tpu_custom_call" | custom-call | flops 2516582400 | bytes 9830404 | tf_op jit(solution)/shard_map/local/pallas_call | solution.py:29
  37.1 12.0 %halo.1 = (bf16[1280,256]{1,0:T(8,128)(2,1)S(1)}, bf16[2304,256]{1,0:T(8,128)(2,1)S(1)}, bf16[768,256]{1,0:T(8,128)(2,1)S(1)}) custom-call(s32[1]{0:T(128)} %bitcast.core, bf16[2560,256]{1,0:T(8,128)(2,1)S(1)} %bitcast.61, bf16[2560,256]{1,0:T(8,128)(2,1)S(1)} %hidden.1, bf16[2560,256]{1,0:T(8,128)(2,1)S(1)} %bitcast.55, ...), custom_call_target="tpu_custom_call" | custom-call | flops 6375342080 | bytes 13975556 | tf_op jit(solution)/shard_map/halo/pallas_call | solution.py:29
  52.8 2.2 %fusion = bf16[4,4,96,256]{3,2,1,0:T(8,128)(2,1)} fusion(bf16[4,4,96,256]{3,2,1,0:T(8,128)(2,1)} %collective-permute-done.6, s32[]{:T(128)S(6)} %select_n.52, bf16[4,2,4,72,256]{4,3,2,1,0:T(8,128)(2,1)S(1)} %bitcast.50, bf16[4,2,4,24,256]{4,3,2,1,0:T(8,128)(2,1)S(1)} %bitcast.52), kind=kLoop, calls=%fused_computation.5 | loop fusion | flops 3145728 | bytes 3145732 | tf_op jit(solution)/shard_map/convert_element_type | solution.py:242
  56.2 1.6 %collective-permute-start.7 = (bf16[4,96,256]{2,1,0:T(8,128)(2,1)S(1)}, bf16[4,96,256]{2,1,0:T(8,128)(2,1)S(1)}, u32[]{:S(2)}, u32[]{:S(2)}) collective-permute-start(bf16[4,96,256]{2,1,0:T(8,128)(2,1)S(1)} %get-tuple-element.19), channel_id=1, source_target_pairs={{0,8},{8,0},{16,24},{24,16},{1,9},{9,1},{17,25},{25,17},{2,10},{10... | collective-permute-start | bytes 589832 | tf_op jit(solution)/shard_map/ppermute | solution.py:244
  57.7 1.5 %collective-permute-start.8 = (bf16[4,96,256]{2,1,0:T(8,128)(2,1)S(1)}, bf16[4,96,256]{2,1,0:T(8,128)(2,1)S(1)}, u32[]{:S(2)}, u32[]{:S(2)}) collective-permute-start(bf16[4,96,256]{2,1,0:T(8,128)(2,1)S(1)} %get-tuple-element.21), channel_id=1, source_target_pairs={{0,16},{8,24},{16,0},{24,8},{1,17},{9,25},{17,1},{25,9},{2,18},{10... | collective-permute-start | bytes 589832 | tf_op jit(solution)/shard_map/ppermute | solution.py:244
  59.7 9.7 %collective-permute-done.4.far = bf16[1280,256]{1,0:T(8,128)(2,1)S(1)} collective-permute-done((bf16[1280,256]{1,0:T(8,128)(2,1)}, bf16[1280,256]{1,0:T(8,128)(2,1)S(1)}, u32[]{:S(2)}, u32[]{:S(2)}) %collective-permute-start.4) | collective-permute-done | bytes 655392 | tf_op jit(solution)/shard_map/ppermute | solution.py:285
  69.4 2.4 %collective-permute-start.5 = (bf16[1280,256]{1,0:T(8,128)(2,1)S(1)}, bf16[1280,256]{1,0:T(8,128)(2,1)}, u32[]{:S(2)}, u32[]{:S(2)}) collective-permute-start(bf16[1280,256]{1,0:T(8,128)(2,1)S(1)} %collective-permute-done.4.far), channel_id=1, source_target_pairs={{0,1},{2,3},{4,5},{6,7},{8,9},{10,11},{12,13},{14,15},{16,17},{18,... | collective-permute-start | bytes 1966088 | tf_op jit(solution)/shard_map/ppermute | solution.py:287
  74.2 1.6 %collective-permute-start.10 = (bf16[96,256]{1,0:T(8,128)(2,1)}, bf16[96,256]{1,0:T(8,128)(2,1)S(1)}, u32[]{:S(2)}, u32[]{:S(2)}) collective-permute-start(bf16[96,256]{1,0:T(8,128)(2,1)} %get-tuple-element.22), channel_id=1, source_target_pairs={{0,2},{1,3},{2,0},{3,1},{4,6},{5,7},{6,4},{7,5},{8,10},{9,11},{10,... | collective-permute-start | bytes 147464 | tf_op jit(solution)/shard_map/ppermute | solution.py:249
  76.8 1.8 %collective-permute-start.12 = (bf16[96,256]{1,0:T(8,128)(2,1)S(1)}, bf16[96,256]{1,0:T(8,128)(2,1)}, u32[]{:S(2)}, u32[]{:S(2)}) collective-permute-start(bf16[96,256]{1,0:T(8,128)(2,1)S(1)} %get-tuple-element.23), channel_id=1, source_target_pairs={{0,6},{1,7},{2,4},{3,5},{4,2},{5,3},{6,0},{7,1},{8,14},{9,15},{10,... | collective-permute-start | bytes 147464 | tf_op jit(solution)/shard_map/ppermute | solution.py:249
  79.7 1.7 %copy.7 = bf16[3,3,256,256]{3,2,1,0:T(8,128)(2,1)S(1)} copy(bf16[3,3,256,256]{2,3,1,0:T(8,128)(2,1)} %reverse_bitcast_fusion) | data formatting | bytes 2359296 | tf_op jit(solution)/shard_map/transpose | solution.py:278
  81.5 1.4 %collective-permute-done.12 = bf16[96,256]{1,0:T(8,128)(2,1)} collective-permute-done((bf16[96,256]{1,0:T(8,128)(2,1)S(1)}, bf16[96,256]{1,0:T(8,128)(2,1)}, u32[]{:S(2)}, u32[]{:S(2)}) %collective-permute-start.12) | collective-permute-done | bytes 49184 | tf_op jit(solution)/shard_map/ppermute | solution.py:249
  83.8 1.6 %collective-permute-start.13 = (bf16[96,256]{1,0:T(8,128)(2,1)S(1)}, bf16[96,256]{1,0:T(8,128)(2,1)S(1)}, u32[]{:S(2)}, u32[]{:S(2)}) collective-permute-start(bf16[96,256]{1,0:T(8,128)(2,1)S(1)} %get-tuple-element.16), channel_id=1, source_target_pairs={{8,0},{0,8},{24,16},{16,24},{9,1},{1,9},{25,17},{17,25},{10,2},{2,... | collective-permute-start | bytes 147464 | tf_op jit(solution)/shard_map/ppermute | solution.py:261
  85.4 1.3 %copy-done.7 = bf16[2560,256]{1,0:T(8,128)(2,1)S(1)} copy-done((bf16[2560,256]{1,0:T(8,128)(2,1)S(1)}, bf16[2560,256]{1,0:T(8,128)(2,1)}, u32[]{:S(2)}) %copy-start.7) | copy-done | bytes 1310744
  86.7 1.3 %copy-done.9 = f32[1280,256]{1,0:T(8,128)S(1)} copy-done((f32[1280,256]{1,0:T(8,128)S(1)}, f32[1280,256]{1,0:T(8,128)}, u32[]{:S(2)}) %copy-start.9) | copy-done | bytes 1310744
  88.0 7.7 %back.1 = bf16[2560,256]{1,0:T(8,128)(2,1)} custom-call(bf16[1280,256]{1,0:T(8,128)(2,1)S(1)} %copy-done.11, bf16[2560,256]{1,0:T(8,128)(2,1)S(1)} %copy-done.7, f32[1280,256]{1,0:T(8,128)S(1)} %copy-done.9, bf16[1280,256]{1,0:T(8,128)(2,1)} %collective-permute-done.5.near, bf16[1280,256]{1,0:T(8,128)(2,1)S(1)} %collective-permute-done.4.far, ...), custom_call_target="tpu_custom_call" | custom-call | flops 3355443200 | bytes 7471104 | tf_op jit(solution)/shard_map/back/pallas_call | solution.py:29
  95.7 1.5 %collective-permute-start.14 = (bf16[96,256]{1,0:T(8,128)(2,1)S(1)}, bf16[96,256]{1,0:T(8,128)(2,1)S(1)}, u32[]{:S(2)}, u32[]{:S(2)}) collective-permute-start(bf16[96,256]{1,0:T(8,128)(2,1)S(1)} %get-tuple-element.16), channel_id=1, source_target_pairs={{16,0},{24,8},{0,16},{8,24},{17,1},{25,9},{1,17},{9,25},{18,2},{26... | collective-permute-start | bytes 147464 | tf_op jit(solution)/shard_map/ppermute | solution.py:261
  97.7 2.1 %collective-permute-done.14 = bf16[96,256]{1,0:T(8,128)(2,1)S(1)} collective-permute-done((bf16[96,256]{1,0:T(8,128)(2,1)S(1)}, bf16[96,256]{1,0:T(8,128)(2,1)S(1)}, u32[]{:S(2)}, u32[]{:S(2)}) %collective-permute-start.14) | collective-permute-done | bytes 49184 | tf_op jit(solution)/shard_map/ppermute | solution.py:261
  99.8 2.4 %collective-permute-done.15 = bf16[96,256]{1,0:T(8,128)(2,1)S(1)} collective-permute-done((bf16[96,256]{1,0:T(8,128)(2,1)S(1)}, bf16[96,256]{1,0:T(8,128)(2,1)S(1)}, u32[]{:S(2)}, u32[]{:S(2)}) %collective-permute-start.15) | collective-permute-done | bytes 49184 | tf_op jit(solution)/shard_map/ppermute | solution.py:261
  (55 shorter events, 14.2 us)
Async XLA Ops:
  0.6 30.1 %collective-permute-start = (bf16[2560,256]{1,0:T(8,128)(2,1)}, bf16[2560,256]{1,0:T(8,128)(2,1)}, u32[]{:S(2)}, u32[]{:S(2)}) collective-permute-start(bf16[2560,256]{1,0:T(8,128)(2,1)} %bitcast.53), channel_id=1, source_target_pairs={{0,1},{1,0},{2,3},{3,2},{4,5},{5,4},{6,7},{7,6},{8,9},{9,8},{10,11... | collective-permute-start | bytes 3932168 | tf_op jit(solution)/shard_map/ppermute | solution.py:284
  3.4 22.7 %copy-start.1 = (bf16[3,3,256,256]{3,2,1,0:T(8,128)(2,1)S(1)}, bf16[3,3,256,256]{3,2,1,0:T(8,128)(2,1)}, u32[]{:S(2)}) copy-start(bf16[3,3,256,256]{3,2,1,0:T(8,128)(2,1)} %param.6) | copy-start | bytes 3538948
  3.4 20.1 %collective-permute-start.1 = (bf16[1280,256]{1,0:T(8,128)(2,1)S(1)}, bf16[1280,256]{1,0:T(8,128)(2,1)}, u32[]{:S(2)}, u32[]{:S(2)}) collective-permute-start(bf16[1280,256]{1,0:T(8,128)(2,1)S(1)} %bitcast.62), channel_id=1, source_target_pairs={{2,0},{3,1},{4,2},{5,3},{6,4},{7,5},{10,8},{11,9},{12,10},{13,11},... | collective-permute-start | bytes 1966088 | tf_op jit(solution)/shard_map/ppermute | solution.py:282
  5.7 31.3 %collective-permute-start.3 = (bf16[1440,256]{1,0:T(8,128)(2,1)}, bf16[1440,256]{1,0:T(8,128)(2,1)S(1)}, u32[]{:S(2)}, u32[]{:S(2)}) collective-permute-start(bf16[1440,256]{1,0:T(8,128)(2,1)} %bitcast.5), channel_id=1, source_target_pairs={{0,2},{1,3},{2,4},{3,5},{4,6},{5,7},{8,10},{9,11},{10,12},{11,13},... | collective-permute-start | bytes 2211848 | tf_op jit(solution)/shard_map/ppermute | solution.py:283
  23.5 13.6 %collective-permute-start.2 = (bf16[1280,256]{1,0:T(8,128)(2,1)}, bf16[1280,256]{1,0:T(8,128)(2,1)}, u32[]{:S(2)}, u32[]{:S(2)}) collective-permute-start(bf16[1280,256]{1,0:T(8,128)(2,1)} %collective-permute-done.1.far), channel_id=1, source_target_pairs={{0,1},{2,3},{4,5},{6,7},{8,9},{10,11},{12,13},{14,15},{16,17},{18,... | collective-permute-start | bytes 1966088 | tf_op jit(solution)/shard_map/ppermute | solution.py:286
  26.1 4.7 %copy-start = (bf16[1,1,16,160,256]{4,3,2,1,0:T(8,128)(2,1)S(1)}, bf16[1,1,16,160,256]{4,3,2,1,0:T(8,128)(2,1)}, u32[]{:S(2)}) copy-start(bf16[1,1,16,160,256]{4,3,2,1,0:T(8,128)(2,1)} %param.5) | copy-start | bytes 3932164
  26.1 4.7 %copy-start.4 = (bf16[3,256,256]{2,1,0:T(8,128)(2,1)S(1)}, bf16[3,256,256]{2,1,0:T(8,128)(2,1)}, u32[]{:S(2)}) copy-start(bf16[3,256,256]{2,1,0:T(8,128)(2,1)} %tw.5) | copy-start | bytes 1179652
  30.7 6.4 %copy-start.6 = (bf16[2560,256]{1,0:T(8,128)(2,1)}, bf16[2560,256]{1,0:T(8,128)(2,1)S(1)}, u32[]{:S(2)}) copy-start(bf16[2560,256]{1,0:T(8,128)(2,1)S(1)} %hidden.1) | copy-start | bytes 3932164
  30.7 6.3 %copy-start.3 = (bf16[1,1,16,160,256]{4,3,2,1,0:T(8,128)(2,1)S(1)}, bf16[1,1,16,160,256]{4,3,2,1,0:T(8,128)(2,1)}, u32[]{:S(2)}) copy-start(bf16[1,1,16,160,256]{4,3,2,1,0:T(8,128)(2,1)} %param.4) | copy-start | bytes 3932164
  37.0 12.0 %copy-start.8 = (f32[1280,256]{1,0:T(8,128)}, f32[1280,256]{1,0:T(8,128)S(1)}, u32[]{:S(2)}) copy-start(f32[1280,256]{1,0:T(8,128)S(1)} %get-tuple-element.12.rest) | copy-start | bytes 3932164
  50.2 2.6 %collective-permute-start.6 = (bf16[4,4,96,256]{3,2,1,0:T(8,128)(2,1)}, bf16[4,4,96,256]{3,2,1,0:T(8,128)(2,1)}, u32[]{:S(2)}, u32[]{:S(2)}) collective-permute-start(bf16[4,4,96,256]{3,2,1,0:T(8,128)(2,1)} %fusion.2), channel_id=1, source_target_pairs={{0,1},{1,0},{2,3},{3,2},{4,5},{5,4},{6,7},{7,6},{8,9},{9,8},{10,11... | collective-permute-start | bytes 2359304 | tf_op jit(solution)/shard_map/ppermute | solution.py:241
  50.2 19.2 %collective-permute-start.4 = (bf16[1280,256]{1,0:T(8,128)(2,1)}, bf16[1280,256]{1,0:T(8,128)(2,1)S(1)}, u32[]{:S(2)}, u32[]{:S(2)}) collective-permute-start(bf16[1280,256]{1,0:T(8,128)(2,1)} %bitcast.6), channel_id=1, source_target_pairs={{2,0},{3,1},{4,2},{5,3},{6,4},{7,5},{10,8},{11,9},{12,10},{13,11},... | collective-permute-start | bytes 1966088 | tf_op jit(solution)/shard_map/ppermute | solution.py:285
  56.2 15.7 %collective-permute-start.7 = (bf16[4,96,256]{2,1,0:T(8,128)(2,1)S(1)}, bf16[4,96,256]{2,1,0:T(8,128)(2,1)S(1)}, u32[]{:S(2)}, u32[]{:S(2)}) collective-permute-start(bf16[4,96,256]{2,1,0:T(8,128)(2,1)S(1)} %get-tuple-element.19), channel_id=1, source_target_pairs={{0,8},{8,0},{16,24},{24,16},{1,9},{9,1},{17,25},{25,17},{2,10},{10... | collective-permute-start | bytes 589832 | tf_op jit(solution)/shard_map/ppermute | solution.py:244
  57.7 14.1 %collective-permute-start.8 = (bf16[4,96,256]{2,1,0:T(8,128)(2,1)S(1)}, bf16[4,96,256]{2,1,0:T(8,128)(2,1)S(1)}, u32[]{:S(2)}, u32[]{:S(2)}) collective-permute-start(bf16[4,96,256]{2,1,0:T(8,128)(2,1)S(1)} %get-tuple-element.21), channel_id=1, source_target_pairs={{0,16},{8,24},{16,0},{24,8},{1,17},{9,25},{17,1},{25,9},{2,18},{10... | collective-permute-start | bytes 589832 | tf_op jit(solution)/shard_map/ppermute | solution.py:244
  59.3 12.6 %collective-permute-start.9 = (bf16[4,96,256]{2,1,0:T(8,128)(2,1)S(1)}, bf16[4,96,256]{2,1,0:T(8,128)(2,1)S(1)}, u32[]{:S(2)}, u32[]{:S(2)}) collective-permute-start(bf16[4,96,256]{2,1,0:T(8,128)(2,1)S(1)} %get-tuple-element.20), channel_id=1, source_target_pairs={{0,24},{8,16},{16,8},{24,0},{1,25},{9,17},{17,9},{25,1},{2,26},{10... | collective-permute-start | bytes 589832 | tf_op jit(solution)/shard_map/ppermute | solution.py:244
  69.4 15.9 %collective-permute-start.5 = (bf16[1280,256]{1,0:T(8,128)(2,1)S(1)}, bf16[1280,256]{1,0:T(8,128)(2,1)}, u32[]{:S(2)}, u32[]{:S(2)}) collective-permute-start(bf16[1280,256]{1,0:T(8,128)(2,1)S(1)} %collective-permute-done.4.far), channel_id=1, source_target_pairs={{0,1},{2,3},{4,5},{6,7},{8,9},{10,11},{12,13},{14,15},{16,17},{18,... | collective-permute-start | bytes 1966088 | tf_op jit(solution)/shard_map/ppermute | solution.py:287
  74.2 7.2 %collective-permute-start.10 = (bf16[96,256]{1,0:T(8,128)(2,1)}, bf16[96,256]{1,0:T(8,128)(2,1)S(1)}, u32[]{:S(2)}, u32[]{:S(2)}) collective-permute-start(bf16[96,256]{1,0:T(8,128)(2,1)} %get-tuple-element.22), channel_id=1, source_target_pairs={{0,2},{1,3},{2,0},{3,1},{4,6},{5,7},{6,4},{7,5},{8,10},{9,11},{10,... | collective-permute-start | bytes 147464 | tf_op jit(solution)/shard_map/ppermute | solution.py:249
  75.8 5.7 %collective-permute-start.11 = (bf16[96,256]{1,0:T(8,128)(2,1)}, bf16[96,256]{1,0:T(8,128)(2,1)S(1)}, u32[]{:S(2)}, u32[]{:S(2)}) collective-permute-start(bf16[96,256]{1,0:T(8,128)(2,1)} %get-tuple-element.24), channel_id=1, source_target_pairs={{0,4},{1,5},{2,6},{3,7},{4,0},{5,1},{6,2},{7,3},{8,12},{9,13},{10,... | collective-permute-start | bytes 147464 | tf_op jit(solution)/shard_map/ppermute | solution.py:249
  76.8 6.1 %collective-permute-start.12 = (bf16[96,256]{1,0:T(8,128)(2,1)S(1)}, bf16[96,256]{1,0:T(8,128)(2,1)}, u32[]{:S(2)}, u32[]{:S(2)}) collective-permute-start(bf16[96,256]{1,0:T(8,128)(2,1)S(1)} %get-tuple-element.23), channel_id=1, source_target_pairs={{0,6},{1,7},{2,4},{3,5},{4,2},{5,3},{6,0},{7,1},{8,14},{9,15},{10,... | collective-permute-start | bytes 147464 | tf_op jit(solution)/shard_map/ppermute | solution.py:249
  79.7 5.7 %copy-start.5 = (bf16[3,256,256]{2,1,0:T(8,128)(2,1)S(1)}, bf16[3,256,256]{2,1,0:T(8,128)(2,1)}, u32[]{:S(2)}) copy-start(bf16[3,256,256]{2,1,0:T(8,128)(2,1)} %tw.5) | copy-start | bytes 1179652
  79.7 5.7 %copy-start.11 = (bf16[1280,256]{1,0:T(8,128)(2,1)S(1)}, bf16[1280,256]{1,0:T(8,128)(2,1)}, u32[]{:S(2)}) copy-start(bf16[1280,256]{1,0:T(8,128)(2,1)} %copy-done.10) | copy-start | bytes 1966084
  83.8 13.9 %collective-permute-start.13 = (bf16[96,256]{1,0:T(8,128)(2,1)S(1)}, bf16[96,256]{1,0:T(8,128)(2,1)S(1)}, u32[]{:S(2)}, u32[]{:S(2)}) collective-permute-start(bf16[96,256]{1,0:T(8,128)(2,1)S(1)} %get-tuple-element.16), channel_id=1, source_target_pairs={{8,0},{0,8},{24,16},{16,24},{9,1},{1,9},{25,17},{17,25},{10,2},{2,... | collective-permute-start | bytes 147464 | tf_op jit(solution)/shard_map/ppermute | solution.py:261
  95.7 4.1 %collective-permute-start.14 = (bf16[96,256]{1,0:T(8,128)(2,1)S(1)}, bf16[96,256]{1,0:T(8,128)(2,1)S(1)}, u32[]{:S(2)}, u32[]{:S(2)}) collective-permute-start(bf16[96,256]{1,0:T(8,128)(2,1)S(1)} %get-tuple-element.16), channel_id=1, source_target_pairs={{16,0},{24,8},{0,16},{8,24},{17,1},{25,9},{1,17},{9,25},{18,2},{26... | collective-permute-start | bytes 147464 | tf_op jit(solution)/shard_map/ppermute | solution.py:261
  97.2 5.0 %collective-permute-start.15 = (bf16[96,256]{1,0:T(8,128)(2,1)S(1)}, bf16[96,256]{1,0:T(8,128)(2,1)S(1)}, u32[]{:S(2)}, u32[]{:S(2)}) collective-permute-start(bf16[96,256]{1,0:T(8,128)(2,1)S(1)} %get-tuple-element.16), channel_id=1, source_target_pairs={{24,0},{16,8},{8,16},{0,24},{25,1},{17,9},{9,17},{1,25},{26,2},{18... | collective-permute-start | bytes 147464 | tf_op jit(solution)/shard_map/ppermute | solution.py:261
  (5 other events, 8.6 us)

commit v2 on v0

v2 whole, which is shorter than its diff:
```python
import functools

import jax
import jax.numpy as jnp
from jax import lax
from jax.experimental import pallas as pl
from jax.experimental.pallas import tpu as pltpu
from jax.sharding import PartitionSpec as P

BF16, F32 = jnp.bfloat16, jnp.float32
EDGE = 8
LIMIT, FULL = 24 * 2**20, 60 * 2**20
REMOTE = 6
SPARE = 45056


def dot(a, b):
    return jnp.dot(a, b, preferred_element_type=F32)


def dot_rt(a, b):
    return lax.dot_general(a, b, (((1,), (1,)), ((), ())), preferred_element_type=F32)


def dot_lt(a, b):
    return lax.dot_general(a, b, (((0,), (0,)), ((), ())), preferred_element_type=F32)


def like(dtype, *shape):
    return jax.ShapeDtypeStruct(shape, dtype)


SPACE = {
    "s": pl.BlockSpec(memory_space=pltpu.SMEM),
    "v": pl.BlockSpec(memory_space=pltpu.VMEM),
    "h": pl.BlockSpec(memory_space=pl.ANY),
}


def call(kernel, name, spaces, flops, args, outs, scratch=(), copies=1, after=(), alias=None, limit=LIMIT):
    nbytes = sum(a.size * a.dtype.itemsize for a in (*args, *outs))
    ins, results = spaces.split()
    n_in, n_out = len(args), len(outs)

    def body(*refs):
        rest = refs[n_in + len(after) :]
        kernel(*refs[:n_in], *rest[:n_out], *rest[n_out + 1 :])
        rest[n_out][...] = jnp.zeros(TOKEN.shape, TOKEN.dtype)

    return pl.pallas_call(
        body,
        out_shape=[*outs, TOKEN],
        in_specs=[SPACE[c] for c in ins] + [SPACE["v"]] * len(after),
        out_specs=[SPACE[c] for c in results] + [SPACE["v"]],
        scratch_shapes=[*(pltpu.VMEM(s.shape, s.dtype) for s in scratch), pltpu.SemaphoreType.DMA((copies,))],
        input_output_aliases={} if alias is None else alias,
        compiler_params=pltpu.CompilerParams(vmem_limit_bytes=limit),
        cost_estimate=pl.CostEstimate(flops=flops, bytes_accessed=nbytes, transcendentals=0),
        name=name,
    )(*args, *after)


def start_all(sems, pairs, first=0):
    copies = [pltpu.make_async_copy(a, b, sems.at[first + i]) for i, (a, b) in enumerate(pairs)]
    for c in copies:
        c.start()
    return copies


def wait_all(copies):
    for c in copies:
        c.wait()


def behind(value, token):
    return lax.optimization_barrier((value, token))


TOKEN = like(F32, 8, 128)


def tile(i, size, base=0):
    return pl.ds(pl.multiple_of(base + i * size, size), size)


def loop(steps, body):
    def step(i, carry):
        body(i)
        return carry

    lax.fori_loop(0, steps, step, 0)


def silu_parts(v):
    v = v.astype(F32)
    sig = 0.5 * jnp.tanh(0.5 * v) + 0.5
    act = v * sig
    return act.astype(BF16), sig + act * (1.0 - sig)


def clear_edges(pad):
    n, long, chans = pad.shape
    pad[:, :EDGE] = jnp.zeros((n, EDGE, chans), F32)
    pad[:, long - EDGE :] = jnp.zeros((n, EDGE, chans), F32)


def put_shifts(cat, where, mid, pad):
    n, long, chans = pad.shape
    width = long - 2 * EDGE
    pad[:, EDGE : EDGE + width] = mid.astype(F32).reshape(n, width, chans)
    cat[where, chans : 2 * chans] = mid
    cat[where, :chans] = pad[:, EDGE + 1 : EDGE + 1 + width].astype(BF16).reshape(n * width, chans)
    cat[where, 2 * chans :] = pad[:, EDGE - 1 : EDGE - 1 + width].astype(BF16).reshape(n * width, chans)


def conv_rows(rows3, tap, out, step, wide, at=0):
    _, n, long, chans = wide.shape
    width = long - 2 * EDGE
    for side in range(2):
        clear_edges(wide.at[side])

    def body(i):
        start = i * step
        rows = [rows3[pl.ds(pl.multiple_of(start + a * width, width), step)] for a in range(3)]
        rows = jnp.concatenate(rows, axis=1)
        wide[0, :, EDGE : EDGE + width] = tap(rows, 0).reshape(n, width, chans)
        wide[1, :, EDGE : EDGE + width] = tap(rows, 2).reshape(n, width, chans)
        mid = tap(rows, 1).reshape(n, width, chans)
        mid += wide[0, :, EDGE - 1 : EDGE - 1 + width] + wide[1, :, EDGE + 1 : EDGE + 1 + width]
        out[tile(i, step, at)] = mid.reshape(step, chans).astype(BF16)

    loop((rows3.shape[0] - 2 * width) // step, body)


def forward_tap(sw):
    return lambda rows, b: dot(rows, jnp.concatenate([sw[a, b] for a in range(3)], axis=0))


def back_tap(sw):
    return lambda rows, b: dot_rt(rows, jnp.concatenate([sw[2 - a, 2 - b] for a in range(3)], axis=1))


def tap_parts(video, cat, first, last, base, height, width):
    chans = video.shape[1]
    for a in range(3):
        low, high = max(first, 1 - a), min(last, height + 1 - a)
        rows = video[(low + a - 1 - base) * width : (high + a - 1 - base) * width]
        part = dot_lt(rows, cat[(low - first) * width : (high - first) * width])
        for b in range(3):
            yield 3 * a + b, part[:, b * chans : (b + 1) * chans]


def cut_kernel(ranges, *refs):
    n = len(ranges)
    sources, targets, held, sems = refs[:n], refs[n : 2 * n], refs[2 * n : 3 * n], refs[-1]
    copies = start_all(sems, [(a.at[low:high], b) for a, b, (low, high) in zip(sources, held, ranges)])
    out = []
    for i, c in enumerate(copies):
        c.wait()
        out += start_all(sems, [(held[i], targets[i])], n + i)
    wait_all(out)


def local_kernel(
    height, width, upper, core, video, cot, mate, sw, tw, low, full, spatial, temporal,
    rows3, both, sw_v, tw_v, hidden_v, act, cat, wide, pad, rest, sems,
):
    rows, chans = video.shape
    step = 2 * width
    head = start_all(sems, [(video, rows3.at[width : rows + width]), (sw, sw_v)])
    tail = start_all(sems, [(cot, both.at[:, :chans]), (mate, both.at[:, chans:]), (tw, tw_v)], 2)
    rows3[:width] = jnp.zeros((width, chans), BF16)
    rows3[rows + width :] = jnp.zeros((width, chans), BF16)
    clear_edges(pad)
    wait_all(head)
    conv_rows(rows3, forward_tap(sw_v), hidden_v, wide.shape[1] * width, wide)
    out = start_all(sems, [(hidden_v, low.at[:rows])], 5)
    wait_all(tail)
    even = core[0] == 0
    tap0 = tw_v[0]
    tap1 = jnp.where(even, tw_v[1], jnp.zeros_like(tap0))
    taps = jnp.concatenate([tap0, tap1], axis=1)

    def top(i):
        here = tile(i, step)
        act[here] = silu_parts(hidden_v[here])[0]
        rest[here] = dot_rt(both[here], taps)

    def bottom(i):
        here = tile(i, step, upper * width)
        act_rows, slope = silu_parts(hidden_v[here])
        act[here] = act_rows
        grad = dot_rt(both[here], taps)
        rest[here] = grad
        put_shifts(cat, tile(i, step), (grad * slope).astype(BF16), pad)

    loop((height - upper) // 2, bottom)
    loop(upper // 2, top)
    out += start_all(sems, [(rest, full.at[:rows])], 6)
    for tap, part in tap_parts(rows3, cat, upper, height, -1, height, width):
        spatial[tap] = part
    part = dot_lt(act[...], both[...])
    temporal[0] = part[:, :chans]
    temporal[1] = jnp.where(even, part[:, chans:], 0.0)
    temporal[2] = jnp.zeros((chans, chans), F32)
    wait_all(out)


def remote_kernel(
    height, width, upper, core, above, cot, mate, sw, tw, spatial, temporal, spatial_out, temporal_out,
    rows3, both, sw_v, tw_v, other, act, cat, wide, pad, sems,
):
    chans = cot.shape[1]
    step = 2 * width
    at = upper * width
    held = above.shape[0]
    head = start_all(sems, [(above, rows3.at[:held]), (sw, sw_v)])
    tail = start_all(sems, [(mate.at[at:], both.at[:, :chans]), (cot.at[at:], both.at[:, chans:]), (tw, tw_v)], 2)
    even = core[0] == 0
    clear_edges(pad)
    rows3[held:] = jnp.zeros((width, chans), BF16)
    wait_all(head)
    conv_rows(rows3, forward_tap(sw_v), other, wide.shape[1] * width, wide)
    wait_all(tail)
    tap2 = tw_v[2]
    taps = jnp.concatenate([jnp.where(even, jnp.zeros_like(tap2), tw_v[1]), tap2], axis=1)

    def remote(i):
        here = tile(i, step)
        act_rows, slope = silu_parts(other[here])
        act[here] = act_rows
        grad = dot_rt(both[here], taps)
        put_shifts(cat, here, (grad * slope).astype(BF16), pad)

    loop((height - upper) // 2, remote)
    for tap, part in tap_parts(rows3, cat, upper, height, upper - 1, height, width):
        spatial_out[tap] = spatial[tap] + part
    part = dot_lt(act[...], both[...])
    temporal_out[0] = temporal[0]
    temporal_out[1] = temporal[1] + jnp.where(even, 0.0, part[:, :chans])
    temporal_out[2] = temporal[2] + part[:, chans:]


def last_kernel(
    height, width, upper, plan, core, video, near, far, tw, spatial, temporal, low_in, full_in,
    low, full, send, *scratch,
):
    rows, both, tw_v, hidden_v, rest, grad_v, act, cat, pad, total, total_t, *blocks, sems = scratch
    step = 2 * width
    chans = video.shape[1]
    count = upper * width
    whole = height * width
    head = start_all(
        sems, [(near, both.at[:, :chans]), (far, both.at[:, chans:]), (tw, tw_v), (low_in.at[:count], hidden_v), (full_in.at[:count], rest)]
    )
    tail = start_all(sems, [(video.at[: count + width], rows)], 5)
    clear_edges(pad)
    wait_all(head)
    taps = jnp.concatenate([tw_v[1], tw_v[2]], axis=1)

    def own(i):
        here = tile(i, step)
        act_rows, slope = silu_parts(hidden_v[here])
        act[here] = act_rows
        grad = rest[here] + dot_rt(both[here], taps)
        mid = (grad * slope).astype(BF16)
        grad_v[here] = mid
        put_shifts(cat, here, mid, pad)

    loop(upper // 2, own)
    out = start_all(sems, [(grad_v, low.at[whole : whole + count])], 6)
    wait_all(tail)
    for tap, part in tap_parts(rows, cat, 0, upper, 0, height, width):
        total[tap * chans : (tap + 1) * chans] = spatial[tap] + part
    part = dot_lt(act[...], both[...])
    total_t[:chans] = temporal[0]
    total_t[chans : 2 * chans] = temporal[1] + part[:, :chans]
    total_t[2 * chans :] = temporal[2] + part[:, chans:]
    if plan is None:
        n = total.shape[0]
        out += start_all(sems, [(total, full.at[whole : whole + n]), (total_t, full.at[whole + n : whole + n + total_t.shape[0]])], 7)
        wait_all(out)
        return
    keep_v, send_v = blocks
    dp, levels, rs, rt = plan

    def block(at, i):
        return jnp.concatenate(
            [
                total[pl.ds(pl.multiple_of((at * dp + i) * rs, 8), rs)],
                total_t[pl.ds(pl.multiple_of((at * dp + i) * rt, 8), rt)],
            ],
            axis=0,
        )

    size = rs + rt
    for level in range(levels):
        for i in range(dp):
            send_v[i, level] = block(2 * level + 1 - core[0], i).astype(BF16)
    out += start_all(sems, [(send_v, send)], 7)
    for i in range(dp):
        for level in range(levels):
            at = (i * levels + level) * size
            keep_v[at : at + size] = block(2 * level + core[0], i)
    n = keep_v.shape[0]
    wait_all(out + start_all(sems, [(keep_v, full.at[whole : whole + n])], 8))


def back_top_kernel(whole, width, low, sw, back, rows3, sw_v, out, wide, sems):
    chans = out.shape[1]
    held = rows3.shape[0] - width
    head = start_all(sems, [(low.at[whole : whole + held], rows3.at[width:]), (sw, sw_v)])
    rows3[:width] = jnp.zeros((width, chans), BF16)
    wait_all(head)
    conv_rows(rows3, back_tap(sw_v), out, wide.shape[1] * width, wide)
    wait_all(start_all(sems, [(out, back.at[: out.shape[0]])], 2))


def back_bottom_kernel(
    whole, width, upper, low, full, near, far, tw, sw, _, back,
    rows3, both, hidden_v, rest, tw_v, sw_v, out, wide, sems,
):
    chans = out.shape[1]
    step = 2 * width
    count = near.shape[0]
    first = upper * width
    top = rows3.shape[0] - width - count
    head = start_all(
        sems,
        [
            (near, both.at[:, :chans]), (far, both.at[:, chans:]), (tw, tw_v), (low.at[first:whole], hidden_v),
            (full.at[first:whole], rest), (low.at[whole + first - top : whole + first], rows3.at[:top]), (sw, sw_v),
        ],
    )
    rows3[rows3.shape[0] - width :] = jnp.zeros((width, chans), BF16)
    wait_all(head)
    taps = jnp.concatenate([tw_v[1], tw_v[2]], axis=1)

    def rest_rows(i):
        here = tile(i, step)
        slope = silu_parts(hidden_v[here])[1]
        grad = rest[here] + dot_rt(both[here], taps)
        rows3[pl.ds(pl.multiple_of(top + i * step, width), step)] = (grad * slope).astype(BF16)

    loop(count // step, rest_rows)
    conv_rows(rows3, back_tap(sw_v), out, wide.shape[1] * width, wide)
    wait_all(start_all(sems, [(out, back.at[back.shape[0] - out.shape[0] :])], 7))


def peer(index, k, size):
    return index ^ k if size & (size - 1) == 0 else (index + k) % size


def split_kernel(size, first, where, kept, swapped, own, *refs):
    sends, (keep_v, swapped_v, own_v, send_v, sems) = refs[: size - 1], refs[size - 1 :]
    q = where[0]
    levels, each = own.shape[:2]
    n = keep_v.shape[0]
    wait_all(start_all(sems, [(kept.at[first : first + n], keep_v), (swapped, swapped_v)]))

    def total(i):
        mine = keep_v[pl.ds(pl.multiple_of(i * levels * each, 8), levels * each)]
        return mine.reshape(own.shape) + swapped_v[i].astype(F32)

    out = []
    for k, send in enumerate(sends):
        send_v[k] = total(peer(q, k + 1, size)).astype(BF16)
        out += start_all(sems, [(send_v.at[k], send)], 2 + k)
    own_v[...] = total(q)
    wait_all(out + start_all(sems, [(own_v, own)], 1 + size))


def level_kernel(size, where, own, *refs):
    got = refs[: -size - 3]
    mine, *sends = refs[-size - 3 : -3]
    own_v, got_v, sems = refs[-3:]
    level = where[0]
    wait_all(start_all(sems, [(own, own_v), *((g, got_v.at[k]) for k, g in enumerate(got))]))

    def total(i):
        return sum((got_v[k, i].astype(F32) for k in range(len(got))), own_v[i])

    mine[...] = total(level)
    for k, out in enumerate(sends, 1):
        out[...] = total(peer(level, k, size)).astype(BF16)


def sum_kernel(own, *refs):
    *got, out, _ = refs
    out[...] = sum((g[...].astype(F32) for g in got), own[...]).astype(BF16)


def place_kernel(scale, where, small, *refs):
    *got, spatial, temporal, _ = refs
    size, rs, rt = len(got) + 1, spatial.shape[1], temporal.shape[1]
    for k, part in enumerate((small, *got)):
        at = peer(where[0], k, size)
        rows = part[...].astype(F32) * scale
        spatial[at] = rows[:rs]
        temporal[at] = rows[rs:]


def shards(video, cotangent, spatial_weight, temporal_weight):
    height, width, chans = (video.shape[2], video.shape[3], video.shape[4])
    rows = height * width
    dp, seq = lax.axis_size("dp"), lax.axis_size("seq")
    levels = seq // 2
    scale = float((dp * video.shape[0] * seq * rows) ** -0.5)
    dp_at, seq_at = lax.axis_index("dp").astype(jnp.int32), lax.axis_index("seq").astype(jnp.int32)
    core, level, q = (v.reshape(1) for v in (seq_at % 2, seq_at // 2, dp_at))
    x = video.reshape(rows, chans)
    cot = cotangent.reshape(rows, chans)
    sw, tw = spatial_weight, temporal_weight
    upper = height - REMOTE
    whole = rows
    down = [(i + 2, i) for i in range(seq - 2)]
    up = [(i, i + 2) for i in range(seq - 2)]
    across = [(i, i + 1) for i in range(0, seq, 2)]
    swap = [(i, i ^ 1) for i in range(seq)]

    mac = rows * chans * chans
    long = width + 2 * EDGE
    pad = like(F32, 2, long, chans)
    taps9, taps3 = (like(F32, n, chans, chans) for n in (9, 3))

    def rows_of(n, columns=chans, dtype=BF16):
        return like(dtype, n * width, columns)

    def wide(n):
        return like(F32, 2, n, long, chans)

    mate = lax.ppermute(cot, "seq", swap)
    ranges = [((upper - 1) * width, rows), (0, upper * width), (upper * width, rows)]
    slices = [like(BF16, high - low, chans) for low, high in ranges]
    *slices, token = call(
        functools.partial(cut_kernel, ranges), "cut", "hhh hhh", 0, [x, cot, cot], slices, slices, copies=6, limit=FULL
    )
    above = lax.ppermute(slices[0], "seq", up)
    far = lax.ppermute(slices[1], "seq", down)
    far3 = lax.ppermute(slices[2], "seq", down)
    low, full, spatial, temporal, token = call(
        functools.partial(local_kernel, height, width, upper), "local", "shhhhh hhvv", 34 * mac,
        [core, x, cot, mate, sw, tw], [like(BF16, 2 * SPARE, chans), like(F32, SPARE, chans), taps9, taps3],
        [
            rows_of(height + 2), rows_of(height, 2 * chans), sw, tw, rows_of(height), rows_of(height),
            rows_of(REMOTE, 3 * chans), wide(height // 2), pad, rows_of(height, dtype=F32),
        ],
        copies=7,
    )
    spatial, temporal, token = call(
        functools.partial(remote_kernel, height, width, upper), "remote", "shhhhhvv vv", 16 * mac,
        [core, above, cot, mate, sw, tw, spatial, temporal], [taps9, taps3],
        [
            rows_of(REMOTE + 2), rows_of(REMOTE, 2 * chans), sw, tw, rows_of(REMOTE), rows_of(REMOTE),
            rows_of(REMOTE, 3 * chans), wide(REMOTE), pad,
        ],
        copies=5, after=[token],
    )

    far, token = behind(far, token)
    near = lax.ppermute(far, "seq", across)
    rs, rt = 9 * chans // (seq * dp), 3 * chans // (seq * dp)
    plain = rs % 8 or rt % 8 or (rs + rt) % 16
    flat = [like(F32, 9 * chans, chans), like(F32, 3 * chans, chans)]
    send = like(BF16, dp, levels, rs + rt, chans)
    blocks = [] if plain else [like(F32, 12 * chans // 2, chans), send]
    low, full, send, token = call(
        functools.partial(last_kernel, height, width, upper, None if plain else (dp, levels, rs, rt)), "last", "shhhhvvhh hhh", 16 * mac,
        [core, x, near, far, tw, spatial, temporal, low, full], [low, full, send],
        [
            rows_of(upper + 1), rows_of(upper, 2 * chans), tw, rows_of(upper), rows_of(upper, dtype=F32), rows_of(upper),
            rows_of(upper), rows_of(upper, 3 * chans), pad, *flat, *blocks,
        ],
        copies=9, after=[token], alias={7: 0, 8: 1},
    )
    kept, first = full, whole
    if plain:
        parts = (full[whole : whole + 9 * chans], full[whole + 9 * chans : whole + 12 * chans])
        both = jnp.concatenate([g.reshape(levels, 2, dp, -1, chans) for g in parts], axis=3)
        both = jnp.transpose(both, (1, 2, 0, 3, 4))
        kept, first = lax.dynamic_index_in_dim(both, core[0], 0, keepdims=False).reshape(-1, chans), 0
        send = lax.dynamic_index_in_dim(both, 1 - core[0], 0, keepdims=False).astype(BF16)

    got = lax.ppermute(send, "seq", swap)
    piece = (levels, rs + rt, chans)
    own, *sends, token = call(
        functools.partial(split_kernel, dp, first), "split", "shh " + "h" * dp, mac // 8, [q, kept, got],
        [like(F32, *piece)] + [like(BF16, *piece)] * (dp - 1),
        [like(F32, 12 * chans // 2, chans), send, like(F32, *piece), like(BF16, dp - 1, *piece)], copies=dp + 2,
    )
    got = [lax.ppermute(s, "dp", [(i, peer(i, k, dp)) for i in range(dp)]) for k, s in enumerate(sends, 1)]
    back, token = call(
        functools.partial(back_top_kernel, whole, width), "back_top", "hh h", 9 * mac, [low, sw], [rows_of(height)],
        [rows_of(height // 2 + 2), sw, rows_of(height // 2), wide(height // 2)], copies=3, after=[token],
    )
    level_piece = (rs + rt, chans)
    own, *sends, token = call(
        functools.partial(level_kernel, levels), "level", "sh" + "h" * (dp - 1) + " " + "v" * levels, mac // 8,
        [level, own, *got], [like(F32, *level_piece)] + [like(BF16, *level_piece)] * (levels - 1),
        [like(F32, *piece), like(BF16, dp - 1, *piece)], copies=dp, after=[token],
    )
    far3, token = behind(far3, token)
    near3 = lax.ppermute(far3, "seq", across)
    got = [
        lax.ppermute(s, "seq", [(i, 2 * peer(i // 2, k, levels) + i % 2) for i in range(seq)])
        for k, s in enumerate(sends, 1)
    ]
    back, token = call(
        functools.partial(back_bottom_kernel, whole, width, upper), "back_bottom", "hhhhhhh h", 12 * mac,
        [low, full, near3, far3, tw, sw, back], [rows_of(height)],
        [
            rows_of(height // 2 + 2), rows_of(REMOTE, 2 * chans), rows_of(REMOTE), rows_of(REMOTE, dtype=F32),
            tw, sw, rows_of(height // 2), wide(height // 2),
        ],
        copies=8, after=[token], alias={6: 0},
    )
    small, token = call(
        sum_kernel, "sum", "v" * levels + " v", mac // 8, [own, *got], [like(BF16, *level_piece)], after=[token]
    )
    got = [lax.ppermute(small, "dp", [(peer(i, k, dp), i) for i in range(dp)]) for k in range(1, dp)]
    spatial, temporal, token = call(
        functools.partial(place_kernel, scale), "place", "s" + "v" * dp + " vv", mac // 8, [q, small, *got],
        [like(F32, dp, rs, chans), like(F32, dp, rt, chans)],
    )
    return (back.reshape(video.shape), spatial.reshape(-1, chans), temporal.reshape(-1, chans))


def solution(mesh):
    placed = (P("dp", "seq", None, None, None), P("dp", "seq", None, None, None), P(), P())
    return jax.shard_map(
        shards,
        mesh=mesh,
        in_specs=placed,
        out_specs=(P("dp", "seq", None, None, None), P("seq", None), P("seq", None)),
        check_vma=False,
    )
```

time: 269 us -> 83.3 us (0.31)
  waiting for transfers between devices: 101 us -> 16.5 us
  local copies, waits for them, and re-layouts: 54 us -> 1.29 us
  matrix products: 51.1 us -> 0 us
  Pallas kernels: 0 us -> 40.9 us
  other arithmetic: 33.2 us -> 0 us
  between operations: 13.9 us -> 1.02 us
  starting transfers between devices: 15.5 us -> 23.1 us
    dot_general x33 -> x0, matrix products: 51.1 us -> none  [the longest x9 25.7 us: shards(): jnp.einsum('hwd,cd->hwc', grad_pad2[2 - a:2 - a + height, 2 - b:2 - b + w...]
    all_to_all x3 -> x0, waiting for transfers between devices: 44.2 us -> none  [the longest x1 24 us: shards(): lax.all_to_all(grad_rows_h, 'seq', split_axis=0, concat_axis=1, tiled=True)]
    pallas_call x0 -> x10, Pallas kernels: none -> 40.9 us  [call(): pl.pallas_call(body, out_shape=[*outs, TOKEN], in_specs=[SPACE[c] for c i...]
    psum x1 -> x0, waiting for transfers between devices: 37.5 us -> none  [reduce_grads(): whole = lax.psum(partial_sum, 'dp')]
    unnamed x2 -> x0, other arithmetic: 28.3 us -> none
    unnamed x31 -> x12, local copies, waits for them, and re-layouts: 27.7 us -> 1.29 us
    ppermute x0 -> x16, starting transfers between devices: none -> 23.1 us  [the longest x1 5.2 us: shards(): above = lax.ppermute(slices[0], 'seq', up)]
    reduce_scatter x2 -> x0, waiting for transfers between devices: 18.9 us -> none  [reduce_grads(): return lax.psum_scatter(whole, 'seq', scatter_dimension=0, tiled=True)]
  transfers between devices with their start and end apart: 6 -> 16, of which waited for: 4 -> 9; matrix products, arithmetic and copies ran while one was open for 36% -> 0% of each run, Pallas kernels for 0% -> 37%
where the time goes in v2:
time: 83.3 us; the launch traced here: 82.9 us
  Pallas kernels  40.9 us (49%)
  starting transfers between devices  23.1 us (28%)
  waiting for transfers between devices  16.5 us (20%)
  local copies, waits for them, and re-layouts  1.29 us (2%)
  between operations  1.02 us (1%)
    pallas_call x10, Pallas kernels, call(): pl.pallas_call(body, out_shape=[*outs, TOKEN], in_specs=[SPACE[c] for c i...  40.9 us
    ppermute x3, waiting for transfers between devices, shards(): lax.ppermute(s, 'dp', [(i, peer(i, k, dp)) for i in range(dp)])  5.58 us
    ppermute x1, starting transfers between devices, shards(): above = lax.ppermute(slices[0], 'seq', up)  5.2 us
    ppermute x1, waiting for transfers between devices, shards(): far = lax.ppermute(slices[1], 'seq', down)  4.83 us
    ppermute x3, starting transfers between devices, shards(): lax.ppermute(s, 'seq', [(i, 2 * peer(i // 2, k, levels) + i % 2) for i in...  4.45 us
    ppermute x3, starting transfers between devices, shards(): lax.ppermute(s, 'dp', [(i, peer(i, k, dp)) for i in range(dp)])  3.57 us
    ppermute x3, starting transfers between devices, shards(): lax.ppermute(small, 'dp', [(peer(i, k, dp), i) for i in range(dp)])  3.55 us
    ppermute x3, waiting for transfers between devices, shards(): lax.ppermute(small, 'dp', [(peer(i, k, dp), i) for i in range(dp)])  3.46 us
  transfers between devices with their start and end apart: 16, of which 9 were waited for; matrix products, arithmetic and copies ran while one was open for 0% of the time, Pallas kernels for 37%

profile of v2, /device:TPU:0, one launch (start us, length us, event | category | flops | bytes accessed | tf_op | source)
XLA Modules:
  0.0 82.9 jit_solution(16232201255610836747)
XLA Ops:
  1.2 3.3 %cut.1 = (bf16[1120,256]{1,0:T(8,128)(2,1)}, bf16[1600,256]{1,0:T(8,128)(2,1)}, bf16[960,256]{1,0:T(8,128)(2,1)}, f32[8,128]{1,0:T(8,128)}) custom-call(bf16[2560,256]{1,0:T(8,128)(2,1)} %bitcast.13, bf16[2560,256]{1,0:T(8,128)(2,1)} %bitcast.9, bf16[2560,256]{1,0:T(8,128)(2,1)} %bitcast.10), custom_call_target="tpu_custom_call" | custom-call | bytes 5816320 | tf_op jit(solution)/shard_map/cut/pallas_call | solution.py:50
  4.5 5.2 %collective-permute-start.1 = (bf16[1120,256]{1,0:T(8,128)(2,1)}, bf16[1120,256]{1,0:T(8,128)(2,1)}, u32[]{:S(2)}, u32[]{:S(2)}) collective-permute-start(bf16[1120,256]{1,0:T(8,128)(2,1)} %get-tuple-element.39), channel_id=1, source_target_pairs={{0,2},{1,3},{2,4},{3,5},{4,6},{5,7},{8,10},{9,11},{10,12},{11,13},... | collective-permute-start | bytes 1720328 | tf_op jit(solution)/shard_map/ppermute | solution.py:438
  9.7 1.3 %collective-permute-start = (bf16[1600,256]{1,0:T(8,128)(2,1)}, bf16[1600,256]{1,0:T(8,128)(2,1)}, u32[]{:S(2)}, u32[]{:S(2)}) collective-permute-start(bf16[1600,256]{1,0:T(8,128)(2,1)} %get-tuple-element.38), channel_id=1, source_target_pairs={{2,0},{3,1},{4,2},{5,3},{6,4},{7,5},{10,8},{11,9},{12,10},{13,11},... | collective-permute-start | bytes 2457608 | tf_op jit(solution)/shard_map/ppermute | solution.py:439
  11.0 1.3 %copy-done.2 = bf16[3,3,256,256]{3,2,1,0:T(8,128)(2,1)S(1)} copy-done((bf16[3,3,256,256]{3,2,1,0:T(8,128)(2,1)S(1)}, bf16[3,3,256,256]{3,2,1,0:T(8,128)(2,1)}, u32[]{:S(2)}) %copy-start.2) | copy-done | bytes 1179672
  12.3 9.6 %local.1 = (bf16[90112,256]{1,0:T(8,128)(2,1)}, f32[45056,256]{1,0:T(8,128)}, f32[9,256,256]{2,1,0:T(8,128)S(1)}, f32[3,256,256]{2,1,0:T(8,128)S(1)}, f32[8,128]{1,0:T(8,128)S(1)}) custom-call(s32[1]{0:T(128)} %bitcast.refs_0_, bf16[2560,256]{1,0:T(8,128)(2,1)S(1)} %bitcast.14, bf16[2560,256]{1,0:T(8,128)(2,1)S(1)} %bitcast.11, ...), custom_call_target="tpu_custom_call" | custom-call | flops 5704253440 | bytes 100925440 | tf_op jit(solution)/shard_map/local/pallas_call | solution.py:50
  22.0 5.3 %remote.1 = (f32[9,256,256]{2,1,0:T(8,128)S(1)}, f32[3,256,256]{2,1,0:T(8,128)S(1)}, f32[8,128]{1,0:T(8,128)S(1)}) custom-call(s32[1]{0:T(128)} %bitcast.refs_0_, bf16[1120,256]{1,0:T(8,128)(2,1)} %collective-permute-done.1.refs_1_, bf16[2560,256]{1,0:T(8,128)(2,1)S(1)} %bitcast.12, bf16[2560,256]{1,0:T(8,128)(2,1)} %collective-permute-done.2.refs_3_, ...), custom_call_target="tpu_custom_call" | custom-call | flops 2684354560 | bytes 11059204 | tf_op jit(solution)/shard_map/remote/pallas_call | solution.py:50
  27.4 4.8 %collective-permute-done.refs_3_ = bf16[1600,256]{1,0:T(8,128)(2,1)} collective-permute-done((bf16[1600,256]{1,0:T(8,128)(2,1)}, bf16[1600,256]{1,0:T(8,128)(2,1)}, u32[]{:S(2)}, u32[]{:S(2)}) %collective-permute-start) | collective-permute-done | bytes 819232 | tf_op jit(solution)/shard_map/ppermute | solution.py:439
  32.2 1.3 %collective-permute-start.3 = (bf16[1600,256]{1,0:T(8,128)(2,1)}, bf16[1600,256]{1,0:T(8,128)(2,1)S(1)}, u32[]{:S(2)}, u32[]{:S(2)}) collective-permute-start(bf16[1600,256]{1,0:T(8,128)(2,1)} %collective-permute-done.refs_3_), channel_id=1, source_target_pairs={{0,1},{2,3},{4,5},{6,7},{8,9},{10,11},{12,13},{14,15},{16,17},{18,... | collective-permute-start | bytes 2457608 | tf_op jit(solution)/shard_map/ppermute | solution.py:461
  33.6 2.1 %collective-permute-done.3.refs_2_ = bf16[1600,256]{1,0:T(8,128)(2,1)S(1)} collective-permute-done((bf16[1600,256]{1,0:T(8,128)(2,1)}, bf16[1600,256]{1,0:T(8,128)(2,1)S(1)}, u32[]{:S(2)}, u32[]{:S(2)}) %collective-permute-start.3) | collective-permute-done | bytes 819232 | tf_op jit(solution)/shard_map/ppermute | solution.py:461
  35.7 8.9 %last.1 = (bf16[90112,256]{1,0:T(8,128)(2,1)}, f32[45056,256]{1,0:T(8,128)}, bf16[4,4,96,256]{3,2,1,0:T(8,128)(2,1)S(1)}, f32[8,128]{1,0:T(8,128)}) custom-call(s32[1]{0:T(128)} %bitcast.refs_0_, bf16[2560,256]{1,0:T(8,128)(2,1)S(1)} %bitcast.15, bf16[1600,256]{1,0:T(8,128)(2,1)S(1)} %collective-permute-done.3.refs_2_, ...), custom_call_target="tpu_custom_call", output_to_operand_aliasing={{0}: (7, {}), {1}: (8, {})} | custom-call | flops 2684354560 | bytes 191823872 | tf_op jit(solution)/shard_map/last/pallas_call | solution.py:50
  45.0 1.5 %collective-permute-start.4 = (bf16[960,256]{1,0:T(8,128)(2,1)}, bf16[960,256]{1,0:T(8,128)(2,1)S(1)}, u32[]{:S(2)}, u32[]{:S(2)}) collective-permute-start(bf16[960,256]{1,0:T(8,128)(2,1)} %get-tuple-element.52), channel_id=1, source_target_pairs={{2,0},{3,1},{4,2},{5,3},{6,4},{7,5},{10,8},{11,9},{12,10},{13,11},... | collective-permute-start | bytes 1474568 | tf_op jit(solution)/shard_map/ppermute | solution.py:440
  46.9 2.4 %split.1 = (f32[4,96,256]{2,1,0:T(8,128)S(1)}, bf16[4,96,256]{2,1,0:T(8,128)(2,1)}, bf16[4,96,256]{2,1,0:T(8,128)(2,1)}, bf16[4,96,256]{2,1,0:T(8,128)(2,1)}, f32[8,128]{1,0:T(8,128)S(1)}) custom-call(s32[1]{0:T(128)} %bitcast.4.refs_0_, f32[45056,256]{1,0:T(8,128)} %get-tuple-element.51.refs_1_, bf16[4,4,96,256]{3,2,1,0:T(8,128)(2,1)S(1)} %collective-permute-done.5.refs_2_), custom_call_target="tpu_custom_call" | custom-call | flops 20971520 | bytes 47906820 | tf_op jit(solution)/shard_map/split/pallas_call | solution.py:50
  49.3 1.6 %collective-permute-start.6 = (bf16[4,96,256]{2,1,0:T(8,128)(2,1)}, bf16[4,96,256]{2,1,0:T(8,128)(2,1)S(1)}, u32[]{:S(2)}, u32[]{:S(2)}) collective-permute-start(bf16[4,96,256]{2,1,0:T(8,128)(2,1)} %get-tuple-element.55), channel_id=1, source_target_pairs={{0,8},{8,0},{16,24},{24,16},{1,9},{9,1},{17,25},{25,17},{2,10},{10... | collective-permute-start | bytes 589832 | tf_op jit(solution)/shard_map/ppermute | solution.py:491
  50.9 1.5 %collective-permute-start.7 = (bf16[4,96,256]{2,1,0:T(8,128)(2,1)}, bf16[4,96,256]{2,1,0:T(8,128)(2,1)S(1)}, u32[]{:S(2)}, u32[]{:S(2)}) collective-permute-start(bf16[4,96,256]{2,1,0:T(8,128)(2,1)} %get-tuple-element.56), channel_id=1, source_target_pairs={{0,16},{8,24},{16,0},{24,8},{1,17},{9,25},{17,1},{25,9},{2,18},{10... | collective-permute-start | bytes 589832 | tf_op jit(solution)/shard_map/ppermute | solution.py:491
  52.9 3.7 %back_top.1 = (bf16[2560,256]{1,0:T(8,128)(2,1)}, f32[8,128]{1,0:T(8,128)S(1)}) custom-call(bf16[90112,256]{1,0:T(8,128)(2,1)} %get-tuple-element.50.refs_0_, bf16[3,3,256,256]{3,2,1,0:T(8,128)(2,1)S(1)} %copy-done.4, f32[8,128]{1,0:T(8,128)S(1)} %get-tuple-element.58.refs_2_), custom_call_target="tpu_custom_call" | custom-call | flops 1509949440 | bytes 48627712 | tf_op jit(solution)/shard_map/back_top/pallas_call | solution.py:50
  57.3 4.9 %collective-permute-done.7.refs_3_ = bf16[4,96,256]{2,1,0:T(8,128)(2,1)S(1)} collective-permute-done((bf16[4,96,256]{2,1,0:T(8,128)(2,1)}, bf16[4,96,256]{2,1,0:T(8,128)(2,1)S(1)}, u32[]{:S(2)}, u32[]{:S(2)}) %collective-permute-start.7) | collective-permute-done | bytes 196640 | tf_op jit(solution)/shard_map/ppermute | solution.py:491
  63.3 1.3 %collective-permute-start.9 = (bf16[960,256]{1,0:T(8,128)(2,1)S(1)}, bf16[960,256]{1,0:T(8,128)(2,1)S(1)}, u32[]{:S(2)}, u32[]{:S(2)}) collective-permute-start(bf16[960,256]{1,0:T(8,128)(2,1)S(1)} %collective-permute-done.4.refs_3_), channel_id=1, source_target_pairs={{0,1},{2,3},{4,5},{6,7},{8,9},{10,11},{12,13},{14,15},{16,17},{18,... | collective-permute-start | bytes 1474568 | tf_op jit(solution)/shard_map/ppermute | solution.py:503
  64.6 1.8 %collective-permute-start.10 = (bf16[96,256]{1,0:T(8,128)(2,1)S(1)}, bf16[96,256]{1,0:T(8,128)(2,1)S(1)}, u32[]{:S(2)}, u32[]{:S(2)}) collective-permute-start(bf16[96,256]{1,0:T(8,128)(2,1)S(1)} %get-tuple-element.66), channel_id=1, source_target_pairs={{0,2},{1,3},{2,0},{3,1},{4,6},{5,7},{6,4},{7,5},{8,10},{9,11},{10,... | collective-permute-start | bytes 147464 | tf_op jit(solution)/shard_map/ppermute | solution.py:505
  66.4 1.8 %collective-permute-start.11 = (bf16[96,256]{1,0:T(8,128)(2,1)S(1)}, bf16[96,256]{1,0:T(8,128)(2,1)S(1)}, u32[]{:S(2)}, u32[]{:S(2)}) collective-permute-start(bf16[96,256]{1,0:T(8,128)(2,1)S(1)} %get-tuple-element.67), channel_id=1, source_target_pairs={{0,4},{1,5},{2,6},{3,7},{4,0},{5,1},{6,2},{7,3},{8,12},{9,13},{10,... | collective-permute-start | bytes 147464 | tf_op jit(solution)/shard_map/ppermute | solution.py:505
  69.1 5.2 %back_bottom.1 = (bf16[2560,256]{1,0:T(8,128)(2,1)}, f32[8,128]{1,0:T(8,128)S(1)}) custom-call(bf16[90112,256]{1,0:T(8,128)(2,1)} %get-tuple-element.50.refs_0_, f32[45056,256]{1,0:T(8,128)} %get-tuple-element.51.refs_1_, bf16[960,256]{1,0:T(8,128)(2,1)S(1)} %collective-permute-done.9.refs_2_, ...), custom_call_target="tpu_custom_call", output_to_operand_aliasing={{0}: (6, {})} | custom-call | flops 2013265920 | bytes 97452032 | tf_op jit(solution)/shard_map/back_bottom/pallas_call | solution.py:50
  74.9 1.5 %collective-permute-start.15 = (bf16[96,256]{1,0:T(8,128)(2,1)S(1)}, bf16[96,256]{1,0:T(8,128)(2,1)S(1)}, u32[]{:S(2)}, u32[]{:S(2)}) collective-permute-start(bf16[96,256]{1,0:T(8,128)(2,1)S(1)} %get-tuple-element.70.refs_1_), channel_id=1, source_target_pairs={{24,0},{16,8},{8,16},{0,24},{25,1},{17,9},{9,17},{1,25},{26,2},{18... | collective-permute-start | bytes 147464 | tf_op jit(solution)/shard_map/ppermute | solution.py:520
  76.4 1.4 %collective-permute-start.14 = (bf16[96,256]{1,0:T(8,128)(2,1)S(1)}, bf16[96,256]{1,0:T(8,128)(2,1)S(1)}, u32[]{:S(2)}, u32[]{:S(2)}) collective-permute-start(bf16[96,256]{1,0:T(8,128)(2,1)S(1)} %get-tuple-element.70.refs_1_), channel_id=1, source_target_pairs={{16,0},{24,8},{0,16},{8,24},{17,1},{25,9},{1,17},{9,25},{18,2},{26... | collective-permute-start | bytes 147464 | tf_op jit(solution)/shard_map/ppermute | solution.py:520
  78.4 1.5 %collective-permute-done.15.refs_4_ = bf16[96,256]{1,0:T(8,128)(2,1)S(1)} collective-permute-done((bf16[96,256]{1,0:T(8,128)(2,1)S(1)}, bf16[96,256]{1,0:T(8,128)(2,1)S(1)}, u32[]{:S(2)}, u32[]{:S(2)}) %collective-permute-start.15) | collective-permute-done | bytes 49184 | tf_op jit(solution)/shard_map/ppermute | solution.py:520
  80.5 1.4 %collective-permute-done.13.refs_2_ = bf16[96,256]{1,0:T(8,128)(2,1)S(1)} collective-permute-done((bf16[96,256]{1,0:T(8,128)(2,1)S(1)}, bf16[96,256]{1,0:T(8,128)(2,1)S(1)}, u32[]{:S(2)}, u32[]{:S(2)}) %collective-permute-start.13) | collective-permute-done | bytes 49184 | tf_op jit(solution)/shard_map/ppermute | solution.py:520
  (30 shorter events, 7.3 us)
Async XLA Ops:
  0.6 10.4 %copy-start = (bf16[1,1,16,160,256]{4,3,2,1,0:T(8,128)(2,1)S(1)}, bf16[1,1,16,160,256]{4,3,2,1,0:T(8,128)(2,1)}, u32[]{:S(2)}) copy-start(bf16[1,1,16,160,256]{4,3,2,1,0:T(8,128)(2,1)} %param.5) | copy-start | bytes 3932164
  0.6 10.4 %copy-start.1 = (bf16[1,1,16,160,256]{4,3,2,1,0:T(8,128)(2,1)S(1)}, bf16[1,1,16,160,256]{4,3,2,1,0:T(8,128)(2,1)}, u32[]{:S(2)}) copy-start(bf16[1,1,16,160,256]{4,3,2,1,0:T(8,128)(2,1)} %param.4) | copy-start | bytes 3932164
  0.7 10.4 %copy-start.5 = (bf16[3,256,256]{2,1,0:T(8,128)(2,1)S(1)}, bf16[3,256,256]{2,1,0:T(8,128)(2,1)}, u32[]{:S(2)}) copy-start(bf16[3,256,256]{2,1,0:T(8,128)(2,1)} %refs_4_.7) | copy-start | bytes 1179652
  0.7 10.3 %collective-permute-start.2 = (bf16[2560,256]{1,0:T(8,128)(2,1)}, bf16[2560,256]{1,0:T(8,128)(2,1)}, u32[]{:S(2)}, u32[]{:S(2)}) collective-permute-start(bf16[2560,256]{1,0:T(8,128)(2,1)} %bitcast.8), channel_id=1, source_target_pairs={{0,1},{1,0},{2,3},{3,2},{4,5},{5,4},{6,7},{7,6},{8,9},{9,8},{10,11... | collective-permute-start | bytes 3932168 | tf_op jit(solution)/shard_map/ppermute | solution.py:432
  4.5 17.6 %collective-permute-start.1 = (bf16[1120,256]{1,0:T(8,128)(2,1)}, bf16[1120,256]{1,0:T(8,128)(2,1)}, u32[]{:S(2)}, u32[]{:S(2)}) collective-permute-start(bf16[1120,256]{1,0:T(8,128)(2,1)} %get-tuple-element.39), channel_id=1, source_target_pairs={{0,2},{1,3},{2,4},{3,5},{4,6},{5,7},{8,10},{9,11},{10,12},{11,13},... | collective-permute-start | bytes 1720328 | tf_op jit(solution)/shard_map/ppermute | solution.py:438
  9.7 22.5 %collective-permute-start = (bf16[1600,256]{1,0:T(8,128)(2,1)}, bf16[1600,256]{1,0:T(8,128)(2,1)}, u32[]{:S(2)}, u32[]{:S(2)}) collective-permute-start(bf16[1600,256]{1,0:T(8,128)(2,1)} %get-tuple-element.38), channel_id=1, source_target_pairs={{2,0},{3,1},{4,2},{5,3},{6,4},{7,5},{10,8},{11,9},{12,10},{13,11},... | collective-permute-start | bytes 2457608 | tf_op jit(solution)/shard_map/ppermute | solution.py:439
  11.0 1.3 %copy-start.2 = (bf16[3,3,256,256]{3,2,1,0:T(8,128)(2,1)S(1)}, bf16[3,3,256,256]{3,2,1,0:T(8,128)(2,1)}, u32[]{:S(2)}) copy-start(bf16[3,3,256,256]{3,2,1,0:T(8,128)(2,1)} %refs_5_.5) | copy-start | bytes 3538948
  12.3 9.8 %copy-start.3 = (bf16[3,3,256,256]{3,2,1,0:T(8,128)(2,1)S(1)}, bf16[3,3,256,256]{3,2,1,0:T(8,128)(2,1)}, u32[]{:S(2)}) copy-start(bf16[3,3,256,256]{3,2,1,0:T(8,128)(2,1)} %refs_5_.5) | copy-start | bytes 3538948
  32.2 3.4 %collective-permute-start.3 = (bf16[1600,256]{1,0:T(8,128)(2,1)}, bf16[1600,256]{1,0:T(8,128)(2,1)S(1)}, u32[]{:S(2)}, u32[]{:S(2)}) collective-permute-start(bf16[1600,256]{1,0:T(8,128)(2,1)} %collective-permute-done.refs_3_), channel_id=1, source_target_pairs={{0,1},{2,3},{4,5},{6,7},{8,9},{10,11},{12,13},{14,15},{16,17},{18,... | collective-permute-start | bytes 2457608 | tf_op jit(solution)/shard_map/ppermute | solution.py:461
  44.5 2.4 %collective-permute-start.5 = (bf16[4,4,96,256]{3,2,1,0:T(8,128)(2,1)S(1)}, bf16[4,4,96,256]{3,2,1,0:T(8,128)(2,1)S(1)}, u32[]{:S(2)}, u32[]{:S(2)}) collective-permute-start(bf16[4,4,96,256]{3,2,1,0:T(8,128)(2,1)S(1)} %get-tuple-element.53), channel_id=1, source_target_pairs={{0,1},{1,0},{2,3},{3,2},{4,5},{5,4},{6,7},{7,6},{8,9},{9,8},{10,11... | collective-permute-start | bytes 2359304 | tf_op jit(solution)/shard_map/ppermute | solution.py:484
  45.0 18.3 %collective-permute-start.4 = (bf16[960,256]{1,0:T(8,128)(2,1)}, bf16[960,256]{1,0:T(8,128)(2,1)S(1)}, u32[]{:S(2)}, u32[]{:S(2)}) collective-permute-start(bf16[960,256]{1,0:T(8,128)(2,1)} %get-tuple-element.52), channel_id=1, source_target_pairs={{2,0},{3,1},{4,2},{5,3},{6,4},{7,5},{10,8},{11,9},{12,10},{13,11},... | collective-permute-start | bytes 1474568 | tf_op jit(solution)/shard_map/ppermute | solution.py:440
  46.9 6.0 %copy-start.4 = (bf16[3,3,256,256]{3,2,1,0:T(8,128)(2,1)S(1)}, bf16[3,3,256,256]{3,2,1,0:T(8,128)(2,1)}, u32[]{:S(2)}) copy-start(bf16[3,3,256,256]{3,2,1,0:T(8,128)(2,1)} %refs_5_.5) | copy-start | bytes 3538948
  49.3 8.0 %collective-permute-start.6 = (bf16[4,96,256]{2,1,0:T(8,128)(2,1)}, bf16[4,96,256]{2,1,0:T(8,128)(2,1)S(1)}, u32[]{:S(2)}, u32[]{:S(2)}) collective-permute-start(bf16[4,96,256]{2,1,0:T(8,128)(2,1)} %get-tuple-element.55), channel_id=1, source_target_pairs={{0,8},{8,0},{16,24},{24,16},{1,9},{9,1},{17,25},{25,17},{2,10},{10... | collective-permute-start | bytes 589832 | tf_op jit(solution)/shard_map/ppermute | solution.py:491
  50.9 11.3 %collective-permute-start.7 = (bf16[4,96,256]{2,1,0:T(8,128)(2,1)}, bf16[4,96,256]{2,1,0:T(8,128)(2,1)S(1)}, u32[]{:S(2)}, u32[]{:S(2)}) collective-permute-start(bf16[4,96,256]{2,1,0:T(8,128)(2,1)} %get-tuple-element.56), channel_id=1, source_target_pairs={{0,16},{8,24},{16,0},{24,8},{1,17},{9,25},{17,1},{25,9},{2,18},{10... | collective-permute-start | bytes 589832 | tf_op jit(solution)/shard_map/ppermute | solution.py:491
  52.4 9.8 %collective-permute-start.8 = (bf16[4,96,256]{2,1,0:T(8,128)(2,1)}, bf16[4,96,256]{2,1,0:T(8,128)(2,1)S(1)}, u32[]{:S(2)}, u32[]{:S(2)}) collective-permute-start(bf16[4,96,256]{2,1,0:T(8,128)(2,1)} %get-tuple-element.57), channel_id=1, source_target_pairs={{0,24},{8,16},{16,8},{24,0},{1,25},{9,17},{17,9},{25,1},{2,26},{10... | collective-permute-start | bytes 589832 | tf_op jit(solution)/shard_map/ppermute | solution.py:491
  63.3 5.8 %collective-permute-start.9 = (bf16[960,256]{1,0:T(8,128)(2,1)S(1)}, bf16[960,256]{1,0:T(8,128)(2,1)S(1)}, u32[]{:S(2)}, u32[]{:S(2)}) collective-permute-start(bf16[960,256]{1,0:T(8,128)(2,1)S(1)} %collective-permute-done.4.refs_3_), channel_id=1, source_target_pairs={{0,1},{2,3},{4,5},{6,7},{8,9},{10,11},{12,13},{14,15},{16,17},{18,... | collective-permute-start | bytes 1474568 | tf_op jit(solution)/shard_map/ppermute | solution.py:503
  64.6 9.6 %collective-permute-start.10 = (bf16[96,256]{1,0:T(8,128)(2,1)S(1)}, bf16[96,256]{1,0:T(8,128)(2,1)S(1)}, u32[]{:S(2)}, u32[]{:S(2)}) collective-permute-start(bf16[96,256]{1,0:T(8,128)(2,1)S(1)} %get-tuple-element.66), channel_id=1, source_target_pairs={{0,2},{1,3},{2,0},{3,1},{4,6},{5,7},{6,4},{7,5},{8,10},{9,11},{10,... | collective-permute-start | bytes 147464 | tf_op jit(solution)/shard_map/ppermute | solution.py:505
  66.4 7.9 %collective-permute-start.11 = (bf16[96,256]{1,0:T(8,128)(2,1)S(1)}, bf16[96,256]{1,0:T(8,128)(2,1)S(1)}, u32[]{:S(2)}, u32[]{:S(2)}) collective-permute-start(bf16[96,256]{1,0:T(8,128)(2,1)S(1)} %get-tuple-element.67), channel_id=1, source_target_pairs={{0,4},{1,5},{2,6},{3,7},{4,0},{5,1},{6,2},{7,3},{8,12},{9,13},{10,... | collective-permute-start | bytes 147464 | tf_op jit(solution)/shard_map/ppermute | solution.py:505
  68.2 6.1 %collective-permute-start.12 = (bf16[96,256]{1,0:T(8,128)(2,1)S(1)}, bf16[96,256]{1,0:T(8,128)(2,1)S(1)}, u32[]{:S(2)}, u32[]{:S(2)}) collective-permute-start(bf16[96,256]{1,0:T(8,128)(2,1)S(1)} %get-tuple-element.68), channel_id=1, source_target_pairs={{0,6},{1,7},{2,4},{3,5},{4,2},{5,3},{6,0},{7,1},{8,14},{9,15},{10,... | collective-permute-start | bytes 147464 | tf_op jit(solution)/shard_map/ppermute | solution.py:505
  74.9 5.1 %collective-permute-start.15 = (bf16[96,256]{1,0:T(8,128)(2,1)S(1)}, bf16[96,256]{1,0:T(8,128)(2,1)S(1)}, u32[]{:S(2)}, u32[]{:S(2)}) collective-permute-start(bf16[96,256]{1,0:T(8,128)(2,1)S(1)} %get-tuple-element.70.refs_1_), channel_id=1, source_target_pairs={{24,0},{16,8},{8,16},{0,24},{25,1},{17,9},{9,17},{1,25},{26,2},{18... | collective-permute-start | bytes 147464 | tf_op jit(solution)/shard_map/ppermute | solution.py:520
  76.4 4.1 %collective-permute-start.14 = (bf16[96,256]{1,0:T(8,128)(2,1)S(1)}, bf16[96,256]{1,0:T(8,128)(2,1)S(1)}, u32[]{:S(2)}, u32[]{:S(2)}) collective-permute-start(bf16[96,256]{1,0:T(8,128)(2,1)S(1)} %get-tuple-element.70.refs_1_), channel_id=1, source_target_pairs={{16,0},{24,8},{0,16},{8,24},{17,1},{25,9},{1,17},{9,25},{18,2},{26... | collective-permute-start | bytes 147464 | tf_op jit(solution)/shard_map/ppermute | solution.py:520
  77.8 4.1 %collective-permute-start.13 = (bf16[96,256]{1,0:T(8,128)(2,1)S(1)}, bf16[96,256]{1,0:T(8,128)(2,1)S(1)}, u32[]{:S(2)}, u32[]{:S(2)}) collective-permute-start(bf16[96,256]{1,0:T(8,128)(2,1)S(1)} %get-tuple-element.70.refs_1_), channel_id=1, source_target_pairs={{8,0},{0,8},{24,16},{16,24},{9,1},{1,9},{25,17},{17,25},{10,2},{2,... | collective-permute-start | bytes 147464 | tf_op jit(solution)/shard_map/ppermute | solution.py:520

commit v3 on v2

v3 whole, which is shorter than its diff:
```python
import functools

import jax
import jax.numpy as jnp
from jax import lax
from jax.experimental import pallas as pl
from jax.experimental.pallas import tpu as pltpu
from jax.sharding import PartitionSpec as P

BF16, F32 = jnp.bfloat16, jnp.float32
EDGE = 8
LIMIT, FULL = 24 * 2**20, 60 * 2**20
REMOTE = 6
SPARE = 45056


def dot(a, b):
    return jnp.dot(a, b, preferred_element_type=F32)


def dot_rt(a, b):
    return lax.dot_general(a, b, (((1,), (1,)), ((), ())), preferred_element_type=F32)


def dot_lt(a, b):
    return lax.dot_general(a, b, (((0,), (0,)), ((), ())), preferred_element_type=F32)


def like(dtype, *shape):
    return jax.ShapeDtypeStruct(shape, dtype)


SPACE = {
    "s": pl.BlockSpec(memory_space=pltpu.SMEM),
    "v": pl.BlockSpec(memory_space=pltpu.VMEM),
    "h": pl.BlockSpec(memory_space=pl.ANY),
}


def call(kernel, name, spaces, flops, args, outs, scratch=(), copies=0, after=(), alias=None, limit=LIMIT):
    nbytes = sum(a.size * a.dtype.itemsize for a in (*args, *outs) if a.shape[0] < SPARE)
    ins, results = spaces.split()
    n_in, n_out = len(args), len(outs)

    def body(*refs):
        rest = refs[n_in + len(after) :]
        kernel(*refs[:n_in], *rest[:n_out], *rest[n_out + 1 :])
        rest[n_out][...] = jnp.zeros(TOKEN.shape, TOKEN.dtype)

    return pl.pallas_call(
        body,
        out_shape=[*outs, TOKEN],
        in_specs=[SPACE[c] for c in ins] + [SPACE["v"]] * len(after),
        out_specs=[SPACE[c] for c in results] + [SPACE["v"]],
        scratch_shapes=[*(pltpu.VMEM(s.shape, s.dtype) for s in scratch), *([pltpu.SemaphoreType.DMA((copies,))] if copies else [])],
        input_output_aliases={} if alias is None else alias,
        compiler_params=pltpu.CompilerParams(vmem_limit_bytes=limit),
        cost_estimate=pl.CostEstimate(flops=flops, bytes_accessed=nbytes, transcendentals=0),
        name=name,
    )(*args, *after)


class Copies:
    def __init__(self, sems):
        self.sems, self.used = sems, 0

    def start(self, *pairs):
        started = []
        for a, b in pairs:
            started.append(pltpu.make_async_copy(a, b, self.sems.at[self.used]))
            self.used += 1
            started[-1].start()
        return started


def wait_all(copies):
    for c in copies:
        c.wait()


def behind(value, token):
    return lax.optimization_barrier((value, token))


TOKEN = like(F32, 8, 128)


def tile(i, size, base=0):
    return pl.ds(pl.multiple_of(base + i * size, size), size)


def loop(steps, body):
    def step(i, carry):
        body(i)
        return carry

    lax.fori_loop(0, steps, step, 0)


def silu_parts(v):
    v = v.astype(F32)
    sig = 0.5 * jnp.tanh(0.5 * v) + 0.5
    act = v * sig
    return act.astype(BF16), sig + act * (1.0 - sig)


def clear_edges(pad):
    n, long, chans = pad.shape
    pad[:, :EDGE] = jnp.zeros((n, EDGE, chans), F32)
    pad[:, long - EDGE :] = jnp.zeros((n, EDGE, chans), F32)


def put_shifts(cat, where, mid, pad):
    n, long, chans = pad.shape
    width = long - 2 * EDGE
    pad[:, EDGE : EDGE + width] = mid.astype(F32).reshape(n, width, chans)
    cat[where, chans : 2 * chans] = mid
    cat[where, :chans] = pad[:, EDGE + 1 : EDGE + 1 + width].astype(BF16).reshape(n * width, chans)
    cat[where, 2 * chans :] = pad[:, EDGE - 1 : EDGE - 1 + width].astype(BF16).reshape(n * width, chans)


def conv_rows(rows3, tap, out, step, wide, at=0):
    _, n, long, chans = wide.shape
    width = long - 2 * EDGE
    for side in range(2):
        clear_edges(wide.at[side])

    def body(i):
        start = i * step
        rows = [rows3[pl.ds(pl.multiple_of(start + a * width, width), step)] for a in range(3)]
        rows = jnp.concatenate(rows, axis=1)
        wide[0, :, EDGE : EDGE + width] = tap(rows, 0).reshape(n, width, chans)
        wide[1, :, EDGE : EDGE + width] = tap(rows, 2).reshape(n, width, chans)
        mid = tap(rows, 1).reshape(n, width, chans)
        mid += wide[0, :, EDGE - 1 : EDGE - 1 + width] + wide[1, :, EDGE + 1 : EDGE + 1 + width]
        out[tile(i, step, at)] = mid.reshape(step, chans).astype(BF16)

    loop((rows3.shape[0] - 2 * width) // step, body)


def forward_tap(sw):
    return lambda rows, b: dot(rows, jnp.concatenate([sw[a, b] for a in range(3)], axis=0))


def back_tap(sw):
    return lambda rows, b: dot_rt(rows, jnp.concatenate([sw[2 - a, 2 - b] for a in range(3)], axis=1))


def tap_parts(video, cat, first, last, base, height, width):
    chans = video.shape[1]
    for a in range(3):
        low, high = max(first, 1 - a), min(last, height + 1 - a)
        rows = video[(low + a - 1 - base) * width : (high + a - 1 - base) * width]
        part = dot_lt(rows, cat[(low - first) * width : (high - first) * width])
        for b in range(3):
            yield 3 * a + b, part[:, b * chans : (b + 1) * chans]


def local_kernel(
    height, width, upper, core, video, cot, mate, sw, tw, hidden_top, rest, spatial, temporal, low,
    rows3, both, sw_v, tw_v, hidden_v, act, cat, wide, pad, grad_v, sems,
):
    rows, chans = video.shape
    top_rows = upper * width
    copies = Copies(sems)
    head = copies.start((video, rows3.at[width : rows + width]), (sw, sw_v))
    tail = copies.start((cot, both.at[:, :chans]), (mate, both.at[:, chans:]), (tw, tw_v))
    rows3[:width] = jnp.zeros((width, chans), BF16)
    rows3[rows + width :] = jnp.zeros((width, chans), BF16)
    clear_edges(pad)
    wait_all(head)
    conv_rows(rows3, forward_tap(sw_v), hidden_v, wide.shape[1] * width, wide)
    wait_all(tail)
    even = core[0] == 0
    tap0 = tw_v[0]
    tap1 = jnp.where(even, tw_v[1], jnp.zeros_like(tap0))
    taps = jnp.concatenate([tap0, tap1], axis=1)
    step = pad.shape[0] * width

    def bottom(i):
        here = pl.ds(pl.multiple_of(top_rows + i * step, width), step)
        act_rows, slope = silu_parts(hidden_v[here])
        act[here] = act_rows
        mid = (dot_rt(both[here], taps) * slope).astype(BF16)
        grad_v[tile(i, step)] = mid
        put_shifts(cat, tile(i, step), mid, pad)

    loop((rows - top_rows) // step, bottom)
    out = copies.start((grad_v, low.at[rows + top_rows : 2 * rows]))
    top_step = top_rows // 2

    def top(i):
        here = tile(i, top_step)
        v = hidden_v[here]
        hidden_top[here] = v
        act[here] = silu_parts(v)[0]
        rest[here] = dot_rt(both[here], taps)

    loop(2, top)
    for tap, part in tap_parts(rows3, cat, upper, height, -1, height, width):
        spatial[tap] = part
    part = dot_lt(act[...], both[...])
    temporal[0] = part[:, :chans]
    temporal[1] = jnp.where(even, part[:, chans:], 0.0)
    temporal[2] = jnp.zeros((chans, chans), F32)
    wait_all(out)


def remote_kernel(
    height, width, upper, core, above, cot, mate, sw, tw, spatial, temporal, spatial_out, temporal_out, grad,
    rows3, both, sw_v, tw_v, other, act, cat, wide, pad, grad_v, sems,
):
    chans = cot.shape[1]
    at = upper * width
    held = above.shape[0]
    copies = Copies(sems)
    head = copies.start((above, rows3.at[:held]), (sw, sw_v))
    tail = copies.start((mate.at[at:], both.at[:, :chans]), (cot.at[at:], both.at[:, chans:]), (tw, tw_v))
    even = core[0] == 0
    clear_edges(pad)
    rows3[held:] = jnp.zeros((width, chans), BF16)
    wait_all(head)
    conv_rows(rows3, forward_tap(sw_v), other, wide.shape[1] * width, wide)
    wait_all(tail)
    tap2 = tw_v[2]
    taps = jnp.concatenate([jnp.where(even, jnp.zeros_like(tap2), tw_v[1]), tap2], axis=1)
    step = pad.shape[0] * width

    def remote(i):
        here = tile(i, step)
        act_rows, slope = silu_parts(other[here])
        act[here] = act_rows
        mid = (dot_rt(both[here], taps) * slope).astype(BF16)
        grad_v[here] = mid
        put_shifts(cat, here, mid, pad)

    loop((height - upper) * width // step, remote)
    out = copies.start((grad_v, grad))
    for tap, part in tap_parts(rows3, cat, upper, height, upper - 1, height, width):
        spatial_out[tap] = spatial[tap] + part
    part = dot_lt(act[...], both[...])
    temporal_out[0] = temporal[0]
    temporal_out[1] = temporal[1] + jnp.where(even, 0.0, part[:, :chans])
    temporal_out[2] = temporal[2] + part[:, chans:]
    wait_all(out)


def own_kernel(
    height, width, upper, plain, core, video, hidden, rest, near, far, tw, spatial, temporal, low_in, low, full, send,
    rows, both, tw_v, act, cat, pad, grad_v, total, total_t, send_v, sems,
):
    count, chans = near.shape
    whole = height * width
    copies = Copies(sems)
    head = copies.start((near, both.at[:, :chans]), (far, both.at[:, chans:]), (tw, tw_v))
    tail = copies.start((video.at[: count + width], rows))
    clear_edges(pad)
    wait_all(head)
    taps = jnp.concatenate([tw_v[1], tw_v[2]], axis=1)
    step = pad.shape[0] * width

    def own(i):
        here = tile(i, step)
        act_rows, slope = silu_parts(hidden[here])
        act[here] = act_rows
        grad = rest[here] + dot_rt(both[here], taps)
        mid = (grad * slope).astype(BF16)
        grad_v[here] = mid
        put_shifts(cat, here, mid, pad)

    loop(count // step, own)
    out = copies.start((grad_v, low.at[whole : whole + count]))
    part = dot_lt(act[...], both[...])
    total_t[:chans] = temporal[0]
    total_t[chans : 2 * chans] = temporal[1] + part[:, :chans]
    total_t[2 * chans :] = temporal[2] + part[:, chans:]
    n, first = total.shape[0], 0
    out += copies.start((total_t, full.at[n : n + total_t.shape[0]]))
    wait_all(tail)
    levels, each = send.shape[:2]
    rt = total_t.shape[0] // (2 * levels)
    rs = each - rt
    for tap, part in tap_parts(rows, cat, 0, upper, 0, height, width):
        total[tap * chans : (tap + 1) * chans] = spatial[tap] + part
        if tap % 3 == 2:
            at = (tap - 2) * chans
            out += copies.start((total.at[at : at + 3 * chans], full.at[at : at + 3 * chans]))
        if plain:
            continue
        while first < levels and (first + 1) * 2 * rs <= (tap + 1) * chans:
            at = 2 * first + 1 - core[0]
            send_v[first, :rs] = total[pl.ds(pl.multiple_of(at * rs, 8), rs)].astype(BF16)
            send_v[first, rs:] = total_t[pl.ds(pl.multiple_of(at * rt, 8), rt)].astype(BF16)
            out += copies.start((send_v.at[first], send.at[first]))
            first += 1
    wait_all(out)


def back_top_kernel(whole, width, low, sw, back, rows3, sw_v, out, wide, sems):
    chans = out.shape[1]
    held = rows3.shape[0] - width
    copies = Copies(sems)
    head = copies.start((low.at[whole : whole + held], rows3.at[width:]), (sw, sw_v))
    rows3[:width] = jnp.zeros((width, chans), BF16)
    wait_all(head)
    conv_rows(rows3, back_tap(sw_v), out, wide.shape[1] * width, wide)
    wait_all(copies.start((out, back.at[: out.shape[0]])))


def back_bottom_kernel(whole, width, low, got, sw, _, back, rows3, got_v, sw_v, out, wide, sems):
    chans = out.shape[1]
    held = rows3.shape[0] - width
    count = got.shape[0]
    copies = Copies(sems)
    head = copies.start((low.at[2 * whole - held : 2 * whole], rows3.at[:held]), (sw, sw_v))
    head += copies.start((got, got_v))
    rows3[held:] = jnp.zeros((width, chans), BF16)
    wait_all(head)

    def add(i):
        here = pl.ds(pl.multiple_of(held - count + i * width, width), width)
        rows3[here] = (rows3[here].astype(F32) + got_v[tile(i, width)].astype(F32)).astype(BF16)

    loop(count // width, add)
    conv_rows(rows3, back_tap(sw_v), out, wide.shape[1] * width, wide)
    wait_all(copies.start((out, back.at[back.shape[0] - out.shape[0] :])))


def peer(index, k, size):
    return index ^ k if size & (size - 1) == 0 else (index + k) % size


def split_kernel(size, where, kept, swapped, own, *refs):
    sends, (keep_v, swapped_v, send_v, sems) = refs[: size - 1], refs[size - 1 :]
    core, q = where[0], where[1]
    levels, each, chans = swapped.shape
    rs = own.shape[1] * 3 // 4
    rt = own.shape[1] - rs
    copies = Copies(sems)
    pairs = [(swapped, swapped_v)]
    for level in range(levels):
        at = 2 * level + core
        low = pl.ds(pl.multiple_of(at * size * rs, 8), size * rs)
        high = pl.ds(pl.multiple_of(2 * levels * size * rs + at * size * rt, 8), size * rt)
        pairs += [(kept.at[low], keep_v.at[level, : size * rs]), (kept.at[high], keep_v.at[level, size * rs :])]
    ins = copies.start(*pairs)
    ins[0].wait()
    for level in range(levels):
        wait_all(ins[1 + 2 * level : 3 + 2 * level])
        keep_v[level] += swapped_v[level].astype(F32)

    def total(i, level):
        low = keep_v[level, pl.ds(pl.multiple_of(i * rs, 8), rs)]
        return jnp.concatenate([low, keep_v[level, pl.ds(pl.multiple_of(size * rs + i * rt, 8), rt)]], axis=0)

    out = []
    for k, send in enumerate(sends):
        for level in range(levels):
            send_v[k, level] = total(peer(q, k + 1, size), level).astype(BF16)
        out += copies.start((send_v.at[k], send))
    for level in range(levels):
        own[level] = total(q, level)
    wait_all(out)


def level_kernel(size, where, own, *refs):
    got = refs[: -size - 2]
    mine, *sends = refs[-size - 2 : -2]
    got_v, sems = refs[-2:]
    level = where[0]
    copies = Copies(sems)
    wait_all(copies.start(*((g, got_v.at[k]) for k, g in enumerate(got))))

    def total(i):
        return sum((got_v[k, i].astype(F32) for k in range(len(got))), own[i])

    mine[...] = total(level)
    for k, out in enumerate(sends, 1):
        out[...] = total(peer(level, k, size)).astype(BF16)


def sum_kernel(own, *refs):
    *got, out = refs
    out[...] = sum((g[...].astype(F32) for g in got), own[...]).astype(BF16)


def place_kernel(scale, where, small, *refs):
    *got, spatial, temporal = refs
    size, rs, rt = len(got) + 1, spatial.shape[1], temporal.shape[1]
    for k, part in enumerate((small, *got)):
        at = peer(where[0], k, size)
        rows = part[...].astype(F32) * scale
        spatial[at] = rows[:rs]
        temporal[at] = rows[rs:]


def shards(video, cotangent, spatial_weight, temporal_weight):
    height, width, chans = (video.shape[2], video.shape[3], video.shape[4])
    rows = height * width
    dp, seq = lax.axis_size("dp"), lax.axis_size("seq")
    levels = seq // 2
    scale = float((dp * video.shape[0] * seq * rows) ** -0.5)
    dp_at, seq_at = lax.axis_index("dp").astype(jnp.int32), lax.axis_index("seq").astype(jnp.int32)
    core, level, q = (v.reshape(1) for v in (seq_at % 2, seq_at // 2, dp_at))
    x = video.reshape(rows, chans)
    cot = cotangent.reshape(rows, chans)
    sw, tw = spatial_weight, temporal_weight
    upper = height - REMOTE
    down = [(i + 2, i) for i in range(seq - 2)]
    up = [(i, i + 2) for i in range(seq - 2)]
    across = [(i, i + 1) for i in range(0, seq, 2)]
    swap = [(i, i ^ 1) for i in range(seq)]

    mac = rows * chans * chans
    long = width + 2 * EDGE
    taps9, taps3 = (like(F32, n, chans, chans) for n in (9, 3))

    def rows_of(n, columns=chans, dtype=BF16):
        return like(dtype, n * width, columns)

    def wide(n):
        return like(F32, 2, n, long, chans)

    mate = lax.ppermute(cot, "seq", swap)
    far = lax.ppermute(cot[: upper * width], "seq", down)
    above = lax.ppermute(x[(upper - 1) * width :], "seq", up)

    def pad(n):
        return like(F32, n, long, chans)

    hidden, rest, spatial, temporal, low, token = call(
        functools.partial(local_kernel, height, width, upper), "local", "shhhhh vvvvh", 34 * mac, [core, x, cot, mate, sw, tw],
        [rows_of(upper), rows_of(upper, dtype=F32), taps9, taps3, like(BF16, 2 * SPARE, chans)],
        [
            rows_of(height + 2), rows_of(height, 2 * chans), sw, tw, rows_of(height), rows_of(height),
            rows_of(REMOTE, 3 * chans), wide(height // 2), pad(REMOTE), rows_of(REMOTE),
        ],
        copies=6,
    )
    far, token = behind(far, token)
    near = lax.ppermute(far, "seq", across)
    spatial, temporal, cross, token = call(
        functools.partial(remote_kernel, height, width, upper), "remote", "shhhhhvv vvh", 16 * mac,
        [core, above, cot, mate, sw, tw, spatial, temporal], [taps9, taps3, rows_of(REMOTE)],
        [
            rows_of(REMOTE + 2), rows_of(REMOTE, 2 * chans), sw, tw, rows_of(REMOTE), rows_of(REMOTE),
            rows_of(REMOTE, 3 * chans), wide(REMOTE), pad(REMOTE), rows_of(REMOTE),
        ],
        copies=6, after=[token],
    )
    rs, rt = 9 * chans // (seq * dp), 3 * chans // (seq * dp)
    plain = bool(rs % 8 or rt % 8 or dp * rs % 16 or dp * rt % 16)
    send = like(BF16, levels, dp * (rs + rt), chans)
    low, full, send, token = call(
        functools.partial(own_kernel, height, width, upper, plain), "own", "shvvhhhvvh hhh", 16 * mac,
        [core, x, hidden, rest, near, far, tw, spatial, temporal, low], [low, like(F32, SPARE, chans), send],
        [
            rows_of(upper + 1), rows_of(upper, 2 * chans), tw, rows_of(upper), rows_of(upper, 3 * chans), pad(upper // 2),
            rows_of(upper), like(F32, 9 * chans, chans), like(F32, 3 * chans, chans), send,
        ],
        copies=9 + levels, after=[token], alias={9: 0},
    )
    piece = (levels, rs + rt, chans)
    if plain:
        parts = (full[: 9 * chans], full[9 * chans : 12 * chans])
        both = jnp.concatenate([g.reshape(levels, 2, dp, -1, chans) for g in parts], axis=3)
        pick = functools.partial(lax.dynamic_index_in_dim, keepdims=False)
        got = lax.ppermute(pick(both, 1 - core[0], 1).astype(BF16), "seq", swap)
        mine = pick(both, core[0], 1) + got.astype(F32)
        own = pick(mine, q[0], 1)
        sends = [pick(mine, peer(q[0], k, dp), 1).astype(BF16) for k in range(1, dp)]
    else:
        got = lax.ppermute(send, "seq", swap)
        own, *sends, token = call(
            functools.partial(split_kernel, dp), "split", "shh v" + "h" * (dp - 1), mac // 8,
            [jnp.concatenate([core, q]), full, got],
            [like(F32, *piece)] + [like(BF16, *piece)] * (dp - 1),
            [like(F32, *send.shape), like(BF16, *send.shape), like(BF16, dp - 1, *piece)],
            copies=2 * levels + dp,
        )
    got = [lax.ppermute(s, "dp", [(i, peer(i, k, dp)) for i in range(dp)]) for k, s in enumerate(sends, 1)]
    cross = lax.ppermute(cross, "seq", down)
    back, token = call(
        functools.partial(back_top_kernel, rows, width), "back_top", "hh h", 9 * mac, [low, sw], [rows_of(height)],
        [rows_of(height // 2 + 2), sw, rows_of(height // 2), wide(height // 2)], copies=3, after=[token],
    )
    level_piece = (rs + rt, chans)
    own, *sends, token = call(
        functools.partial(level_kernel, levels), "level", "sv" + "h" * (dp - 1) + " " + "v" * levels, mac // 8,
        [level, own, *got], [like(F32, *level_piece)] + [like(BF16, *level_piece)] * (levels - 1),
        [like(BF16, dp - 1, *piece)], copies=dp - 1, after=[token],
    )
    got = [
        lax.ppermute(s, "seq", [(i, 2 * peer(i // 2, k, levels) + i % 2) for i in range(seq)])
        for k, s in enumerate(sends, 1)
    ]
    back, token = call(
        functools.partial(back_bottom_kernel, rows, width), "back_bottom", "hhhh h", 9 * mac,
        [low, cross, sw, back], [rows_of(height)],
        [rows_of(height // 2 + 2), rows_of(REMOTE), sw, rows_of(height // 2), wide(height // 2)],
        copies=4, after=[token], alias={3: 0},
    )
    small, token = call(
        sum_kernel, "sum", "v" * levels + " v", mac // 8, [own, *got], [like(BF16, *level_piece)], after=[token]
    )
    got = [lax.ppermute(small, "dp", [(peer(i, k, dp), i) for i in range(dp)]) for k in range(1, dp)]
    spatial, temporal, token = call(
        functools.partial(place_kernel, scale), "place", "s" + "v" * dp + " vv", mac // 8, [q, small, *got],
        [like(F32, dp, rs, chans), like(F32, dp, rt, chans)],
    )
    return (back.reshape(video.shape), spatial.reshape(-1, chans), temporal.reshape(-1, chans))


def solution(mesh):
    placed = (P("dp", "seq", None, None, None), P("dp", "seq", None, None, None), P(), P())
    return jax.shard_map(
        shards,
        mesh=mesh,
        in_specs=placed,
        out_specs=(P("dp", "seq", None, None, None), P("seq", None), P("seq", None)),
        check_vma=False,
    )
```

time: 83.3 us -> 78.8 us (0.946)
  Pallas kernels: 40.9 us -> 33.5 us
  local copies, waits for them, and re-layouts: 1.29 us -> 5.48 us
    pallas_call x10 -> x9, Pallas kernels: 40.9 us -> 33.5 us  [call(): pl.pallas_call(body, out_shape=[*outs, TOKEN], in_specs=[SPACE[c] for c i...]
    slice x0 -> x2, local copies, waits for them, and re-layouts: none -> 3.15 us  [the longest x1 2.3 us: shards(): far = lax.ppermute(cot[:upper * width], 'seq', down)]
    ppermute x1, waiting for transfers between devices: 2.1 us -> 0.01 us  [shards(): near = lax.ppermute(far, 'seq', across)]
    ppermute x3, waiting for transfers between devices: 0.01 us -> 1.83 us  [shards(): lax.ppermute(s, 'seq', [(i, 2 * peer(i // 2, k, levels) + i % 2) for i in...]
    unnamed x12, local copies, waits for them, and re-layouts: 1.29 us -> 2.33 us
    ppermute x4 -> x3, starting transfers between devices: 9.26 us -> 8.44 us  [the longest x1 5.87 us: shards(): above = lax.ppermute(x[(upper - 1) * width:], 'seq', up)]
    ppermute x4 -> x3, waiting for transfers between devices: 4.93 us -> 4.76 us  [the longest x1 4.76 us: shards(): far = lax.ppermute(cot[:upper * width], 'seq', down)]
  transfers between devices with their start and end apart: 16 -> 15, of which waited for: 9 -> 8; matrix products, arithmetic and copies ran while one was open for 0% -> 4% of each run, Pallas kernels for 37% -> 32%
where the time goes in v3:
time: 78.8 us; the launch traced here: 78.4 us
  Pallas kernels  33.5 us (43%)
  starting transfers between devices  22.5 us (29%)
  waiting for transfers between devices  16 us (20%)
  local copies, waits for them, and re-layouts  5.48 us (7%)
  between operations  0.81 us (1%)
    pallas_call x9, Pallas kernels, call(): pl.pallas_call(body, out_shape=[*outs, TOKEN], in_specs=[SPACE[c] for c i...  33.5 us
    ppermute x1, starting transfers between devices, shards(): above = lax.ppermute(x[(upper - 1) * width:], 'seq', up)  5.87 us
    ppermute x3, waiting for transfers between devices, shards(): lax.ppermute(s, 'dp', [(i, peer(i, k, dp)) for i in range(dp)])  4.98 us
    ppermute x1, waiting for transfers between devices, shards(): far = lax.ppermute(cot[:upper * width], 'seq', down)  4.76 us
    ppermute x3, starting transfers between devices, shards(): lax.ppermute(s, 'seq', [(i, 2 * peer(i // 2, k, levels) + i % 2) for i in...  4.45 us
    ppermute x3, starting transfers between devices, shards(): lax.ppermute(s, 'dp', [(i, peer(i, k, dp)) for i in range(dp)])  3.55 us
    ppermute x3, starting transfers between devices, shards(): lax.ppermute(small, 'dp', [(peer(i, k, dp), i) for i in range(dp)])  3.49 us
    ppermute x3, waiting for transfers between devices, shards(): lax.ppermute(small, 'dp', [(peer(i, k, dp), i) for i in range(dp)])  3.28 us
  transfers between devices with their start and end apart: 15, of which 8 were waited for; matrix products, arithmetic and copies ran while one was open for 4% of the time, Pallas kernels for 32%

profile of v3, /device:TPU:0, one launch (start us, length us, event | category | flops | bytes accessed | tf_op | source)
XLA Modules:
  0.0 78.4 jit_solution(5545324260924225652)
XLA Ops:
  1.2 2.3 %slice.12 = bf16[1,1,10,160,256]{4,3,2,1,0:T(8,128)(2,1)} slice(bf16[1,1,16,160,256]{4,3,2,1,0:T(8,128)(2,1)} %param.5), slice={[0:1], [0:1], [0:10], [0:160], [0:256]} | slice | bytes 1638400 | tf_op jit(solution)/shard_map/slice | solution.py:425
  3.5 1.3 %collective-permute-start.1 = (bf16[1600,256]{1,0:T(8,128)(2,1)}, bf16[1600,256]{1,0:T(8,128)(2,1)S(1)}, u32[]{:S(2)}, u32[]{:S(2)}) collective-permute-start(bf16[1600,256]{1,0:T(8,128)(2,1)} %bitcast.3), channel_id=1, source_target_pairs={{2,0},{3,1},{4,2},{5,3},{6,4},{7,5},{10,8},{11,9},{12,10},{13,11},... | collective-permute-start | bytes 2457608 | tf_op jit(solution)/shard_map/ppermute | solution.py:425
  5.6 5.9 %collective-permute-start.3 = (bf16[1120,256]{1,0:T(8,128)(2,1)}, bf16[1120,256]{1,0:T(8,128)(2,1)}, u32[]{:S(2)}, u32[]{:S(2)}) collective-permute-start(bf16[1120,256]{1,0:T(8,128)(2,1)} %bitcast.4), channel_id=1, source_target_pairs={{0,2},{1,3},{2,4},{3,5},{4,6},{5,7},{8,10},{9,11},{10,12},{11,13},... | collective-permute-start | bytes 1720328 | tf_op jit(solution)/shard_map/ppermute | solution.py:426
  11.5 1.3 %copy-done.2 = bf16[1,1,16,160,256]{4,3,2,1,0:T(8,128)(2,1)S(1)} copy-done((bf16[1,1,16,160,256]{4,3,2,1,0:T(8,128)(2,1)S(1)}, bf16[1,1,16,160,256]{4,3,2,1,0:T(8,128)(2,1)}, u32[]{:S(2)}) %copy-start.2) | copy-done | bytes 1310744
  13.8 8.3 %local.1 = (bf16[1600,256]{1,0:T(8,128)(2,1)S(1)}, f32[1600,256]{1,0:T(8,128)S(1)}, f32[9,256,256]{2,1,0:T(8,128)S(1)}, f32[3,256,256]{2,1,0:T(8,128)S(1)}, bf16...) custom-call(s32[1]{0:T(128)} %bitcast.refs_0_, bf16[2560,256]{1,0:T(8,128)(2,1)S(1)} %bitcast.10, ...), custom_call_target="tpu_custom_call" | custom-call | flops 5704253440 | bytes 11108356 | tf_op jit(solution)/shard_map/local/pallas_call | solution.py:50
  22.1 4.8 %collective-permute-done.1.refs_5_ = bf16[1600,256]{1,0:T(8,128)(2,1)S(1)} collective-permute-done((bf16[1600,256]{1,0:T(8,128)(2,1)}, bf16[1600,256]{1,0:T(8,128)(2,1)S(1)}, u32[]{:S(2)}, u32[]{:S(2)}) %collective-permute-start.1) | collective-permute-done | bytes 819232 | tf_op jit(solution)/shard_map/ppermute | solution.py:425
  26.8 2.0 %collective-permute-start.2 = (bf16[1600,256]{1,0:T(8,128)(2,1)S(1)}, bf16[1600,256]{1,0:T(8,128)(2,1)S(1)}, u32[]{:S(2)}, u32[]{:S(2)}) collective-permute-start(bf16[1600,256]{1,0:T(8,128)(2,1)S(1)} %collective-permute-done.1.refs_5_), channel_id=1, source_target_pairs={{0,1},{2,3},{4,5},{6,7},{8,9},{10,11},{12,13},{14,15},{16,17},{18,... | collective-permute-start | bytes 2457608 | tf_op jit(solution)/shard_map/ppermute | solution.py:441
  28.9 5.4 %remote.1 = (f32[9,256,256]{2,1,0:T(8,128)S(1)}, f32[3,256,256]{2,1,0:T(8,128)S(1)}, bf16[960,256]{1,0:T(8,128)(2,1)}, f32[8,128]{1,0:T(8,128)S(1)}) custom-call(s32[1]{0:T(128)} %bitcast.refs_0_, bf16[1120,256]{1,0:T(8,128)(2,1)} %collective-permute-done.3.refs_1_, bf16[2560,256]{1,0:T(8,128)(2,1)S(1)} %bitcast.14, ...), custom_call_target="tpu_custom_call" | custom-call | flops 2684354560 | bytes 11550724 | tf_op jit(solution)/shard_map/remote/pallas_call | solution.py:50
  34.2 7.1 %own.1 = (bf16[90112,256]{1,0:T(8,128)(2,1)}, f32[45056,256]{1,0:T(8,128)}, bf16[4,384,256]{2,1,0:T(8,128)(2,1)}, f32[8,128]{1,0:T(8,128)}) custom-call(s32[1]{0:T(128)} %bitcast.refs_0_, bf16[2560,256]{1,0:T(8,128)(2,1)S(1)} %bitcast.11, bf16[1600,256]{1,0:T(8,128)(2,1)S(1)} %get-tuple-element.35.refs_2_, ...), custom_call_target="tpu_custom_call", output_to_operand_aliasing={{0}: (9, {})} | custom-call | flops 2684354560 | bytes 9732100 | tf_op jit(solution)/shard_map/own/pallas_call | solution.py:50
  41.4 1.3 %collective-permute-start.4 = (bf16[960,256]{1,0:T(8,128)(2,1)}, bf16[960,256]{1,0:T(8,128)(2,1)S(1)}, u32[]{:S(2)}, u32[]{:S(2)}) collective-permute-start(bf16[960,256]{1,0:T(8,128)(2,1)} %get-tuple-element.47), channel_id=1, source_target_pairs={{2,0},{3,1},{4,2},{5,3},{6,4},{7,5},{10,8},{11,9},{12,10},{13,11},... | collective-permute-start | bytes 1474568 | tf_op jit(solution)/shard_map/ppermute | solution.py:482
  42.8 1.1 %collective-permute-done.5.refs_2_ = bf16[4,384,256]{2,1,0:T(8,128)(2,1)S(1)} collective-permute-done((bf16[4,384,256]{2,1,0:T(8,128)(2,1)}, bf16[4,384,256]{2,1,0:T(8,128)(2,1)S(1)}, u32[]{:S(2)}, u32[]{:S(2)}) %collective-permute-start.5) | collective-permute-done | bytes 786464 | tf_op jit(solution)/shard_map/ppermute | solution.py:473
  43.9 3.0 %split.1 = (f32[4,96,256]{2,1,0:T(8,128)S(1)}, bf16[4,96,256]{2,1,0:T(8,128)(2,1)S(1)}, bf16[4,96,256]{2,1,0:T(8,128)(2,1)S(1)}, bf16[4,96,256]{2,1,0:T(8,128)(2,1)S(1)}, f32[8,128]{1,0:T(8,128)S(1)}) custom-call(s32[2]{0:T(128)S(1)} %pad_add_fusion.refs_0_, f32[45056,256]{1,0:T(8,128)} %get-tuple-element.48.refs_1_, ...), custom_call_target="tpu_custom_call" | custom-call | flops 20971520 | bytes 1769480 | tf_op jit(solution)/shard_map/split/pallas_call | solution.py:50
  46.9 1.4 %collective-permute-start.6 = (bf16[4,96,256]{2,1,0:T(8,128)(2,1)S(1)}, bf16[4,96,256]{2,1,0:T(8,128)(2,1)S(1)}, u32[]{:S(2)}, u32[]{:S(2)}) collective-permute-start(bf16[4,96,256]{2,1,0:T(8,128)(2,1)S(1)} %get-tuple-element.53), channel_id=1, source_target_pairs={{0,8},{8,0},{16,24},{24,16},{1,9},{9,1},{17,25},{25,17},{2,10},{10... | collective-permute-start | bytes 589832 | tf_op jit(solution)/shard_map/ppermute | solution.py:481
  48.3 1.5 %collective-permute-start.7 = (bf16[4,96,256]{2,1,0:T(8,128)(2,1)S(1)}, bf16[4,96,256]{2,1,0:T(8,128)(2,1)S(1)}, u32[]{:S(2)}, u32[]{:S(2)}) collective-permute-start(bf16[4,96,256]{2,1,0:T(8,128)(2,1)S(1)} %get-tuple-element.54), channel_id=1, source_target_pairs={{0,16},{8,24},{16,0},{24,8},{1,17},{9,25},{17,1},{25,9},{2,18},{10... | collective-permute-start | bytes 589832 | tf_op jit(solution)/shard_map/ppermute | solution.py:481
  50.5 3.7 %back_top.1 = (bf16[2560,256]{1,0:T(8,128)(2,1)}, f32[8,128]{1,0:T(8,128)S(1)}) custom-call(bf16[90112,256]{1,0:T(8,128)(2,1)} %get-tuple-element.46.refs_0_, bf16[3,3,256,256]{3,2,1,0:T(8,128)(2,1)S(1)} %copy-done, f32[8,128]{1,0:T(8,128)S(1)} %get-tuple-element.50.refs_2_), custom_call_target="tpu_custom_call" | custom-call | flops 1509949440 | bytes 2490368 | tf_op jit(solution)/shard_map/back_top/pallas_call | solution.py:50
  54.7 4.5 %collective-permute-done.7.refs_3_ = bf16[4,96,256]{2,1,0:T(8,128)(2,1)S(1)} collective-permute-done((bf16[4,96,256]{2,1,0:T(8,128)(2,1)S(1)}, bf16[4,96,256]{2,1,0:T(8,128)(2,1)S(1)}, u32[]{:S(2)}, u32[]{:S(2)}) %collective-permute-start.7) | collective-permute-done | bytes 196640 | tf_op jit(solution)/shard_map/ppermute | solution.py:481
  60.0 1.7 %collective-permute-start.9 = (bf16[96,256]{1,0:T(8,128)(2,1)S(1)}, bf16[96,256]{1,0:T(8,128)(2,1)S(1)}, u32[]{:S(2)}, u32[]{:S(2)}) collective-permute-start(bf16[96,256]{1,0:T(8,128)(2,1)S(1)} %get-tuple-element.60), channel_id=1, source_target_pairs={{0,2},{1,3},{2,0},{3,1},{4,6},{5,7},{6,4},{7,5},{8,10},{9,11},{10,... | collective-permute-start | bytes 147464 | tf_op jit(solution)/shard_map/ppermute | solution.py:494
  61.7 2.6 %collective-permute-start.10 = (bf16[96,256]{1,0:T(8,128)(2,1)S(1)}, bf16[96,256]{1,0:T(8,128)(2,1)S(1)}, u32[]{:S(2)}, u32[]{:S(2)}) collective-permute-start(bf16[96,256]{1,0:T(8,128)(2,1)S(1)} %get-tuple-element.61), channel_id=1, source_target_pairs={{0,4},{1,5},{2,6},{3,7},{4,0},{5,1},{6,2},{7,3},{8,12},{9,13},{10,... | collective-permute-start | bytes 147464 | tf_op jit(solution)/shard_map/ppermute | solution.py:494
  64.5 3.9 %back_bottom.1 = (bf16[2560,256]{1,0:T(8,128)(2,1)}, f32[8,128]{1,0:T(8,128)S(1)}) custom-call(bf16[90112,256]{1,0:T(8,128)(2,1)} %get-tuple-element.46.refs_0_, bf16[960,256]{1,0:T(8,128)(2,1)S(1)} %collective-permute-done.4.refs_1_, bf16[3,3,256,256]{3,2,1,0:T(8,128)(2,1)S(1)} %copy-done, ...), custom_call_target="tpu_custom_call", output_to_operand_aliasing={{0}: (3, {})} | custom-call | flops 1509949440 | bytes 4292608 | tf_op jit(solution)/shard_map/back_bottom/pallas_call | solution.py:50
  68.4 1.8 %collective-permute-done.11.refs_3_ = bf16[96,256]{1,0:T(8,128)(2,1)S(1)} collective-permute-done((bf16[96,256]{1,0:T(8,128)(2,1)S(1)}, bf16[96,256]{1,0:T(8,128)(2,1)S(1)}, u32[]{:S(2)}, u32[]{:S(2)}) %collective-permute-start.11) | collective-permute-done | bytes 49184 | tf_op jit(solution)/shard_map/ppermute | solution.py:494
  70.8 1.5 %collective-permute-start.14 = (bf16[96,256]{1,0:T(8,128)(2,1)S(1)}, bf16[96,256]{1,0:T(8,128)(2,1)S(1)}, u32[]{:S(2)}, u32[]{:S(2)}) collective-permute-start(bf16[96,256]{1,0:T(8,128)(2,1)S(1)} %get-tuple-element.64.refs_1_), channel_id=1, source_target_pairs={{24,0},{16,8},{8,16},{0,24},{25,1},{17,9},{9,17},{1,25},{26,2},{18... | collective-permute-start | bytes 147464 | tf_op jit(solution)/shard_map/ppermute | solution.py:506
  72.3 1.2 %collective-permute-start.13 = (bf16[96,256]{1,0:T(8,128)(2,1)S(1)}, bf16[96,256]{1,0:T(8,128)(2,1)S(1)}, u32[]{:S(2)}, u32[]{:S(2)}) collective-permute-start(bf16[96,256]{1,0:T(8,128)(2,1)S(1)} %get-tuple-element.64.refs_1_), channel_id=1, source_target_pairs={{16,0},{24,8},{0,16},{8,24},{17,1},{25,9},{1,17},{9,25},{18,2},{26... | collective-permute-start | bytes 147464 | tf_op jit(solution)/shard_map/ppermute | solution.py:506
  74.3 1.5 %collective-permute-done.14.refs_4_ = bf16[96,256]{1,0:T(8,128)(2,1)S(1)} collective-permute-done((bf16[96,256]{1,0:T(8,128)(2,1)S(1)}, bf16[96,256]{1,0:T(8,128)(2,1)S(1)}, u32[]{:S(2)}, u32[]{:S(2)}) %collective-permute-start.14) | collective-permute-done | bytes 49184 | tf_op jit(solution)/shard_map/ppermute | solution.py:506
  76.4 1.2 %collective-permute-done.12.refs_2_ = bf16[96,256]{1,0:T(8,128)(2,1)S(1)} collective-permute-done((bf16[96,256]{1,0:T(8,128)(2,1)S(1)}, bf16[96,256]{1,0:T(8,128)(2,1)S(1)}, u32[]{:S(2)}, u32[]{:S(2)}) %collective-permute-start.12) | collective-permute-done | bytes 49184 | tf_op jit(solution)/shard_map/ppermute | solution.py:506
  (30 shorter events, 7.5 us)
Async XLA Ops:
  0.6 4.1 %copy-start.1 = (bf16[1,1,16,160,256]{4,3,2,1,0:T(8,128)(2,1)S(1)}, bf16[1,1,16,160,256]{4,3,2,1,0:T(8,128)(2,1)}, u32[]{:S(2)}) copy-start(bf16[1,1,16,160,256]{4,3,2,1,0:T(8,128)(2,1)} %param.4) | copy-start | bytes 3932164
  0.6 10.9 %copy-start = (bf16[3,3,256,256]{3,2,1,0:T(8,128)(2,1)S(1)}, bf16[3,3,256,256]{3,2,1,0:T(8,128)(2,1)}, u32[]{:S(2)}) copy-start(bf16[3,3,256,256]{3,2,1,0:T(8,128)(2,1)} %refs_2_.1) | copy-start | bytes 3538948
  0.6 10.8 %collective-permute-start = (bf16[2560,256]{1,0:T(8,128)(2,1)}, bf16[2560,256]{1,0:T(8,128)(2,1)}, u32[]{:S(2)}, u32[]{:S(2)}) collective-permute-start(bf16[2560,256]{1,0:T(8,128)(2,1)} %bitcast.12), channel_id=1, source_target_pairs={{0,1},{1,0},{2,3},{3,2},{4,5},{5,4},{6,7},{7,6},{8,9},{9,8},{10,11... | collective-permute-start | bytes 3932168 | tf_op jit(solution)/shard_map/ppermute | solution.py:424
  3.5 23.4 %collective-permute-start.1 = (bf16[1600,256]{1,0:T(8,128)(2,1)}, bf16[1600,256]{1,0:T(8,128)(2,1)S(1)}, u32[]{:S(2)}, u32[]{:S(2)}) collective-permute-start(bf16[1600,256]{1,0:T(8,128)(2,1)} %bitcast.3), channel_id=1, source_target_pairs={{2,0},{3,1},{4,2},{5,3},{6,4},{7,5},{10,8},{11,9},{12,10},{13,11},... | collective-permute-start | bytes 2457608 | tf_op jit(solution)/shard_map/ppermute | solution.py:425
  5.6 23.2 %collective-permute-start.3 = (bf16[1120,256]{1,0:T(8,128)(2,1)}, bf16[1120,256]{1,0:T(8,128)(2,1)}, u32[]{:S(2)}, u32[]{:S(2)}) collective-permute-start(bf16[1120,256]{1,0:T(8,128)(2,1)} %bitcast.4), channel_id=1, source_target_pairs={{0,2},{1,3},{2,4},{3,5},{4,6},{5,7},{8,10},{9,11},{10,12},{11,13},... | collective-permute-start | bytes 1720328 | tf_op jit(solution)/shard_map/ppermute | solution.py:426
  11.5 1.3 %copy-start.2 = (bf16[1,1,16,160,256]{4,3,2,1,0:T(8,128)(2,1)S(1)}, bf16[1,1,16,160,256]{4,3,2,1,0:T(8,128)(2,1)}, u32[]{:S(2)}) copy-start(bf16[1,1,16,160,256]{4,3,2,1,0:T(8,128)(2,1)} %param.5) | copy-start | bytes 3932164
  12.8 1.0 %copy-start.4 = (bf16[3,256,256]{2,1,0:T(8,128)(2,1)S(1)}, bf16[3,256,256]{2,1,0:T(8,128)(2,1)}, u32[]{:S(2)}) copy-start(bf16[3,256,256]{2,1,0:T(8,128)(2,1)} %refs_6_.1) | copy-start | bytes 1179652
  13.8 15.0 %copy-start.3 = (bf16[1,1,16,160,256]{4,3,2,1,0:T(8,128)(2,1)S(1)}, bf16[1,1,16,160,256]{4,3,2,1,0:T(8,128)(2,1)}, u32[]{:S(2)}) copy-start(bf16[1,1,16,160,256]{4,3,2,1,0:T(8,128)(2,1)} %param.5) | copy-start | bytes 3932164
  13.8 15.0 %copy-start.5 = (bf16[3,256,256]{2,1,0:T(8,128)(2,1)S(1)}, bf16[3,256,256]{2,1,0:T(8,128)(2,1)}, u32[]{:S(2)}) copy-start(bf16[3,256,256]{2,1,0:T(8,128)(2,1)} %refs_6_.1) | copy-start | bytes 1179652
  26.8 7.4 %collective-permute-start.2 = (bf16[1600,256]{1,0:T(8,128)(2,1)S(1)}, bf16[1600,256]{1,0:T(8,128)(2,1)S(1)}, u32[]{:S(2)}, u32[]{:S(2)}) collective-permute-start(bf16[1600,256]{1,0:T(8,128)(2,1)S(1)} %collective-permute-done.1.refs_5_), channel_id=1, source_target_pairs={{0,1},{2,3},{4,5},{6,7},{8,9},{10,11},{12,13},{14,15},{16,17},{18,... | collective-permute-start | bytes 2457608 | tf_op jit(solution)/shard_map/ppermute | solution.py:441
  41.4 2.6 %collective-permute-start.5 = (bf16[4,384,256]{2,1,0:T(8,128)(2,1)}, bf16[4,384,256]{2,1,0:T(8,128)(2,1)S(1)}, u32[]{:S(2)}, u32[]{:S(2)}) collective-permute-start(bf16[4,384,256]{2,1,0:T(8,128)(2,1)} %get-tuple-element.49), channel_id=1, source_target_pairs={{0,1},{1,0},{2,3},{3,2},{4,5},{5,4},{6,7},{7,6},{8,9},{9,8},{10,11... | collective-permute-start | bytes 2359304 | tf_op jit(solution)/shard_map/ppermute | solution.py:473
  41.4 23.1 %collective-permute-start.4 = (bf16[960,256]{1,0:T(8,128)(2,1)}, bf16[960,256]{1,0:T(8,128)(2,1)S(1)}, u32[]{:S(2)}, u32[]{:S(2)}) collective-permute-start(bf16[960,256]{1,0:T(8,128)(2,1)} %get-tuple-element.47), channel_id=1, source_target_pairs={{2,0},{3,1},{4,2},{5,3},{6,4},{7,5},{10,8},{11,9},{12,10},{13,11},... | collective-permute-start | bytes 1474568 | tf_op jit(solution)/shard_map/ppermute | solution.py:482
  46.9 7.8 %collective-permute-start.6 = (bf16[4,96,256]{2,1,0:T(8,128)(2,1)S(1)}, bf16[4,96,256]{2,1,0:T(8,128)(2,1)S(1)}, u32[]{:S(2)}, u32[]{:S(2)}) collective-permute-start(bf16[4,96,256]{2,1,0:T(8,128)(2,1)S(1)} %get-tuple-element.53), channel_id=1, source_target_pairs={{0,8},{8,0},{16,24},{24,16},{1,9},{9,1},{17,25},{25,17},{2,10},{10... | collective-permute-start | bytes 589832 | tf_op jit(solution)/shard_map/ppermute | solution.py:481
  48.3 10.9 %collective-permute-start.7 = (bf16[4,96,256]{2,1,0:T(8,128)(2,1)S(1)}, bf16[4,96,256]{2,1,0:T(8,128)(2,1)S(1)}, u32[]{:S(2)}, u32[]{:S(2)}) collective-permute-start(bf16[4,96,256]{2,1,0:T(8,128)(2,1)S(1)} %get-tuple-element.54), channel_id=1, source_target_pairs={{0,16},{8,24},{16,0},{24,8},{1,17},{9,25},{17,1},{25,9},{2,18},{10... | collective-permute-start | bytes 589832 | tf_op jit(solution)/shard_map/ppermute | solution.py:481
  49.8 9.4 %collective-permute-start.8 = (bf16[4,96,256]{2,1,0:T(8,128)(2,1)S(1)}, bf16[4,96,256]{2,1,0:T(8,128)(2,1)S(1)}, u32[]{:S(2)}, u32[]{:S(2)}) collective-permute-start(bf16[4,96,256]{2,1,0:T(8,128)(2,1)S(1)} %get-tuple-element.55), channel_id=1, source_target_pairs={{0,24},{8,16},{16,8},{24,0},{1,25},{9,17},{17,9},{25,1},{2,26},{10... | collective-permute-start | bytes 589832 | tf_op jit(solution)/shard_map/ppermute | solution.py:481
  60.0 8.3 %collective-permute-start.9 = (bf16[96,256]{1,0:T(8,128)(2,1)S(1)}, bf16[96,256]{1,0:T(8,128)(2,1)S(1)}, u32[]{:S(2)}, u32[]{:S(2)}) collective-permute-start(bf16[96,256]{1,0:T(8,128)(2,1)S(1)} %get-tuple-element.60), channel_id=1, source_target_pairs={{0,2},{1,3},{2,0},{3,1},{4,6},{5,7},{6,4},{7,5},{8,10},{9,11},{10,... | collective-permute-start | bytes 147464 | tf_op jit(solution)/shard_map/ppermute | solution.py:494
  61.7 6.7 %collective-permute-start.10 = (bf16[96,256]{1,0:T(8,128)(2,1)S(1)}, bf16[96,256]{1,0:T(8,128)(2,1)S(1)}, u32[]{:S(2)}, u32[]{:S(2)}) collective-permute-start(bf16[96,256]{1,0:T(8,128)(2,1)S(1)} %get-tuple-element.61), channel_id=1, source_target_pairs={{0,4},{1,5},{2,6},{3,7},{4,0},{5,1},{6,2},{7,3},{8,12},{9,13},{10,... | collective-permute-start | bytes 147464 | tf_op jit(solution)/shard_map/ppermute | solution.py:494
  64.3 5.9 %collective-permute-start.11 = (bf16[96,256]{1,0:T(8,128)(2,1)S(1)}, bf16[96,256]{1,0:T(8,128)(2,1)S(1)}, u32[]{:S(2)}, u32[]{:S(2)}) collective-permute-start(bf16[96,256]{1,0:T(8,128)(2,1)S(1)} %get-tuple-element.62), channel_id=1, source_target_pairs={{0,6},{1,7},{2,4},{3,5},{4,2},{5,3},{6,0},{7,1},{8,14},{9,15},{10,... | collective-permute-start | bytes 147464 | tf_op jit(solution)/shard_map/ppermute | solution.py:494
  70.8 5.0 %collective-permute-start.14 = (bf16[96,256]{1,0:T(8,128)(2,1)S(1)}, bf16[96,256]{1,0:T(8,128)(2,1)S(1)}, u32[]{:S(2)}, u32[]{:S(2)}) collective-permute-start(bf16[96,256]{1,0:T(8,128)(2,1)S(1)} %get-tuple-element.64.refs_1_), channel_id=1, source_target_pairs={{24,0},{16,8},{8,16},{0,24},{25,1},{17,9},{9,17},{1,25},{26,2},{18... | collective-permute-start | bytes 147464 | tf_op jit(solution)/shard_map/ppermute | solution.py:506
  72.3 4.1 %collective-permute-start.13 = (bf16[96,256]{1,0:T(8,128)(2,1)S(1)}, bf16[96,256]{1,0:T(8,128)(2,1)S(1)}, u32[]{:S(2)}, u32[]{:S(2)}) collective-permute-start(bf16[96,256]{1,0:T(8,128)(2,1)S(1)} %get-tuple-element.64.refs_1_), channel_id=1, source_target_pairs={{16,0},{24,8},{0,16},{8,24},{17,1},{25,9},{1,17},{9,25},{18,2},{26... | collective-permute-start | bytes 147464 | tf_op jit(solution)/shard_map/ppermute | solution.py:506
  73.5 4.1 %collective-permute-start.12 = (bf16[96,256]{1,0:T(8,128)(2,1)S(1)}, bf16[96,256]{1,0:T(8,128)(2,1)S(1)}, u32[]{:S(2)}, u32[]{:S(2)}) collective-permute-start(bf16[96,256]{1,0:T(8,128)(2,1)S(1)} %get-tuple-element.64.refs_1_), channel_id=1, source_target_pairs={{8,0},{0,8},{24,16},{16,24},{9,1},{1,9},{25,17},{17,25},{10,2},{2,... | collective-permute-start | bytes 147464 | tf_op jit(solution)/shard_map/ppermute | solution.py:506

commit v4 on v3

--- a/solution.py
+++ b/solution.py
@@ -10,7 +10,7 @@
 BF16, F32 = jnp.bfloat16, jnp.float32
 EDGE = 8
 LIMIT, FULL = 24 * 2**20, 60 * 2**20
-REMOTE = 6
+REMOTE = 7
 SPARE = 45056
 
 
@@ -97,6 +97,10 @@
     lax.fori_loop(0, steps, step, 0)
 
 
+def chunk(n):
+    return n if n < 8 else max(d for d in range(1, 7) if n % d == 0)
+
+
 def silu_parts(v):
     v = v.astype(F32)
     sig = 0.5 * jnp.tanh(0.5 * v) + 0.5
@@ -119,23 +123,27 @@
     cat[where, 2 * chans :] = pad[:, EDGE - 1 : EDGE - 1 + width].astype(BF16).reshape(n * width, chans)
 
 
-def conv_rows(rows3, tap, out, step, wide, at=0):
-    _, n, long, chans = wide.shape
-    width = long - 2 * EDGE
-    for side in range(2):
-        clear_edges(wide.at[side])
+def conv_rows(rows3, tap, out, step, wide):
+    width = wide.shape[2] - 2 * EDGE
 
     def body(i):
         start = i * step
         rows = [rows3[pl.ds(pl.multiple_of(start + a * width, width), step)] for a in range(3)]
-        rows = jnp.concatenate(rows, axis=1)
-        wide[0, :, EDGE : EDGE + width] = tap(rows, 0).reshape(n, width, chans)
-        wide[1, :, EDGE : EDGE + width] = tap(rows, 2).reshape(n, width, chans)
-        mid = tap(rows, 1).reshape(n, width, chans)
-        mid += wide[0, :, EDGE - 1 : EDGE - 1 + width] + wide[1, :, EDGE + 1 : EDGE + 1 + width]
-        out[tile(i, step, at)] = mid.reshape(step, chans).astype(BF16)
-
+        conv_tile(jnp.concatenate(rows, axis=1), tap, out, tile(i, step), wide)
+
+    for side in range(2):
+        clear_edges(wide.at[side])
     loop((rows3.shape[0] - 2 * width) // step, body)
+
+
+def conv_tile(rows, tap, out, where, wide):
+    _, n, long, chans = wide.shape
+    width = long - 2 * EDGE
+    wide[0, :, EDGE : EDGE + width] = tap(rows, 0).reshape(n, width, chans)
+    wide[1, :, EDGE : EDGE + width] = tap(rows, 2).reshape(n, width, chans)
+    mid = tap(rows, 1).reshape(n, width, chans)
+    mid += wide[0, :, EDGE - 1 : EDGE - 1 + width] + wide[1, :, EDGE + 1 : EDGE + 1 + width]
+    out[where] = mid.reshape(n * width, chans).astype(BF16)
 
 
 def forward_tap(sw):
@@ -157,8 +165,8 @@
 
 
 def local_kernel(
-    height, width, upper, core, video, cot, mate, sw, tw, hidden_top, rest, spatial, temporal, low,
-    rows3, both, sw_v, tw_v, hidden_v, act, cat, wide, pad, grad_v, sems,
+    height, width, upper, core, video, cot, mate, sw, tw, act_top, slope_top, rest, cross, spatial, temporal, sw_v, low,
+    rows3, both, tw_v, hidden_v, act, cat, wide, pad, grad_v, sems,
 ):
     rows, chans = video.shape
     top_rows = upper * width
@@ -175,28 +183,32 @@
     tap0 = tw_v[0]
     tap1 = jnp.where(even, tw_v[1], jnp.zeros_like(tap0))
     taps = jnp.concatenate([tap0, tap1], axis=1)
+    taps_cross = jnp.concatenate([tw_v[2], jnp.where(even, jnp.zeros_like(tap0), tw_v[1])], axis=1)
     step = pad.shape[0] * width
 
     def bottom(i):
         here = pl.ds(pl.multiple_of(top_rows + i * step, width), step)
         act_rows, slope = silu_parts(hidden_v[here])
         act[here] = act_rows
-        mid = (dot_rt(both[here], taps) * slope).astype(BF16)
+        pair = both[here]
+        mid = (dot_rt(pair, taps) * slope).astype(BF16)
+        cross[tile(i, step)] = dot_rt(pair, taps_cross)
         grad_v[tile(i, step)] = mid
         put_shifts(cat, tile(i, step), mid, pad)
 
     loop((rows - top_rows) // step, bottom)
     out = copies.start((grad_v, low.at[rows + top_rows : 2 * rows]))
-    top_step = top_rows // 2
+    top_step = chunk(upper) * width
 
     def top(i):
         here = tile(i, top_step)
-        v = hidden_v[here]
-        hidden_top[here] = v
-        act[here] = silu_parts(v)[0]
+        act_rows, slope = silu_parts(hidden_v[here])
+        act[here] = act_rows
+        act_top[here] = act_rows
+        slope_top[here] = slope
         rest[here] = dot_rt(both[here], taps)
 
-    loop(2, top)
+    loop(top_rows // top_step, top)
     for tap, part in tap_parts(rows3, cat, upper, height, -1, height, width):
         spatial[tap] = part
     part = dot_lt(act[...], both[...])
@@ -207,37 +219,36 @@
 
 
 def remote_kernel(
-    height, width, upper, core, above, cot, mate, sw, tw, spatial, temporal, spatial_out, temporal_out, grad,
-    rows3, both, sw_v, tw_v, other, act, cat, wide, pad, grad_v, sems,
+    height, width, upper, core, above, cot, mate, part, sw, spatial, temporal, spatial_out, temporal_out, grad,
+    both, other, act, cat, wide, pad, grad_v, sems,
 ):
     chans = cot.shape[1]
     at = upper * width
-    held = above.shape[0]
-    copies = Copies(sems)
-    head = copies.start((above, rows3.at[:held]), (sw, sw_v))
-    tail = copies.start((mate.at[at:], both.at[:, :chans]), (cot.at[at:], both.at[:, chans:]), (tw, tw_v))
+    count = part.shape[0]
+    copies = Copies(sems)
+    tail = copies.start((mate.at[at:], both.at[:, :chans]), (cot.at[at:], both.at[:, chans:]))
     even = core[0] == 0
     clear_edges(pad)
-    rows3[held:] = jnp.zeros((width, chans), BF16)
-    wait_all(head)
-    conv_rows(rows3, forward_tap(sw_v), other, wide.shape[1] * width, wide)
-    wait_all(tail)
-    tap2 = tw_v[2]
-    taps = jnp.concatenate([jnp.where(even, jnp.zeros_like(tap2), tw_v[1]), tap2], axis=1)
+    for side in range(2):
+        clear_edges(wide.at[side])
+    last = jnp.concatenate([above[2 * width :], jnp.zeros((width, chans), BF16)], axis=0)
+    rows = jnp.concatenate([above[:count], above[width : width + count], last], axis=1)
+    conv_tile(rows, forward_tap(sw), other, slice(0, count), wide)
     step = pad.shape[0] * width
 
     def remote(i):
         here = tile(i, step)
         act_rows, slope = silu_parts(other[here])
         act[here] = act_rows
-        mid = (dot_rt(both[here], taps) * slope).astype(BF16)
+        mid = (part[here] * slope).astype(BF16)
         grad_v[here] = mid
         put_shifts(cat, here, mid, pad)
 
-    loop((height - upper) * width // step, remote)
+    loop(count // step, remote)
     out = copies.start((grad_v, grad))
-    for tap, part in tap_parts(rows3, cat, upper, height, upper - 1, height, width):
+    for tap, part in tap_parts(above, cat, upper, height, upper - 1, height, width):
         spatial_out[tap] = spatial[tap] + part
+    wait_all(tail)
     part = dot_lt(act[...], both[...])
     temporal_out[0] = temporal[0]
     temporal_out[1] = temporal[1] + jnp.where(even, 0.0, part[:, :chans])
@@ -246,53 +257,51 @@
 
 
 def own_kernel(
-    height, width, upper, plain, core, video, hidden, rest, near, far, tw, spatial, temporal, low_in, low, full, send,
-    rows, both, tw_v, act, cat, pad, grad_v, total, total_t, send_v, sems,
+    height, width, upper, plain, core, video, act, slope, rest, near, far, tw, spatial, temporal, low_in, low, full, send,
+    rows, cat, pad, grad_v, total, total_t, send_v, sems,
 ):
     count, chans = near.shape
     whole = height * width
     copies = Copies(sems)
-    head = copies.start((near, both.at[:, :chans]), (far, both.at[:, chans:]), (tw, tw_v))
     tail = copies.start((video.at[: count + width], rows))
     clear_edges(pad)
-    wait_all(head)
-    taps = jnp.concatenate([tw_v[1], tw_v[2]], axis=1)
+    even = core[0] == 0
+    taps = jnp.concatenate([jnp.where(even, jnp.zeros_like(tw[1]), tw[1]), tw[2]], axis=1)
     step = pad.shape[0] * width
 
     def own(i):
         here = tile(i, step)
-        act_rows, slope = silu_parts(hidden[here])
-        act[here] = act_rows
-        grad = rest[here] + dot_rt(both[here], taps)
-        mid = (grad * slope).astype(BF16)
+        grad = rest[here] + dot_rt(jnp.concatenate([near[here], far[here]], axis=1), taps)
+        mid = (grad * slope[here]).astype(BF16)
         grad_v[here] = mid
         put_shifts(cat, here, mid, pad)
 
     loop(count // step, own)
     out = copies.start((grad_v, low.at[whole : whole + count]))
-    part = dot_lt(act[...], both[...])
+    part = dot_lt(act[...], jnp.concatenate([near[...], far[...]], axis=1))
     total_t[:chans] = temporal[0]
-    total_t[chans : 2 * chans] = temporal[1] + part[:, :chans]
+    total_t[chans : 2 * chans] = temporal[1] + jnp.where(even, 0.0, part[:, :chans])
     total_t[2 * chans :] = temporal[2] + part[:, chans:]
     n, first = total.shape[0], 0
-    out += copies.start((total_t, full.at[n : n + total_t.shape[0]]))
     wait_all(tail)
     levels, each = send.shape[:2]
     rt = total_t.shape[0] // (2 * levels)
     rs = each - rt
     for tap, part in tap_parts(rows, cat, 0, upper, 0, height, width):
         total[tap * chans : (tap + 1) * chans] = spatial[tap] + part
-        if tap % 3 == 2:
-            at = (tap - 2) * chans
-            out += copies.start((total.at[at : at + 3 * chans], full.at[at : at + 3 * chans]))
-        if plain:
-            continue
-        while first < levels and (first + 1) * 2 * rs <= (tap + 1) * chans:
-            at = 2 * first + 1 - core[0]
-            send_v[first, :rs] = total[pl.ds(pl.multiple_of(at * rs, 8), rs)].astype(BF16)
-            send_v[first, rs:] = total_t[pl.ds(pl.multiple_of(at * rt, 8), rt)].astype(BF16)
-            out += copies.start((send_v.at[first], send.at[first]))
+        while not plain and first < levels and (first + 1) * 2 * rs <= (tap + 1) * chans:
+            theirs, ours = 2 * first + 1 - core[0], 2 * first + core[0]
+            send_v[first, :rs] = total[pl.ds(pl.multiple_of(theirs * rs, 8), rs)].astype(BF16)
+            send_v[first, rs:] = total_t[pl.ds(pl.multiple_of(theirs * rt, 8), rt)].astype(BF16)
+            at = first * each
+            out += copies.start(
+                (send_v.at[first], send.at[first]),
+                (total.at[pl.ds(pl.multiple_of(ours * rs, 8), rs)], full.at[at : at + rs]),
+                (total_t.at[pl.ds(pl.multiple_of(ours * rt, 8), rt)], full.at[at + rs : at + each]),
+            )
             first += 1
+    if plain:
+        out += copies.start((total, full.at[:n]), (total_t, full.at[n : n + total_t.shape[0]]))
     wait_all(out)
 
 
@@ -331,36 +340,24 @@
 
 
 def split_kernel(size, where, kept, swapped, own, *refs):
-    sends, (keep_v, swapped_v, send_v, sems) = refs[: size - 1], refs[size - 1 :]
-    core, q = where[0], where[1]
+    sends, (keep_v, sems) = refs[: size - 1], refs[size - 1 :]
+    q = where[0]
     levels, each, chans = swapped.shape
     rs = own.shape[1] * 3 // 4
     rt = own.shape[1] - rs
     copies = Copies(sems)
-    pairs = [(swapped, swapped_v)]
+    ins = copies.start(*((kept.at[level * each : (level + 1) * each], keep_v.at[level]) for level in range(levels)))
     for level in range(levels):
-        at = 2 * level + core
-        low = pl.ds(pl.multiple_of(at * size * rs, 8), size * rs)
-        high = pl.ds(pl.multiple_of(2 * levels * size * rs + at * size * rt, 8), size * rt)
-        pairs += [(kept.at[low], keep_v.at[level, : size * rs]), (kept.at[high], keep_v.at[level, size * rs :])]
-    ins = copies.start(*pairs)
-    ins[0].wait()
-    for level in range(levels):
-        wait_all(ins[1 + 2 * level : 3 + 2 * level])
-        keep_v[level] += swapped_v[level].astype(F32)
-
-    def total(i, level):
-        low = keep_v[level, pl.ds(pl.multiple_of(i * rs, 8), rs)]
-        return jnp.concatenate([low, keep_v[level, pl.ds(pl.multiple_of(size * rs + i * rt, 8), rt)]], axis=0)
-
-    out = []
-    for k, send in enumerate(sends):
-        for level in range(levels):
-            send_v[k, level] = total(peer(q, k + 1, size), level).astype(BF16)
-        out += copies.start((send_v.at[k], send))
-    for level in range(levels):
-        own[level] = total(q, level)
-    wait_all(out)
+        ins[level].wait()
+        keep_v[level] += swapped[level].astype(F32)
+
+        def total(i):
+            low = keep_v[level, pl.ds(pl.multiple_of(i * rs, 8), rs)]
+            return jnp.concatenate([low, keep_v[level, pl.ds(pl.multiple_of(size * rs + i * rt, 8), rt)]], axis=0)
+
+        for k, send in enumerate(sends):
+            send[level] = total(peer(q, k + 1, size)).astype(BF16)
+        own[level] = total(q)
 
 
 def level_kernel(size, where, own, *refs):
@@ -408,7 +405,6 @@
     upper = height - REMOTE
     down = [(i + 2, i) for i in range(seq - 2)]
     up = [(i, i + 2) for i in range(seq - 2)]
-    across = [(i, i + 1) for i in range(0, seq, 2)]
     swap = [(i, i ^ 1) for i in range(seq)]
 
     mac = rows * chans * chans
@@ -428,37 +424,40 @@
     def pad(n):
         return like(F32, n, long, chans)
 
-    hidden, rest, spatial, temporal, low, token = call(
-        functools.partial(local_kernel, height, width, upper), "local", "shhhhh vvvvh", 34 * mac, [core, x, cot, mate, sw, tw],
-        [rows_of(upper), rows_of(upper, dtype=F32), taps9, taps3, like(BF16, 2 * SPARE, chans)],
+    act, slope, rest, part, spatial, temporal, sw_v, low, token = call(
+        functools.partial(local_kernel, height, width, upper), "local", "shhhhh vvvvvvvh", 34 * mac, [core, x, cot, mate, sw, tw],
         [
-            rows_of(height + 2), rows_of(height, 2 * chans), sw, tw, rows_of(height), rows_of(height),
-            rows_of(REMOTE, 3 * chans), wide(height // 2), pad(REMOTE), rows_of(REMOTE),
+            rows_of(upper), rows_of(upper, dtype=F32), rows_of(upper, dtype=F32), rows_of(REMOTE, dtype=F32), taps9, taps3, sw,
+            like(BF16, 2 * SPARE, chans),
+        ],
+        [
+            rows_of(height + 2), rows_of(height, 2 * chans), tw, rows_of(height), rows_of(height),
+            rows_of(REMOTE, 3 * chans), wide(height // 2), pad(chunk(REMOTE)), rows_of(REMOTE),
         ],
         copies=6,
     )
     far, token = behind(far, token)
-    near = lax.ppermute(far, "seq", across)
+    near = lax.ppermute(far, "seq", swap)
     spatial, temporal, cross, token = call(
-        functools.partial(remote_kernel, height, width, upper), "remote", "shhhhhvv vvh", 16 * mac,
-        [core, above, cot, mate, sw, tw, spatial, temporal], [taps9, taps3, rows_of(REMOTE)],
+        functools.partial(remote_kernel, height, width, upper), "remote", "svhhvvvv vvh", 16 * mac,
+        [core, above, cot, mate, part, sw_v, spatial, temporal], [taps9, taps3, rows_of(REMOTE)],
         [
-            rows_of(REMOTE + 2), rows_of(REMOTE, 2 * chans), sw, tw, rows_of(REMOTE), rows_of(REMOTE),
-            rows_of(REMOTE, 3 * chans), wide(REMOTE), pad(REMOTE), rows_of(REMOTE),
+            rows_of(REMOTE, 2 * chans), rows_of(REMOTE), rows_of(REMOTE),
+            rows_of(REMOTE, 3 * chans), wide(REMOTE), pad(chunk(REMOTE)), rows_of(REMOTE),
         ],
-        copies=6, after=[token],
+        copies=3, after=[token],
     )
     rs, rt = 9 * chans // (seq * dp), 3 * chans // (seq * dp)
     plain = bool(rs % 8 or rt % 8 or dp * rs % 16 or dp * rt % 16)
     send = like(BF16, levels, dp * (rs + rt), chans)
     low, full, send, token = call(
-        functools.partial(own_kernel, height, width, upper, plain), "own", "shvvhhhvvh hhh", 16 * mac,
-        [core, x, hidden, rest, near, far, tw, spatial, temporal, low], [low, like(F32, SPARE, chans), send],
+        functools.partial(own_kernel, height, width, upper, plain), "own", "shvvvvvvvvh hhh", 16 * mac,
+        [core, x, act, slope, rest, near, far, tw, spatial, temporal, low], [low, like(F32, SPARE, chans), send],
         [
-            rows_of(upper + 1), rows_of(upper, 2 * chans), tw, rows_of(upper), rows_of(upper, 3 * chans), pad(upper // 2),
+            rows_of(upper + 1), rows_of(upper, 3 * chans), pad(chunk(upper)),
             rows_of(upper), like(F32, 9 * chans, chans), like(F32, 3 * chans, chans), send,
         ],
-        copies=9 + levels, after=[token], alias={9: 0},
+        copies=4 + 3 * levels, after=[token], alias={10: 0},
     )
     piece = (levels, rs + rt, chans)
     if plain:
@@ -472,11 +471,10 @@
     else:
         got = lax.ppermute(send, "seq", swap)
         own, *sends, token = call(
-            functools.partial(split_kernel, dp), "split", "shh v" + "h" * (dp - 1), mac // 8,
-            [jnp.concatenate([core, q]), full, got],
+            functools.partial(split_kernel, dp), "split", "shv v" + "v" * (dp - 1), mac // 8,
+            [q, full, got],
             [like(F32, *piece)] + [like(BF16, *piece)] * (dp - 1),
-            [like(F32, *send.shape), like(BF16, *send.shape), like(BF16, dp - 1, *piece)],
-            copies=2 * levels + dp,
+            [like(F32, *send.shape)], copies=levels,
         )
     got = [lax.ppermute(s, "dp", [(i, peer(i, k, dp)) for i in range(dp)]) for k, s in enumerate(sends, 1)]
     cross = lax.ppermute(cross, "seq", down)

time: 78.8 us -> 74.6 us (0.947)
  waiting for transfers between devices: 16 us -> 14.1 us
  Pallas kernels: 33.5 us -> 32.2 us
  starting transfers between devices: 22.5 us -> 21.6 us
    ppermute x1, waiting for transfers between devices: 4.76 us -> 2.17 us  [shards(): far = lax.ppermute(cot[:upper * width], 'seq', down)]
    ppermute x1, starting transfers between devices: 1.98 us -> 0.01 us  [shards(): near = lax.ppermute(far, 'seq', swap)]
    pallas_call x9, Pallas kernels: 33.5 us -> 32.2 us  [call(): pl.pallas_call(body, out_shape=[*outs, TOKEN], in_specs=[SPACE[c] for c i...]
    ppermute x3, starting transfers between devices: 4.45 us -> 5.31 us  [shards(): lax.ppermute(s, 'seq', [(i, 2 * peer(i // 2, k, levels) + i % 2) for i in...]
    unnamed x12 -> x10, local copies, waits for them, and re-layouts: 2.33 us -> 2.32 us
  transfers between devices with their start and end apart: 15 -> 15, of which waited for: 8 -> 9; matrix products, arithmetic and copies ran while one was open for 4% -> 4% of each run, Pallas kernels for 32% -> 34%
where the time goes in v4:
time: 74.6 us; the launch traced here: 74.2 us
  Pallas kernels  32.2 us (43%)
  starting transfers between devices  21.6 us (29%)
  waiting for transfers between devices  14.1 us (19%)
  local copies, waits for them, and re-layouts  5.46 us (7%)
  between operations  0.78 us (1%)
    pallas_call x9, Pallas kernels, call(): pl.pallas_call(body, out_shape=[*outs, TOKEN], in_specs=[SPACE[c] for c i...  32.2 us
    ppermute x1, starting transfers between devices, shards(): above = lax.ppermute(x[(upper - 1) * width:], 'seq', up)  5.9 us
    ppermute x3, starting transfers between devices, shards(): lax.ppermute(s, 'seq', [(i, 2 * peer(i // 2, k, levels) + i % 2) for i in...  5.31 us
    ppermute x3, waiting for transfers between devices, shards(): lax.ppermute(s, 'dp', [(i, peer(i, k, dp)) for i in range(dp)])  5.3 us
    ppermute x3, starting transfers between devices, shards(): lax.ppermute(s, 'dp', [(i, peer(i, k, dp)) for i in range(dp)])  3.55 us
    ppermute x3, starting transfers between devices, shards(): lax.ppermute(small, 'dp', [(peer(i, k, dp), i) for i in range(dp)])  3.49 us
    ppermute x3, waiting for transfers between devices, shards(): lax.ppermute(small, 'dp', [(peer(i, k, dp), i) for i in range(dp)])  3.29 us
    unnamed x10, local copies, waits for them, and re-layouts  2.32 us
  transfers between devices with their start and end apart: 15, of which 9 were waited for; matrix products, arithmetic and copies ran while one was open for 4% of the time, Pallas kernels for 34%

profile of v4, /device:TPU:0, one launch (start us, length us, event | category | flops | bytes accessed | tf_op | source)
XLA Modules:
  0.0 74.2 jit_solution(16788076005941068031)
XLA Ops:
  1.2 2.2 %slice.12 = bf16[1,1,9,160,256]{4,3,2,1,0:T(8,128)(2,1)} slice(bf16[1,1,16,160,256]{4,3,2,1,0:T(8,128)(2,1)} %param.5), slice={[0:1], [0:1], [0:9], [0:160], [0:256]} | slice | bytes 1474560 | tf_op jit(solution)/shard_map/slice | solution.py:421
  3.4 1.3 %collective-permute-start.1 = (bf16[1440,256]{1,0:T(8,128)(2,1)}, bf16[1440,256]{1,0:T(8,128)(2,1)S(1)}, u32[]{:S(2)}, u32[]{:S(2)}) collective-permute-start(bf16[1440,256]{1,0:T(8,128)(2,1)} %bitcast.3), channel_id=1, source_target_pairs={{2,0},{3,1},{4,2},{5,3},{6,4},{7,5},{10,8},{11,9},{12,10},{13,11},... | collective-permute-start | bytes 2211848 | tf_op jit(solution)/shard_map/ppermute | solution.py:421
  5.6 5.9 %collective-permute-start.3 = (bf16[1280,256]{1,0:T(8,128)(2,1)}, bf16[1280,256]{1,0:T(8,128)(2,1)}, u32[]{:S(2)}, u32[]{:S(2)}) collective-permute-start(bf16[1280,256]{1,0:T(8,128)(2,1)} %bitcast.4), channel_id=1, source_target_pairs={{0,2},{1,3},{2,4},{3,5},{4,6},{5,7},{8,10},{9,11},{10,12},{11,13},... | collective-permute-start | bytes 1966088 | tf_op jit(solution)/shard_map/ppermute | solution.py:422
  11.5 1.3 %copy-done.2 = bf16[1,1,16,160,256]{4,3,2,1,0:T(8,128)(2,1)S(1)} copy-done((bf16[1,1,16,160,256]{4,3,2,1,0:T(8,128)(2,1)S(1)}, bf16[1,1,16,160,256]{4,3,2,1,0:T(8,128)(2,1)}, u32[]{:S(2)}) %copy-start.2) | copy-done | bytes 1310744
  12.8 1.0 %copy-done.3 = bf16[3,256,256]{2,1,0:T(8,128)(2,1)S(1)} copy-done((bf16[3,256,256]{2,1,0:T(8,128)(2,1)S(1)}, bf16[3,256,256]{2,1,0:T(8,128)(2,1)}, u32[]{:S(2)}) %copy-start.3) | copy-done | bytes 393240
  13.8 9.0 %local.1 = (bf16[1440,256]{1,0:T(8,128)(2,1)S(1)}, f32[1440,256]{1,0:T(8,128)S(1)}, f32[1440,256]{1,0:T(8,128)S(1)}, f32[1120,256]{1,0:T(8,128)S(1)}, f32[9,256,...) custom-call(s32[1]{0:T(128)} %bitcast.refs_0_, ...), custom_call_target="tpu_custom_call" | custom-call | flops 5704253440 | bytes 14663684 | tf_op jit(solution)/shard_map/local/pallas_call | solution.py:50
  22.9 2.2 %collective-permute-done.1.refs_6_ = bf16[1440,256]{1,0:T(8,128)(2,1)S(1)} collective-permute-done((bf16[1440,256]{1,0:T(8,128)(2,1)}, bf16[1440,256]{1,0:T(8,128)(2,1)S(1)}, u32[]{:S(2)}, u32[]{:S(2)}) %collective-permute-start.1) | collective-permute-done | bytes 737312 | tf_op jit(solution)/shard_map/ppermute | solution.py:421
  25.5 6.0 %remote.1 = (f32[9,256,256]{2,1,0:T(8,128)S(1)}, f32[3,256,256]{2,1,0:T(8,128)S(1)}, bf16[1120,256]{1,0:T(8,128)(2,1)}, f32[8,128]{1,0:T(8,128)S(1)}) custom-call(s32[1]{0:T(128)} %bitcast.refs_0_, bf16[1280,256]{1,0:T(8,128)(2,1)} %collective-permute-done.3.refs_1_, bf16[2560,256]{1,0:T(8,128)(2,1)S(1)} %bitcast.14, ...), custom_call_target="tpu_custom_call" | custom-call | flops 2684354560 | bytes 12468228 | tf_op jit(solution)/shard_map/remote/pallas_call | solution.py:50
  31.5 5.9 %own.1 = (bf16[90112,256]{1,0:T(8,128)(2,1)}, f32[45056,256]{1,0:T(8,128)}, bf16[4,384,256]{2,1,0:T(8,128)(2,1)}, f32[8,128]{1,0:T(8,128)}) custom-call(s32[1]{0:T(128)} %bitcast.refs_0_, bf16[2560,256]{1,0:T(8,128)(2,1)S(1)} %bitcast.11, bf16[1440,256]{1,0:T(8,128)(2,1)S(1)} %get-tuple-element.38.refs_2_, ...), custom_call_target="tpu_custom_call", output_to_operand_aliasing={{0}: (10, {})} | custom-call | flops 2684354560 | bytes 10797060 | tf_op jit(solution)/shard_map/own/pallas_call | solution.py:50
  37.5 1.5 %collective-permute-start.4 = (bf16[1120,256]{1,0:T(8,128)(2,1)}, bf16[1120,256]{1,0:T(8,128)(2,1)S(1)}, u32[]{:S(2)}, u32[]{:S(2)}) collective-permute-start(bf16[1120,256]{1,0:T(8,128)(2,1)} %get-tuple-element.53), channel_id=1, source_target_pairs={{2,0},{3,1},{4,2},{5,3},{6,4},{7,5},{10,8},{11,9},{12,10},{13,11},... | collective-permute-start | bytes 1720328 | tf_op jit(solution)/shard_map/ppermute | solution.py:480
  39.0 1.0 %collective-permute-done.5.refs_2_ = bf16[4,384,256]{2,1,0:T(8,128)(2,1)S(1)} collective-permute-done((bf16[4,384,256]{2,1,0:T(8,128)(2,1)}, bf16[4,384,256]{2,1,0:T(8,128)(2,1)S(1)}, u32[]{:S(2)}, u32[]{:S(2)}) %collective-permute-start.5) | collective-permute-done | bytes 786464 | tf_op jit(solution)/shard_map/ppermute | solution.py:472
  40.0 1.4 %split.1 = (f32[4,96,256]{2,1,0:T(8,128)S(1)}, bf16[4,96,256]{2,1,0:T(8,128)(2,1)S(1)}, bf16[4,96,256]{2,1,0:T(8,128)(2,1)S(1)}, bf16[4,96,256]{2,1,0:T(8,128)(2,1)S(1)}, f32[8,128]{1,0:T(8,128)S(1)}) custom-call(s32[1]{0:T(128)} %bitcast.5.refs_0_, f32[45056,256]{1,0:T(8,128)} %get-tuple-element.54.refs_1_, ...), custom_call_target="tpu_custom_call" | custom-call | flops 20971520 | bytes 1769476 | tf_op jit(solution)/shard_map/split/pallas_call | solution.py:50
  41.4 1.7 %collective-permute-start.6 = (bf16[4,96,256]{2,1,0:T(8,128)(2,1)S(1)}, bf16[4,96,256]{2,1,0:T(8,128)(2,1)S(1)}, u32[]{:S(2)}, u32[]{:S(2)}) collective-permute-start(bf16[4,96,256]{2,1,0:T(8,128)(2,1)S(1)} %get-tuple-element.59), channel_id=1, source_target_pairs={{0,8},{8,0},{16,24},{24,16},{1,9},{9,1},{17,25},{25,17},{2,10},{10... | collective-permute-start | bytes 589832 | tf_op jit(solution)/shard_map/ppermute | solution.py:479
  43.1 1.5 %collective-permute-start.7 = (bf16[4,96,256]{2,1,0:T(8,128)(2,1)S(1)}, bf16[4,96,256]{2,1,0:T(8,128)(2,1)S(1)}, u32[]{:S(2)}, u32[]{:S(2)}) collective-permute-start(bf16[4,96,256]{2,1,0:T(8,128)(2,1)S(1)} %get-tuple-element.60), channel_id=1, source_target_pairs={{0,16},{8,24},{16,0},{24,8},{1,17},{9,25},{17,1},{25,9},{2,18},{10... | collective-permute-start | bytes 589832 | tf_op jit(solution)/shard_map/ppermute | solution.py:479
  45.0 3.7 %back_top.1 = (bf16[2560,256]{1,0:T(8,128)(2,1)}, f32[8,128]{1,0:T(8,128)S(1)}) custom-call(bf16[90112,256]{1,0:T(8,128)(2,1)} %get-tuple-element.52.refs_0_, bf16[3,3,256,256]{3,2,1,0:T(8,128)(2,1)S(1)} %copy-done, f32[8,128]{1,0:T(8,128)S(1)} %get-tuple-element.56.refs_2_), custom_call_target="tpu_custom_call" | custom-call | flops 1509949440 | bytes 2490368 | tf_op jit(solution)/shard_map/back_top/pallas_call | solution.py:50
  49.2 4.8 %collective-permute-done.7.refs_3_ = bf16[4,96,256]{2,1,0:T(8,128)(2,1)S(1)} collective-permute-done((bf16[4,96,256]{2,1,0:T(8,128)(2,1)S(1)}, bf16[4,96,256]{2,1,0:T(8,128)(2,1)S(1)}, u32[]{:S(2)}, u32[]{:S(2)}) %collective-permute-start.7) | collective-permute-done | bytes 196640 | tf_op jit(solution)/shard_map/ppermute | solution.py:479
  54.9 2.5 %collective-permute-start.9 = (bf16[96,256]{1,0:T(8,128)(2,1)S(1)}, bf16[96,256]{1,0:T(8,128)(2,1)S(1)}, u32[]{:S(2)}, u32[]{:S(2)}) collective-permute-start(bf16[96,256]{1,0:T(8,128)(2,1)S(1)} %get-tuple-element.66), channel_id=1, source_target_pairs={{0,2},{1,3},{2,0},{3,1},{4,6},{5,7},{6,4},{7,5},{8,10},{9,11},{10,... | collective-permute-start | bytes 147464 | tf_op jit(solution)/shard_map/ppermute | solution.py:492
  57.4 2.8 %collective-permute-start.10 = (bf16[96,256]{1,0:T(8,128)(2,1)S(1)}, bf16[96,256]{1,0:T(8,128)(2,1)S(1)}, u32[]{:S(2)}, u32[]{:S(2)}) collective-permute-start(bf16[96,256]{1,0:T(8,128)(2,1)S(1)} %get-tuple-element.67), channel_id=1, source_target_pairs={{0,4},{1,5},{2,6},{3,7},{4,0},{5,1},{6,2},{7,3},{8,12},{9,13},{10,... | collective-permute-start | bytes 147464 | tf_op jit(solution)/shard_map/ppermute | solution.py:492
  60.2 3.9 %back_bottom.1 = (bf16[2560,256]{1,0:T(8,128)(2,1)}, f32[8,128]{1,0:T(8,128)S(1)}) custom-call(bf16[90112,256]{1,0:T(8,128)(2,1)} %get-tuple-element.52.refs_0_, bf16[1120,256]{1,0:T(8,128)(2,1)S(1)} %collective-permute-done.4.refs_1_, bf16[3,3,256,256]{3,2,1,0:T(8,128)(2,1)S(1)} %copy-done, ...), custom_call_target="tpu_custom_call", output_to_operand_aliasing={{0}: (3, {})} | custom-call | flops 1509949440 | bytes 4374528 | tf_op jit(solution)/shard_map/back_bottom/pallas_call | solution.py:50
  64.1 2.0 %collective-permute-done.11.refs_3_ = bf16[96,256]{1,0:T(8,128)(2,1)S(1)} collective-permute-done((bf16[96,256]{1,0:T(8,128)(2,1)S(1)}, bf16[96,256]{1,0:T(8,128)(2,1)S(1)}, u32[]{:S(2)}, u32[]{:S(2)}) %collective-permute-start.11) | collective-permute-done | bytes 49184 | tf_op jit(solution)/shard_map/ppermute | solution.py:492
  66.7 1.5 %collective-permute-start.14 = (bf16[96,256]{1,0:T(8,128)(2,1)S(1)}, bf16[96,256]{1,0:T(8,128)(2,1)S(1)}, u32[]{:S(2)}, u32[]{:S(2)}) collective-permute-start(bf16[96,256]{1,0:T(8,128)(2,1)S(1)} %get-tuple-element.70.refs_1_), channel_id=1, source_target_pairs={{24,0},{16,8},{8,16},{0,24},{25,1},{17,9},{9,17},{1,25},{26,2},{18... | collective-permute-start | bytes 147464 | tf_op jit(solution)/shard_map/ppermute | solution.py:504
  68.2 1.2 %collective-permute-start.13 = (bf16[96,256]{1,0:T(8,128)(2,1)S(1)}, bf16[96,256]{1,0:T(8,128)(2,1)S(1)}, u32[]{:S(2)}, u32[]{:S(2)}) collective-permute-start(bf16[96,256]{1,0:T(8,128)(2,1)S(1)} %get-tuple-element.70.refs_1_), channel_id=1, source_target_pairs={{16,0},{24,8},{0,16},{8,24},{17,1},{25,9},{1,17},{9,25},{18,2},{26... | collective-permute-start | bytes 147464 | tf_op jit(solution)/shard_map/ppermute | solution.py:504
  70.2 1.5 %collective-permute-done.14.refs_4_ = bf16[96,256]{1,0:T(8,128)(2,1)S(1)} collective-permute-done((bf16[96,256]{1,0:T(8,128)(2,1)S(1)}, bf16[96,256]{1,0:T(8,128)(2,1)S(1)}, u32[]{:S(2)}, u32[]{:S(2)}) %collective-permute-start.14) | collective-permute-done | bytes 49184 | tf_op jit(solution)/shard_map/ppermute | solution.py:504
  72.3 1.2 %collective-permute-done.12.refs_2_ = bf16[96,256]{1,0:T(8,128)(2,1)S(1)} collective-permute-done((bf16[96,256]{1,0:T(8,128)(2,1)S(1)}, bf16[96,256]{1,0:T(8,128)(2,1)S(1)}, u32[]{:S(2)}, u32[]{:S(2)}) %collective-permute-start.12) | collective-permute-done | bytes 49184 | tf_op jit(solution)/shard_map/ppermute | solution.py:504
  (27 shorter events, 6.5 us)
Async XLA Ops:
  0.6 4.1 %copy-start.1 = (bf16[1,1,16,160,256]{4,3,2,1,0:T(8,128)(2,1)S(1)}, bf16[1,1,16,160,256]{4,3,2,1,0:T(8,128)(2,1)}, u32[]{:S(2)}) copy-start(bf16[1,1,16,160,256]{4,3,2,1,0:T(8,128)(2,1)} %param.4) | copy-start | bytes 3932164
  0.6 10.9 %copy-start = (bf16[3,3,256,256]{3,2,1,0:T(8,128)(2,1)S(1)}, bf16[3,3,256,256]{3,2,1,0:T(8,128)(2,1)}, u32[]{:S(2)}) copy-start(bf16[3,3,256,256]{3,2,1,0:T(8,128)(2,1)} %refs_2_.1) | copy-start | bytes 3538948
  0.6 10.9 %collective-permute-start = (bf16[2560,256]{1,0:T(8,128)(2,1)}, bf16[2560,256]{1,0:T(8,128)(2,1)}, u32[]{:S(2)}, u32[]{:S(2)}) collective-permute-start(bf16[2560,256]{1,0:T(8,128)(2,1)} %bitcast.12), channel_id=1, source_target_pairs={{0,1},{1,0},{2,3},{3,2},{4,5},{5,4},{6,7},{7,6},{8,9},{9,8},{10,11... | collective-permute-start | bytes 3932168 | tf_op jit(solution)/shard_map/ppermute | solution.py:420
  3.4 21.6 %collective-permute-start.1 = (bf16[1440,256]{1,0:T(8,128)(2,1)}, bf16[1440,256]{1,0:T(8,128)(2,1)S(1)}, u32[]{:S(2)}, u32[]{:S(2)}) collective-permute-start(bf16[1440,256]{1,0:T(8,128)(2,1)} %bitcast.3), channel_id=1, source_target_pairs={{2,0},{3,1},{4,2},{5,3},{6,4},{7,5},{10,8},{11,9},{12,10},{13,11},... | collective-permute-start | bytes 2211848 | tf_op jit(solution)/shard_map/ppermute | solution.py:421
  5.6 19.9 %collective-permute-start.3 = (bf16[1280,256]{1,0:T(8,128)(2,1)}, bf16[1280,256]{1,0:T(8,128)(2,1)}, u32[]{:S(2)}, u32[]{:S(2)}) collective-permute-start(bf16[1280,256]{1,0:T(8,128)(2,1)} %bitcast.4), channel_id=1, source_target_pairs={{0,2},{1,3},{2,4},{3,5},{4,6},{5,7},{8,10},{9,11},{10,12},{11,13},... | collective-permute-start | bytes 1966088 | tf_op jit(solution)/shard_map/ppermute | solution.py:422
  11.5 1.3 %copy-start.2 = (bf16[1,1,16,160,256]{4,3,2,1,0:T(8,128)(2,1)S(1)}, bf16[1,1,16,160,256]{4,3,2,1,0:T(8,128)(2,1)}, u32[]{:S(2)}) copy-start(bf16[1,1,16,160,256]{4,3,2,1,0:T(8,128)(2,1)} %param.5) | copy-start | bytes 3932164
  12.8 1.0 %copy-start.3 = (bf16[3,256,256]{2,1,0:T(8,128)(2,1)S(1)}, bf16[3,256,256]{2,1,0:T(8,128)(2,1)}, u32[]{:S(2)}) copy-start(bf16[3,256,256]{2,1,0:T(8,128)(2,1)} %refs_7_.1) | copy-start | bytes 1179652
  25.0 6.4 %collective-permute-start.2 = (bf16[1440,256]{1,0:T(8,128)(2,1)S(1)}, bf16[1440,256]{1,0:T(8,128)(2,1)S(1)}, u32[]{:S(2)}, u32[]{:S(2)}) collective-permute-start(bf16[1440,256]{1,0:T(8,128)(2,1)S(1)} %collective-permute-done.1.refs_6_), channel_id=1, source_target_pairs={{0,1},{1,0},{2,3},{3,2},{4,5},{5,4},{6,7},{7,6},{8,9},{9,8},{10,11... | collective-permute-start | bytes 2211848 | tf_op jit(solution)/shard_map/ppermute | solution.py:440
  25.5 6.0 %copy-start.4 = (bf16[3,256,256]{2,1,0:T(8,128)(2,1)S(1)}, bf16[3,256,256]{2,1,0:T(8,128)(2,1)}, u32[]{:S(2)}) copy-start(bf16[3,256,256]{2,1,0:T(8,128)(2,1)} %refs_7_.1) | copy-start | bytes 1179652
  37.4 2.6 %collective-permute-start.5 = (bf16[4,384,256]{2,1,0:T(8,128)(2,1)}, bf16[4,384,256]{2,1,0:T(8,128)(2,1)S(1)}, u32[]{:S(2)}, u32[]{:S(2)}) collective-permute-start(bf16[4,384,256]{2,1,0:T(8,128)(2,1)} %get-tuple-element.55), channel_id=1, source_target_pairs={{0,1},{1,0},{2,3},{3,2},{4,5},{5,4},{6,7},{7,6},{8,9},{9,8},{10,11... | collective-permute-start | bytes 2359304 | tf_op jit(solution)/shard_map/ppermute | solution.py:472
  37.5 22.7 %collective-permute-start.4 = (bf16[1120,256]{1,0:T(8,128)(2,1)}, bf16[1120,256]{1,0:T(8,128)(2,1)S(1)}, u32[]{:S(2)}, u32[]{:S(2)}) collective-permute-start(bf16[1120,256]{1,0:T(8,128)(2,1)} %get-tuple-element.53), channel_id=1, source_target_pairs={{2,0},{3,1},{4,2},{5,3},{6,4},{7,5},{10,8},{11,9},{12,10},{13,11},... | collective-permute-start | bytes 1720328 | tf_op jit(solution)/shard_map/ppermute | solution.py:480
  41.4 7.8 %collective-permute-start.6 = (bf16[4,96,256]{2,1,0:T(8,128)(2,1)S(1)}, bf16[4,96,256]{2,1,0:T(8,128)(2,1)S(1)}, u32[]{:S(2)}, u32[]{:S(2)}) collective-permute-start(bf16[4,96,256]{2,1,0:T(8,128)(2,1)S(1)} %get-tuple-element.59), channel_id=1, source_target_pairs={{0,8},{8,0},{16,24},{24,16},{1,9},{9,1},{17,25},{25,17},{2,10},{10... | collective-permute-start | bytes 589832 | tf_op jit(solution)/shard_map/ppermute | solution.py:479
  43.1 10.9 %collective-permute-start.7 = (bf16[4,96,256]{2,1,0:T(8,128)(2,1)S(1)}, bf16[4,96,256]{2,1,0:T(8,128)(2,1)S(1)}, u32[]{:S(2)}, u32[]{:S(2)}) collective-permute-start(bf16[4,96,256]{2,1,0:T(8,128)(2,1)S(1)} %get-tuple-element.60), channel_id=1, source_target_pairs={{0,16},{8,24},{16,0},{24,8},{1,17},{9,25},{17,1},{25,9},{2,18},{10... | collective-permute-start | bytes 589832 | tf_op jit(solution)/shard_map/ppermute | solution.py:479
  44.6 9.4 %collective-permute-start.8 = (bf16[4,96,256]{2,1,0:T(8,128)(2,1)S(1)}, bf16[4,96,256]{2,1,0:T(8,128)(2,1)S(1)}, u32[]{:S(2)}, u32[]{:S(2)}) collective-permute-start(bf16[4,96,256]{2,1,0:T(8,128)(2,1)S(1)} %get-tuple-element.61), channel_id=1, source_target_pairs={{0,24},{8,16},{16,8},{24,0},{1,25},{9,17},{17,9},{25,1},{2,26},{10... | collective-permute-start | bytes 589832 | tf_op jit(solution)/shard_map/ppermute | solution.py:479
  54.9 9.2 %collective-permute-start.9 = (bf16[96,256]{1,0:T(8,128)(2,1)S(1)}, bf16[96,256]{1,0:T(8,128)(2,1)S(1)}, u32[]{:S(2)}, u32[]{:S(2)}) collective-permute-start(bf16[96,256]{1,0:T(8,128)(2,1)S(1)} %get-tuple-element.66), channel_id=1, source_target_pairs={{0,2},{1,3},{2,0},{3,1},{4,6},{5,7},{6,4},{7,5},{8,10},{9,11},{10,... | collective-permute-start | bytes 147464 | tf_op jit(solution)/shard_map/ppermute | solution.py:492
  57.4 6.7 %collective-permute-start.10 = (bf16[96,256]{1,0:T(8,128)(2,1)S(1)}, bf16[96,256]{1,0:T(8,128)(2,1)S(1)}, u32[]{:S(2)}, u32[]{:S(2)}) collective-permute-start(bf16[96,256]{1,0:T(8,128)(2,1)S(1)} %get-tuple-element.67), channel_id=1, source_target_pairs={{0,4},{1,5},{2,6},{3,7},{4,0},{5,1},{6,2},{7,3},{8,12},{9,13},{10,... | collective-permute-start | bytes 147464 | tf_op jit(solution)/shard_map/ppermute | solution.py:492
  60.2 5.9 %collective-permute-start.11 = (bf16[96,256]{1,0:T(8,128)(2,1)S(1)}, bf16[96,256]{1,0:T(8,128)(2,1)S(1)}, u32[]{:S(2)}, u32[]{:S(2)}) collective-permute-start(bf16[96,256]{1,0:T(8,128)(2,1)S(1)} %get-tuple-element.68), channel_id=1, source_target_pairs={{0,6},{1,7},{2,4},{3,5},{4,2},{5,3},{6,0},{7,1},{8,14},{9,15},{10,... | collective-permute-start | bytes 147464 | tf_op jit(solution)/shard_map/ppermute | solution.py:492
  66.7 5.0 %collective-permute-start.14 = (bf16[96,256]{1,0:T(8,128)(2,1)S(1)}, bf16[96,256]{1,0:T(8,128)(2,1)S(1)}, u32[]{:S(2)}, u32[]{:S(2)}) collective-permute-start(bf16[96,256]{1,0:T(8,128)(2,1)S(1)} %get-tuple-element.70.refs_1_), channel_id=1, source_target_pairs={{24,0},{16,8},{8,16},{0,24},{25,1},{17,9},{9,17},{1,25},{26,2},{18... | collective-permute-start | bytes 147464 | tf_op jit(solution)/shard_map/ppermute | solution.py:504
  68.2 4.1 %collective-permute-start.13 = (bf16[96,256]{1,0:T(8,128)(2,1)S(1)}, bf16[96,256]{1,0:T(8,128)(2,1)S(1)}, u32[]{:S(2)}, u32[]{:S(2)}) collective-permute-start(bf16[96,256]{1,0:T(8,128)(2,1)S(1)} %get-tuple-element.70.refs_1_), channel_id=1, source_target_pairs={{16,0},{24,8},{0,16},{8,24},{17,1},{25,9},{1,17},{9,25},{18,2},{26... | collective-permute-start | bytes 147464 | tf_op jit(solution)/shard_map/ppermute | solution.py:504
  69.4 4.1 %collective-permute-start.12 = (bf16[96,256]{1,0:T(8,128)(2,1)S(1)}, bf16[96,256]{1,0:T(8,128)(2,1)S(1)}, u32[]{:S(2)}, u32[]{:S(2)}) collective-permute-start(bf16[96,256]{1,0:T(8,128)(2,1)S(1)} %get-tuple-element.70.refs_1_), channel_id=1, source_target_pairs={{8,0},{0,8},{24,16},{16,24},{9,1},{1,9},{25,17},{17,25},{10,2},{2,... | collective-permute-start | bytes 147464 | tf_op jit(solution)/shard_map/ppermute | solution.py:504

commit v5 on v4

--- a/solution.py
+++ b/solution.py
@@ -419,7 +419,8 @@
 
     mate = lax.ppermute(cot, "seq", swap)
     far = lax.ppermute(cot[: upper * width], "seq", down)
-    above = lax.ppermute(x[(upper - 1) * width :], "seq", up)
+    above, mate = lax.optimization_barrier((x[(upper - 1) * width :], mate))
+    above = lax.ppermute(above, "seq", up)
 
     def pad(n):
         return like(F32, n, long, chans)

time: 74.6 us -> 73.4 us (0.984)
  Pallas kernels: 32.2 us -> 31.1 us
  starting transfers between devices: 21.6 us -> 20.8 us
  waiting for transfers between devices: 14.1 us -> 14.9 us
    pallas_call x9, Pallas kernels: 32.2 us -> 31.1 us  [call(): pl.pallas_call(body, out_shape=[*outs, TOKEN], in_specs=[SPACE[c] for c i...]
    ppermute x1, starting transfers between devices: 5.9 us -> 5.09 us  [shards(): above = lax.ppermute(above, 'seq', up)]
    ppermute x1, waiting for transfers between devices: 2.17 us -> 2.97 us  [shards(): far = lax.ppermute(cot[:upper * width], 'seq', down)]
  transfers between devices with their start and end apart: 15 -> 15, of which waited for: 9 -> 9; matrix products, arithmetic and copies ran while one was open for 4% -> 4% of each run, Pallas kernels for 34% -> 33%
where the time goes in v5:
time: 73.4 us; the launch traced here: 73 us
  Pallas kernels  31.1 us (42%)
  starting transfers between devices  20.8 us (28%)
  waiting for transfers between devices  14.9 us (20%)
  local copies, waits for them, and re-layouts  5.44 us (7%)
  between operations  0.81 us (1%)
    pallas_call x9, Pallas kernels, call(): pl.pallas_call(body, out_shape=[*outs, TOKEN], in_specs=[SPACE[c] for c i...  31.1 us
    ppermute x3, waiting for transfers between devices, shards(): lax.ppermute(s, 'dp', [(i, peer(i, k, dp)) for i in range(dp)])  5.3 us
    ppermute x3, starting transfers between devices, shards(): lax.ppermute(s, 'seq', [(i, 2 * peer(i // 2, k, levels) + i % 2) for i in...  5.22 us
    ppermute x1, starting transfers between devices, shards(): above = lax.ppermute(above, 'seq', up)  5.09 us
    ppermute x3, starting transfers between devices, shards(): lax.ppermute(s, 'dp', [(i, peer(i, k, dp)) for i in range(dp)])  3.55 us
    ppermute x3, starting transfers between devices, shards(): lax.ppermute(small, 'dp', [(peer(i, k, dp), i) for i in range(dp)])  3.49 us
    ppermute x3, waiting for transfers between devices, shards(): lax.ppermute(small, 'dp', [(peer(i, k, dp), i) for i in range(dp)])  3.28 us
    ppermute x1, waiting for transfers between devices, shards(): far = lax.ppermute(cot[:upper * width], 'seq', down)  2.97 us
  transfers between devices with their start and end apart: 15, of which 9 were waited for; matrix products, arithmetic and copies ran while one was open for 4% of the time, Pallas kernels for 33%

profile of v5, /device:TPU:0, one launch (start us, length us, event | category | flops | bytes accessed | tf_op | source)
XLA Modules:
  0.0 73.0 jit_solution(14686680815315032325)
XLA Ops:
  1.2 2.2 %slice.14 = bf16[1,1,9,160,256]{4,3,2,1,0:T(8,128)(2,1)} slice(bf16[1,1,16,160,256]{4,3,2,1,0:T(8,128)(2,1)} %param.5), slice={[0:1], [0:1], [0:9], [0:160], [0:256]} | slice | bytes 1474560 | tf_op jit(solution)/shard_map/slice | solution.py:421
  3.4 1.3 %collective-permute-start.1 = (bf16[1440,256]{1,0:T(8,128)(2,1)}, bf16[1440,256]{1,0:T(8,128)(2,1)S(1)}, u32[]{:S(2)}, u32[]{:S(2)}) collective-permute-start(bf16[1440,256]{1,0:T(8,128)(2,1)} %bitcast.4), channel_id=1, source_target_pairs={{2,0},{3,1},{4,2},{5,3},{6,4},{7,5},{10,8},{11,9},{12,10},{13,11},... | collective-permute-start | bytes 2211848 | tf_op jit(solution)/shard_map/ppermute | solution.py:421
  5.6 5.1 %collective-permute-start.3 = (bf16[1280,256]{1,0:T(8,128)(2,1)}, bf16[1280,256]{1,0:T(8,128)(2,1)S(1)}, u32[]{:S(2)}, u32[]{:S(2)}) collective-permute-start(bf16[1280,256]{1,0:T(8,128)(2,1)} %bitcast.16), channel_id=1, source_target_pairs={{0,2},{1,3},{2,4},{3,5},{4,6},{5,7},{8,10},{9,11},{10,12},{11,13},... | collective-permute-start | bytes 1966088 | tf_op jit(solution)/shard_map/ppermute | solution.py:423
  10.7 1.3 %copy-done.2 = bf16[1,1,16,160,256]{4,3,2,1,0:T(8,128)(2,1)S(1)} copy-done((bf16[1,1,16,160,256]{4,3,2,1,0:T(8,128)(2,1)S(1)}, bf16[1,1,16,160,256]{4,3,2,1,0:T(8,128)(2,1)}, u32[]{:S(2)}) %copy-start.2) | copy-done | bytes 1310744
  12.0 1.0 %copy-done.3 = bf16[3,256,256]{2,1,0:T(8,128)(2,1)S(1)} copy-done((bf16[3,256,256]{2,1,0:T(8,128)(2,1)S(1)}, bf16[3,256,256]{2,1,0:T(8,128)(2,1)}, u32[]{:S(2)}) %copy-start.3) | copy-done | bytes 393240
  13.0 9.0 %local.1 = (bf16[1440,256]{1,0:T(8,128)(2,1)S(1)}, f32[1440,256]{1,0:T(8,128)S(1)}, f32[1440,256]{1,0:T(8,128)S(1)}, f32[1120,256]{1,0:T(8,128)S(1)}, f32[9,256,...) custom-call(s32[1]{0:T(128)} %bitcast.refs_0_, ...), custom_call_target="tpu_custom_call" | custom-call | flops 5704253440 | bytes 14663684 | tf_op jit(solution)/shard_map/local/pallas_call | solution.py:50
  22.1 3.0 %collective-permute-done.1.refs_6_ = bf16[1440,256]{1,0:T(8,128)(2,1)S(1)} collective-permute-done((bf16[1440,256]{1,0:T(8,128)(2,1)}, bf16[1440,256]{1,0:T(8,128)(2,1)S(1)}, u32[]{:S(2)}, u32[]{:S(2)}) %collective-permute-start.1) | collective-permute-done | bytes 737312 | tf_op jit(solution)/shard_map/ppermute | solution.py:421
  25.5 4.9 %remote.1 = (f32[9,256,256]{2,1,0:T(8,128)S(1)}, f32[3,256,256]{2,1,0:T(8,128)S(1)}, bf16[1120,256]{1,0:T(8,128)(2,1)}, f32[8,128]{1,0:T(8,128)S(1)}) custom-call(s32[1]{0:T(128)} %bitcast.refs_0_, bf16[1280,256]{1,0:T(8,128)(2,1)S(1)} %collective-permute-done.3.refs_1_, bf16[2560,256]{1,0:T(8,128)(2,1)S(1)} %bitcast.14, ...), custom_call_target="tpu_custom_call" | custom-call | flops 2684354560 | bytes 12468228 | tf_op jit(solution)/shard_map/remote/pallas_call | solution.py:50
  30.4 5.9 %own.1 = (bf16[90112,256]{1,0:T(8,128)(2,1)}, f32[45056,256]{1,0:T(8,128)}, bf16[4,384,256]{2,1,0:T(8,128)(2,1)}, f32[8,128]{1,0:T(8,128)}) custom-call(s32[1]{0:T(128)} %bitcast.refs_0_, bf16[2560,256]{1,0:T(8,128)(2,1)S(1)} %bitcast.11, bf16[1440,256]{1,0:T(8,128)(2,1)S(1)} %get-tuple-element.41.refs_2_, ...), custom_call_target="tpu_custom_call", output_to_operand_aliasing={{0}: (10, {})} | custom-call | flops 2684354560 | bytes 10797060 | tf_op jit(solution)/shard_map/own/pallas_call | solution.py:50
  36.4 1.5 %collective-permute-start.4 = (bf16[1120,256]{1,0:T(8,128)(2,1)}, bf16[1120,256]{1,0:T(8,128)(2,1)S(1)}, u32[]{:S(2)}, u32[]{:S(2)}) collective-permute-start(bf16[1120,256]{1,0:T(8,128)(2,1)} %get-tuple-element.57), channel_id=1, source_target_pairs={{2,0},{3,1},{4,2},{5,3},{6,4},{7,5},{10,8},{11,9},{12,10},{13,11},... | collective-permute-start | bytes 1720328 | tf_op jit(solution)/shard_map/ppermute | solution.py:481
  37.9 0.9 %collective-permute-done.5.refs_2_ = bf16[4,384,256]{2,1,0:T(8,128)(2,1)S(1)} collective-permute-done((bf16[4,384,256]{2,1,0:T(8,128)(2,1)}, bf16[4,384,256]{2,1,0:T(8,128)(2,1)S(1)}, u32[]{:S(2)}, u32[]{:S(2)}) %collective-permute-start.5) | collective-permute-done | bytes 786464 | tf_op jit(solution)/shard_map/ppermute | solution.py:473
  38.9 1.4 %split.1 = (f32[4,96,256]{2,1,0:T(8,128)S(1)}, bf16[4,96,256]{2,1,0:T(8,128)(2,1)S(1)}, bf16[4,96,256]{2,1,0:T(8,128)(2,1)S(1)}, bf16[4,96,256]{2,1,0:T(8,128)(2,1)S(1)}, f32[8,128]{1,0:T(8,128)S(1)}) custom-call(s32[1]{0:T(128)} %bitcast.5.refs_0_, f32[45056,256]{1,0:T(8,128)} %get-tuple-element.58.refs_1_, ...), custom_call_target="tpu_custom_call" | custom-call | flops 20971520 | bytes 1769476 | tf_op jit(solution)/shard_map/split/pallas_call | solution.py:50
  40.3 1.7 %collective-permute-start.6 = (bf16[4,96,256]{2,1,0:T(8,128)(2,1)S(1)}, bf16[4,96,256]{2,1,0:T(8,128)(2,1)S(1)}, u32[]{:S(2)}, u32[]{:S(2)}) collective-permute-start(bf16[4,96,256]{2,1,0:T(8,128)(2,1)S(1)} %get-tuple-element.63), channel_id=1, source_target_pairs={{0,8},{8,0},{16,24},{24,16},{1,9},{9,1},{17,25},{25,17},{2,10},{10... | collective-permute-start | bytes 589832 | tf_op jit(solution)/shard_map/ppermute | solution.py:480
  42.0 1.5 %collective-permute-start.7 = (bf16[4,96,256]{2,1,0:T(8,128)(2,1)S(1)}, bf16[4,96,256]{2,1,0:T(8,128)(2,1)S(1)}, u32[]{:S(2)}, u32[]{:S(2)}) collective-permute-start(bf16[4,96,256]{2,1,0:T(8,128)(2,1)S(1)} %get-tuple-element.64), channel_id=1, source_target_pairs={{0,16},{8,24},{16,0},{24,8},{1,17},{9,25},{17,1},{25,9},{2,18},{10... | collective-permute-start | bytes 589832 | tf_op jit(solution)/shard_map/ppermute | solution.py:480
  43.9 3.7 %back_top.1 = (bf16[2560,256]{1,0:T(8,128)(2,1)}, f32[8,128]{1,0:T(8,128)S(1)}) custom-call(bf16[90112,256]{1,0:T(8,128)(2,1)} %get-tuple-element.56.refs_0_, bf16[3,3,256,256]{3,2,1,0:T(8,128)(2,1)S(1)} %copy-done, f32[8,128]{1,0:T(8,128)S(1)} %get-tuple-element.60.refs_2_), custom_call_target="tpu_custom_call" | custom-call | flops 1509949440 | bytes 2490368 | tf_op jit(solution)/shard_map/back_top/pallas_call | solution.py:50
  48.1 4.8 %collective-permute-done.7.refs_3_ = bf16[4,96,256]{2,1,0:T(8,128)(2,1)S(1)} collective-permute-done((bf16[4,96,256]{2,1,0:T(8,128)(2,1)S(1)}, bf16[4,96,256]{2,1,0:T(8,128)(2,1)S(1)}, u32[]{:S(2)}, u32[]{:S(2)}) %collective-permute-start.7) | collective-permute-done | bytes 196640 | tf_op jit(solution)/shard_map/ppermute | solution.py:480
  53.8 2.4 %collective-permute-start.9 = (bf16[96,256]{1,0:T(8,128)(2,1)S(1)}, bf16[96,256]{1,0:T(8,128)(2,1)S(1)}, u32[]{:S(2)}, u32[]{:S(2)}) collective-permute-start(bf16[96,256]{1,0:T(8,128)(2,1)S(1)} %get-tuple-element.70), channel_id=1, source_target_pairs={{0,2},{1,3},{2,0},{3,1},{4,6},{5,7},{6,4},{7,5},{8,10},{9,11},{10,... | collective-permute-start | bytes 147464 | tf_op jit(solution)/shard_map/ppermute | solution.py:493
  56.2 2.8 %collective-permute-start.10 = (bf16[96,256]{1,0:T(8,128)(2,1)S(1)}, bf16[96,256]{1,0:T(8,128)(2,1)S(1)}, u32[]{:S(2)}, u32[]{:S(2)}) collective-permute-start(bf16[96,256]{1,0:T(8,128)(2,1)S(1)} %get-tuple-element.71), channel_id=1, source_target_pairs={{0,4},{1,5},{2,6},{3,7},{4,0},{5,1},{6,2},{7,3},{8,12},{9,13},{10,... | collective-permute-start | bytes 147464 | tf_op jit(solution)/shard_map/ppermute | solution.py:493
  59.0 3.9 %back_bottom.1 = (bf16[2560,256]{1,0:T(8,128)(2,1)}, f32[8,128]{1,0:T(8,128)S(1)}) custom-call(bf16[90112,256]{1,0:T(8,128)(2,1)} %get-tuple-element.56.refs_0_, bf16[1120,256]{1,0:T(8,128)(2,1)S(1)} %collective-permute-done.4.refs_1_, bf16[3,3,256,256]{3,2,1,0:T(8,128)(2,1)S(1)} %copy-done, ...), custom_call_target="tpu_custom_call", output_to_operand_aliasing={{0}: (3, {})} | custom-call | flops 1509949440 | bytes 4374528 | tf_op jit(solution)/shard_map/back_bottom/pallas_call | solution.py:50
  62.9 2.0 %collective-permute-done.11.refs_3_ = bf16[96,256]{1,0:T(8,128)(2,1)S(1)} collective-permute-done((bf16[96,256]{1,0:T(8,128)(2,1)S(1)}, bf16[96,256]{1,0:T(8,128)(2,1)S(1)}, u32[]{:S(2)}, u32[]{:S(2)}) %collective-permute-start.11) | collective-permute-done | bytes 49184 | tf_op jit(solution)/shard_map/ppermute | solution.py:493
  65.5 1.5 %collective-permute-start.14 = (bf16[96,256]{1,0:T(8,128)(2,1)S(1)}, bf16[96,256]{1,0:T(8,128)(2,1)S(1)}, u32[]{:S(2)}, u32[]{:S(2)}) collective-permute-start(bf16[96,256]{1,0:T(8,128)(2,1)S(1)} %get-tuple-element.74.refs_1_), channel_id=1, source_target_pairs={{24,0},{16,8},{8,16},{0,24},{25,1},{17,9},{9,17},{1,25},{26,2},{18... | collective-permute-start | bytes 147464 | tf_op jit(solution)/shard_map/ppermute | solution.py:505
  67.0 1.2 %collective-permute-start.13 = (bf16[96,256]{1,0:T(8,128)(2,1)S(1)}, bf16[96,256]{1,0:T(8,128)(2,1)S(1)}, u32[]{:S(2)}, u32[]{:S(2)}) collective-permute-start(bf16[96,256]{1,0:T(8,128)(2,1)S(1)} %get-tuple-element.74.refs_1_), channel_id=1, source_target_pairs={{16,0},{24,8},{0,16},{8,24},{17,1},{25,9},{1,17},{9,25},{18,2},{26... | collective-permute-start | bytes 147464 | tf_op jit(solution)/shard_map/ppermute | solution.py:505
  69.0 1.5 %collective-permute-done.14.refs_4_ = bf16[96,256]{1,0:T(8,128)(2,1)S(1)} collective-permute-done((bf16[96,256]{1,0:T(8,128)(2,1)S(1)}, bf16[96,256]{1,0:T(8,128)(2,1)S(1)}, u32[]{:S(2)}, u32[]{:S(2)}) %collective-permute-start.14) | collective-permute-done | bytes 49184 | tf_op jit(solution)/shard_map/ppermute | solution.py:505
  71.1 1.2 %collective-permute-done.12.refs_2_ = bf16[96,256]{1,0:T(8,128)(2,1)S(1)} collective-permute-done((bf16[96,256]{1,0:T(8,128)(2,1)S(1)}, bf16[96,256]{1,0:T(8,128)(2,1)S(1)}, u32[]{:S(2)}, u32[]{:S(2)}) %collective-permute-start.12) | collective-permute-done | bytes 49184 | tf_op jit(solution)/shard_map/ppermute | solution.py:505
  (27 shorter events, 6.5 us)
Async XLA Ops:
  0.6 4.1 %copy-start.1 = (bf16[1,1,16,160,256]{4,3,2,1,0:T(8,128)(2,1)S(1)}, bf16[1,1,16,160,256]{4,3,2,1,0:T(8,128)(2,1)}, u32[]{:S(2)}) copy-start(bf16[1,1,16,160,256]{4,3,2,1,0:T(8,128)(2,1)} %param.4) | copy-start | bytes 3932164
  0.6 10.1 %copy-start = (bf16[3,3,256,256]{3,2,1,0:T(8,128)(2,1)S(1)}, bf16[3,3,256,256]{3,2,1,0:T(8,128)(2,1)}, u32[]{:S(2)}) copy-start(bf16[3,3,256,256]{3,2,1,0:T(8,128)(2,1)} %refs_2_.1) | copy-start | bytes 3538948
  0.6 4.9 %collective-permute-start = (bf16[2560,256]{1,0:T(8,128)(2,1)}, bf16[2560,256]{1,0:T(8,128)(2,1)}, u32[]{:S(2)}, u32[]{:S(2)}) collective-permute-start(bf16[2560,256]{1,0:T(8,128)(2,1)} %bitcast.12), channel_id=1, source_target_pairs={{0,1},{1,0},{2,3},{3,2},{4,5},{5,4},{6,7},{7,6},{8,9},{9,8},{10,11... | collective-permute-start | bytes 3932168 | tf_op jit(solution)/shard_map/ppermute | solution.py:420
  3.4 21.6 %collective-permute-start.1 = (bf16[1440,256]{1,0:T(8,128)(2,1)}, bf16[1440,256]{1,0:T(8,128)(2,1)S(1)}, u32[]{:S(2)}, u32[]{:S(2)}) collective-permute-start(bf16[1440,256]{1,0:T(8,128)(2,1)} %bitcast.4), channel_id=1, source_target_pairs={{2,0},{3,1},{4,2},{5,3},{6,4},{7,5},{10,8},{11,9},{12,10},{13,11},... | collective-permute-start | bytes 2211848 | tf_op jit(solution)/shard_map/ppermute | solution.py:421
  5.6 19.9 %collective-permute-start.3 = (bf16[1280,256]{1,0:T(8,128)(2,1)}, bf16[1280,256]{1,0:T(8,128)(2,1)S(1)}, u32[]{:S(2)}, u32[]{:S(2)}) collective-permute-start(bf16[1280,256]{1,0:T(8,128)(2,1)} %bitcast.16), channel_id=1, source_target_pairs={{0,2},{1,3},{2,4},{3,5},{4,6},{5,7},{8,10},{9,11},{10,12},{11,13},... | collective-permute-start | bytes 1966088 | tf_op jit(solution)/shard_map/ppermute | solution.py:423
  10.7 1.3 %copy-start.2 = (bf16[1,1,16,160,256]{4,3,2,1,0:T(8,128)(2,1)S(1)}, bf16[1,1,16,160,256]{4,3,2,1,0:T(8,128)(2,1)}, u32[]{:S(2)}) copy-start(bf16[1,1,16,160,256]{4,3,2,1,0:T(8,128)(2,1)} %param.5) | copy-start | bytes 3932164
  12.0 1.0 %copy-start.3 = (bf16[3,256,256]{2,1,0:T(8,128)(2,1)S(1)}, bf16[3,256,256]{2,1,0:T(8,128)(2,1)}, u32[]{:S(2)}) copy-start(bf16[3,256,256]{2,1,0:T(8,128)(2,1)} %refs_7_.1) | copy-start | bytes 1179652
  25.0 5.3 %collective-permute-start.2 = (bf16[1440,256]{1,0:T(8,128)(2,1)S(1)}, bf16[1440,256]{1,0:T(8,128)(2,1)S(1)}, u32[]{:S(2)}, u32[]{:S(2)}) collective-permute-start(bf16[1440,256]{1,0:T(8,128)(2,1)S(1)} %collective-permute-done.1.refs_6_), channel_id=1, source_target_pairs={{0,1},{1,0},{2,3},{3,2},{4,5},{5,4},{6,7},{7,6},{8,9},{9,8},{10,11... | collective-permute-start | bytes 2211848 | tf_op jit(solution)/shard_map/ppermute | solution.py:441
  25.5 4.9 %copy-start.4 = (bf16[3,256,256]{2,1,0:T(8,128)(2,1)S(1)}, bf16[3,256,256]{2,1,0:T(8,128)(2,1)}, u32[]{:S(2)}) copy-start(bf16[3,256,256]{2,1,0:T(8,128)(2,1)} %refs_7_.1) | copy-start | bytes 1179652
  36.3 2.6 %collective-permute-start.5 = (bf16[4,384,256]{2,1,0:T(8,128)(2,1)}, bf16[4,384,256]{2,1,0:T(8,128)(2,1)S(1)}, u32[]{:S(2)}, u32[]{:S(2)}) collective-permute-start(bf16[4,384,256]{2,1,0:T(8,128)(2,1)} %get-tuple-element.59), channel_id=1, source_target_pairs={{0,1},{1,0},{2,3},{3,2},{4,5},{5,4},{6,7},{7,6},{8,9},{9,8},{10,11... | collective-permute-start | bytes 2359304 | tf_op jit(solution)/shard_map/ppermute | solution.py:473
  36.4 22.5 %collective-permute-start.4 = (bf16[1120,256]{1,0:T(8,128)(2,1)}, bf16[1120,256]{1,0:T(8,128)(2,1)S(1)}, u32[]{:S(2)}, u32[]{:S(2)}) collective-permute-start(bf16[1120,256]{1,0:T(8,128)(2,1)} %get-tuple-element.57), channel_id=1, source_target_pairs={{2,0},{3,1},{4,2},{5,3},{6,4},{7,5},{10,8},{11,9},{12,10},{13,11},... | collective-permute-start | bytes 1720328 | tf_op jit(solution)/shard_map/ppermute | solution.py:481
  40.3 7.8 %collective-permute-start.6 = (bf16[4,96,256]{2,1,0:T(8,128)(2,1)S(1)}, bf16[4,96,256]{2,1,0:T(8,128)(2,1)S(1)}, u32[]{:S(2)}, u32[]{:S(2)}) collective-permute-start(bf16[4,96,256]{2,1,0:T(8,128)(2,1)S(1)} %get-tuple-element.63), channel_id=1, source_target_pairs={{0,8},{8,0},{16,24},{24,16},{1,9},{9,1},{17,25},{25,17},{2,10},{10... | collective-permute-start | bytes 589832 | tf_op jit(solution)/shard_map/ppermute | solution.py:480
  42.0 10.9 %collective-permute-start.7 = (bf16[4,96,256]{2,1,0:T(8,128)(2,1)S(1)}, bf16[4,96,256]{2,1,0:T(8,128)(2,1)S(1)}, u32[]{:S(2)}, u32[]{:S(2)}) collective-permute-start(bf16[4,96,256]{2,1,0:T(8,128)(2,1)S(1)} %get-tuple-element.64), channel_id=1, source_target_pairs={{0,16},{8,24},{16,0},{24,8},{1,17},{9,25},{17,1},{25,9},{2,18},{10... | collective-permute-start | bytes 589832 | tf_op jit(solution)/shard_map/ppermute | solution.py:480
  43.5 9.4 %collective-permute-start.8 = (bf16[4,96,256]{2,1,0:T(8,128)(2,1)S(1)}, bf16[4,96,256]{2,1,0:T(8,128)(2,1)S(1)}, u32[]{:S(2)}, u32[]{:S(2)}) collective-permute-start(bf16[4,96,256]{2,1,0:T(8,128)(2,1)S(1)} %get-tuple-element.65), channel_id=1, source_target_pairs={{0,24},{8,16},{16,8},{24,0},{1,25},{9,17},{17,9},{25,1},{2,26},{10... | collective-permute-start | bytes 589832 | tf_op jit(solution)/shard_map/ppermute | solution.py:480
  53.8 9.1 %collective-permute-start.9 = (bf16[96,256]{1,0:T(8,128)(2,1)S(1)}, bf16[96,256]{1,0:T(8,128)(2,1)S(1)}, u32[]{:S(2)}, u32[]{:S(2)}) collective-permute-start(bf16[96,256]{1,0:T(8,128)(2,1)S(1)} %get-tuple-element.70), channel_id=1, source_target_pairs={{0,2},{1,3},{2,0},{3,1},{4,6},{5,7},{6,4},{7,5},{8,10},{9,11},{10,... | collective-permute-start | bytes 147464 | tf_op jit(solution)/shard_map/ppermute | solution.py:493
  56.2 6.7 %collective-permute-start.10 = (bf16[96,256]{1,0:T(8,128)(2,1)S(1)}, bf16[96,256]{1,0:T(8,128)(2,1)S(1)}, u32[]{:S(2)}, u32[]{:S(2)}) collective-permute-start(bf16[96,256]{1,0:T(8,128)(2,1)S(1)} %get-tuple-element.71), channel_id=1, source_target_pairs={{0,4},{1,5},{2,6},{3,7},{4,0},{5,1},{6,2},{7,3},{8,12},{9,13},{10,... | collective-permute-start | bytes 147464 | tf_op jit(solution)/shard_map/ppermute | solution.py:493
  59.0 5.9 %collective-permute-start.11 = (bf16[96,256]{1,0:T(8,128)(2,1)S(1)}, bf16[96,256]{1,0:T(8,128)(2,1)S(1)}, u32[]{:S(2)}, u32[]{:S(2)}) collective-permute-start(bf16[96,256]{1,0:T(8,128)(2,1)S(1)} %get-tuple-element.72), channel_id=1, source_target_pairs={{0,6},{1,7},{2,4},{3,5},{4,2},{5,3},{6,0},{7,1},{8,14},{9,15},{10,... | collective-permute-start | bytes 147464 | tf_op jit(solution)/shard_map/ppermute | solution.py:493
  65.5 5.0 %collective-permute-start.14 = (bf16[96,256]{1,0:T(8,128)(2,1)S(1)}, bf16[96,256]{1,0:T(8,128)(2,1)S(1)}, u32[]{:S(2)}, u32[]{:S(2)}) collective-permute-start(bf16[96,256]{1,0:T(8,128)(2,1)S(1)} %get-tuple-element.74.refs_1_), channel_id=1, source_target_pairs={{24,0},{16,8},{8,16},{0,24},{25,1},{17,9},{9,17},{1,25},{26,2},{18... | collective-permute-start | bytes 147464 | tf_op jit(solution)/shard_map/ppermute | solution.py:505
  67.0 4.1 %collective-permute-start.13 = (bf16[96,256]{1,0:T(8,128)(2,1)S(1)}, bf16[96,256]{1,0:T(8,128)(2,1)S(1)}, u32[]{:S(2)}, u32[]{:S(2)}) collective-permute-start(bf16[96,256]{1,0:T(8,128)(2,1)S(1)} %get-tuple-element.74.refs_1_), channel_id=1, source_target_pairs={{16,0},{24,8},{0,16},{8,24},{17,1},{25,9},{1,17},{9,25},{18,2},{26... | collective-permute-start | bytes 147464 | tf_op jit(solution)/shard_map/ppermute | solution.py:505
  68.2 4.1 %collective-permute-start.12 = (bf16[96,256]{1,0:T(8,128)(2,1)S(1)}, bf16[96,256]{1,0:T(8,128)(2,1)S(1)}, u32[]{:S(2)}, u32[]{:S(2)}) collective-permute-start(bf16[96,256]{1,0:T(8,128)(2,1)S(1)} %get-tuple-element.74.refs_1_), channel_id=1, source_target_pairs={{8,0},{0,8},{24,16},{16,24},{9,1},{1,9},{25,17},{17,25},{10,2},{2,... | collective-permute-start | bytes 147464 | tf_op jit(solution)/shard_map/ppermute | solution.py:505

commit v6 on v5

--- a/solution.py
+++ b/solution.py
@@ -98,7 +98,7 @@
 
 
 def chunk(n):
-    return n if n < 8 else max(d for d in range(1, 7) if n % d == 0)
+    return n if n < 10 else max(d for d in range(1, 7) if n % d == 0)
 
 
 def silu_parts(v):
@@ -491,7 +491,7 @@
     )
     got = [
         lax.ppermute(s, "seq", [(i, 2 * peer(i // 2, k, levels) + i % 2) for i in range(seq)])
-        for k, s in enumerate(sends, 1)
+        for k, s in reversed(list(enumerate(sends, 1)))
     ]
     back, token = call(
         functools.partial(back_bottom_kernel, rows, width), "back_bottom", "hhhh h", 9 * mac,

time: 73.4 us -> 71.3 us (0.971)
  Pallas kernels: 31.1 us -> 29.2 us
    pallas_call x9, Pallas kernels: 31.1 us -> 29.2 us  [call(): pl.pallas_call(body, out_shape=[*outs, TOKEN], in_specs=[SPACE[c] for c i...]
    ppermute x3, waiting for transfers between devices: 1.96 us -> 0.44 us  [shards(): lax.ppermute(s, 'seq', [(i, 2 * peer(i // 2, k, levels) + i % 2) for i in...]
    ppermute x1, waiting for transfers between devices: 2.97 us -> 4.25 us  [shards(): far = lax.ppermute(cot[:upper * width], 'seq', down)]
  transfers between devices with their start and end apart: 15 -> 15, of which waited for: 9 -> 9; matrix products, arithmetic and copies ran while one was open for 4% -> 4% of each run, Pallas kernels for 33% -> 32%
where the time goes in v6:
time: 71.3 us; the launch traced here: 70.9 us
  Pallas kernels  29.2 us (41%)
  starting transfers between devices  20.8 us (29%)
  waiting for transfers between devices  14.6 us (20%)
  local copies, waits for them, and re-layouts  5.44 us (8%)
  between operations  0.8 us (1%)
    pallas_call x9, Pallas kernels, call(): pl.pallas_call(body, out_shape=[*outs, TOKEN], in_specs=[SPACE[c] for c i...  29.2 us
    ppermute x3, waiting for transfers between devices, shards(): lax.ppermute(s, 'dp', [(i, peer(i, k, dp)) for i in range(dp)])  5.31 us
    ppermute x3, starting transfers between devices, shards(): lax.ppermute(s, 'seq', [(i, 2 * peer(i // 2, k, levels) + i % 2) for i in...  5.29 us
    ppermute x1, starting transfers between devices, shards(): above = lax.ppermute(above, 'seq', up)  5.09 us
    ppermute x1, waiting for transfers between devices, shards(): far = lax.ppermute(cot[:upper * width], 'seq', down)  4.25 us
    ppermute x3, starting transfers between devices, shards(): lax.ppermute(s, 'dp', [(i, peer(i, k, dp)) for i in range(dp)])  3.55 us
    ppermute x3, starting transfers between devices, shards(): lax.ppermute(small, 'dp', [(peer(i, k, dp), i) for i in range(dp)])  3.49 us
    ppermute x3, waiting for transfers between devices, shards(): lax.ppermute(small, 'dp', [(peer(i, k, dp), i) for i in range(dp)])  3.28 us
  transfers between devices with their start and end apart: 15, of which 9 were waited for; matrix products, arithmetic and copies ran while one was open for 4% of the time, Pallas kernels for 32%

profile of v6, /device:TPU:0, one launch (start us, length us, event | category | flops | bytes accessed | tf_op | source)
XLA Modules:
  0.0 70.9 jit_solution(17507118791282126018)
XLA Ops:
  1.2 2.2 %slice.14 = bf16[1,1,9,160,256]{4,3,2,1,0:T(8,128)(2,1)} slice(bf16[1,1,16,160,256]{4,3,2,1,0:T(8,128)(2,1)} %param.5), slice={[0:1], [0:1], [0:9], [0:160], [0:256]} | slice | bytes 1474560 | tf_op jit(solution)/shard_map/slice | solution.py:421
  3.4 1.3 %collective-permute-start.1 = (bf16[1440,256]{1,0:T(8,128)(2,1)}, bf16[1440,256]{1,0:T(8,128)(2,1)S(1)}, u32[]{:S(2)}, u32[]{:S(2)}) collective-permute-start(bf16[1440,256]{1,0:T(8,128)(2,1)} %bitcast.4), channel_id=1, source_target_pairs={{2,0},{3,1},{4,2},{5,3},{6,4},{7,5},{10,8},{11,9},{12,10},{13,11},... | collective-permute-start | bytes 2211848 | tf_op jit(solution)/shard_map/ppermute | solution.py:421
  4.7 0.9 %slice.12 = bf16[1,1,8,160,256]{4,3,2,1,0:T(8,128)(2,1)} slice(bf16[1,1,16,160,256]{4,3,2,1,0:T(8,128)(2,1)S(1)} %copy-done.1), slice={[0:1], [0:1], [8:16], [0:160], [0:256]} | slice | bytes 1310720 | tf_op jit(solution)/shard_map/slice | solution.py:422
  5.6 5.1 %collective-permute-start.3 = (bf16[1280,256]{1,0:T(8,128)(2,1)}, bf16[1280,256]{1,0:T(8,128)(2,1)S(1)}, u32[]{:S(2)}, u32[]{:S(2)}) collective-permute-start(bf16[1280,256]{1,0:T(8,128)(2,1)} %bitcast.16), channel_id=1, source_target_pairs={{0,2},{1,3},{2,4},{3,5},{4,6},{5,7},{8,10},{9,11},{10,12},{11,13},... | collective-permute-start | bytes 1966088 | tf_op jit(solution)/shard_map/ppermute | solution.py:423
  10.7 1.3 %copy-done.2 = bf16[1,1,16,160,256]{4,3,2,1,0:T(8,128)(2,1)S(1)} copy-done((bf16[1,1,16,160,256]{4,3,2,1,0:T(8,128)(2,1)S(1)}, bf16[1,1,16,160,256]{4,3,2,1,0:T(8,128)(2,1)}, u32[]{:S(2)}) %copy-start.2) | copy-done | bytes 1310744
  12.0 1.0 %copy-done.3 = bf16[3,256,256]{2,1,0:T(8,128)(2,1)S(1)} copy-done((bf16[3,256,256]{2,1,0:T(8,128)(2,1)S(1)}, bf16[3,256,256]{2,1,0:T(8,128)(2,1)}, u32[]{:S(2)}) %copy-start.3) | copy-done | bytes 393240
  13.0 7.7 %local.1 = (bf16[1440,256]{1,0:T(8,128)(2,1)S(1)}, f32[1440,256]{1,0:T(8,128)S(1)}, f32[1440,256]{1,0:T(8,128)S(1)}, f32[1120,256]{1,0:T(8,128)S(1)}, f32[9,256,...) custom-call(s32[1]{0:T(128)} %bitcast.refs_0_, ...), custom_call_target="tpu_custom_call" | custom-call | flops 5704253440 | bytes 14663684 | tf_op jit(solution)/shard_map/local/pallas_call | solution.py:50
  20.8 4.3 %collective-permute-done.1.refs_6_ = bf16[1440,256]{1,0:T(8,128)(2,1)S(1)} collective-permute-done((bf16[1440,256]{1,0:T(8,128)(2,1)}, bf16[1440,256]{1,0:T(8,128)(2,1)S(1)}, u32[]{:S(2)}, u32[]{:S(2)}) %collective-permute-start.1) | collective-permute-done | bytes 737312 | tf_op jit(solution)/shard_map/ppermute | solution.py:421
  25.5 4.9 %remote.1 = (f32[9,256,256]{2,1,0:T(8,128)S(1)}, f32[3,256,256]{2,1,0:T(8,128)S(1)}, bf16[1120,256]{1,0:T(8,128)(2,1)}, f32[8,128]{1,0:T(8,128)S(1)}) custom-call(s32[1]{0:T(128)} %bitcast.refs_0_, bf16[1280,256]{1,0:T(8,128)(2,1)S(1)} %collective-permute-done.3.refs_1_, bf16[2560,256]{1,0:T(8,128)(2,1)S(1)} %bitcast.14, ...), custom_call_target="tpu_custom_call" | custom-call | flops 2684354560 | bytes 12468228 | tf_op jit(solution)/shard_map/remote/pallas_call | solution.py:50
  30.4 5.3 %own.1 = (bf16[90112,256]{1,0:T(8,128)(2,1)}, f32[45056,256]{1,0:T(8,128)}, bf16[4,384,256]{2,1,0:T(8,128)(2,1)}, f32[8,128]{1,0:T(8,128)}) custom-call(s32[1]{0:T(128)} %bitcast.refs_0_, bf16[2560,256]{1,0:T(8,128)(2,1)S(1)} %bitcast.11, bf16[1440,256]{1,0:T(8,128)(2,1)S(1)} %get-tuple-element.41.refs_2_, ...), custom_call_target="tpu_custom_call", output_to_operand_aliasing={{0}: (10, {})} | custom-call | flops 2684354560 | bytes 10797060 | tf_op jit(solution)/shard_map/own/pallas_call | solution.py:50
  35.8 1.5 %collective-permute-start.4 = (bf16[1120,256]{1,0:T(8,128)(2,1)}, bf16[1120,256]{1,0:T(8,128)(2,1)S(1)}, u32[]{:S(2)}, u32[]{:S(2)}) collective-permute-start(bf16[1120,256]{1,0:T(8,128)(2,1)} %get-tuple-element.57), channel_id=1, source_target_pairs={{2,0},{3,1},{4,2},{5,3},{6,4},{7,5},{10,8},{11,9},{12,10},{13,11},... | collective-permute-start | bytes 1720328 | tf_op jit(solution)/shard_map/ppermute | solution.py:481
  37.3 0.9 %collective-permute-done.5.refs_2_ = bf16[4,384,256]{2,1,0:T(8,128)(2,1)S(1)} collective-permute-done((bf16[4,384,256]{2,1,0:T(8,128)(2,1)}, bf16[4,384,256]{2,1,0:T(8,128)(2,1)S(1)}, u32[]{:S(2)}, u32[]{:S(2)}) %collective-permute-start.5) | collective-permute-done | bytes 786464 | tf_op jit(solution)/shard_map/ppermute | solution.py:473
  38.2 1.4 %split.1 = (f32[4,96,256]{2,1,0:T(8,128)S(1)}, bf16[4,96,256]{2,1,0:T(8,128)(2,1)S(1)}, bf16[4,96,256]{2,1,0:T(8,128)(2,1)S(1)}, bf16[4,96,256]{2,1,0:T(8,128)(2,1)S(1)}, f32[8,128]{1,0:T(8,128)S(1)}) custom-call(s32[1]{0:T(128)} %bitcast.5.refs_0_, f32[45056,256]{1,0:T(8,128)} %get-tuple-element.58.refs_1_, ...), custom_call_target="tpu_custom_call" | custom-call | flops 20971520 | bytes 1769476 | tf_op jit(solution)/shard_map/split/pallas_call | solution.py:50
  39.7 1.7 %collective-permute-start.6 = (bf16[4,96,256]{2,1,0:T(8,128)(2,1)S(1)}, bf16[4,96,256]{2,1,0:T(8,128)(2,1)S(1)}, u32[]{:S(2)}, u32[]{:S(2)}) collective-permute-start(bf16[4,96,256]{2,1,0:T(8,128)(2,1)S(1)} %get-tuple-element.63), channel_id=1, source_target_pairs={{0,8},{8,0},{16,24},{24,16},{1,9},{9,1},{17,25},{25,17},{2,10},{10... | collective-permute-start | bytes 589832 | tf_op jit(solution)/shard_map/ppermute | solution.py:480
  41.4 1.5 %collective-permute-start.7 = (bf16[4,96,256]{2,1,0:T(8,128)(2,1)S(1)}, bf16[4,96,256]{2,1,0:T(8,128)(2,1)S(1)}, u32[]{:S(2)}, u32[]{:S(2)}) collective-permute-start(bf16[4,96,256]{2,1,0:T(8,128)(2,1)S(1)} %get-tuple-element.64), channel_id=1, source_target_pairs={{0,16},{8,24},{16,0},{24,8},{1,17},{9,25},{17,1},{25,9},{2,18},{10... | collective-permute-start | bytes 589832 | tf_op jit(solution)/shard_map/ppermute | solution.py:480
  43.2 3.7 %back_top.1 = (bf16[2560,256]{1,0:T(8,128)(2,1)}, f32[8,128]{1,0:T(8,128)S(1)}) custom-call(bf16[90112,256]{1,0:T(8,128)(2,1)} %get-tuple-element.56.refs_0_, bf16[3,3,256,256]{3,2,1,0:T(8,128)(2,1)S(1)} %copy-done, f32[8,128]{1,0:T(8,128)S(1)} %get-tuple-element.60.refs_2_), custom_call_target="tpu_custom_call" | custom-call | flops 1509949440 | bytes 2490368 | tf_op jit(solution)/shard_map/back_top/pallas_call | solution.py:50
  47.5 4.8 %collective-permute-done.7.refs_3_ = bf16[4,96,256]{2,1,0:T(8,128)(2,1)S(1)} collective-permute-done((bf16[4,96,256]{2,1,0:T(8,128)(2,1)S(1)}, bf16[4,96,256]{2,1,0:T(8,128)(2,1)S(1)}, u32[]{:S(2)}, u32[]{:S(2)}) %collective-permute-start.7) | collective-permute-done | bytes 196640 | tf_op jit(solution)/shard_map/ppermute | solution.py:480
  52.3 0.9 %level.1 = (f32[96,256]{1,0:T(8,128)S(1)}, bf16[96,256]{1,0:T(8,128)(2,1)S(1)}, bf16[96,256]{1,0:T(8,128)(2,1)S(1)}, bf16[96,256]{1,0:T(8,128)(2,1)S(1)}, f32[8,128]{1,0:T(8,128)S(1)}) custom-call(s32[1]{0:T(128)} %bitcast.6.refs_0_, f32[4,96,256]{2,1,0:T(8,128)S(1)} %get-tuple-element.62.refs_1_, bf16[4,96,256]{2,1,0:T(8,128)(2,1)S(1)} %collective-permute-done.6.refs_2_, ...), custom_call_target="tpu_custom_call" | custom-call | flops 20971520 | bytes 1228804 | tf_op jit(solution)/shard_map/level/pallas_call | solution.py:50
  53.1 4.7 %collective-permute-start.9 = (bf16[96,256]{1,0:T(8,128)(2,1)S(1)}, bf16[96,256]{1,0:T(8,128)(2,1)S(1)}, u32[]{:S(2)}, u32[]{:S(2)}) collective-permute-start(bf16[96,256]{1,0:T(8,128)(2,1)S(1)} %get-tuple-element.70), channel_id=1, source_target_pairs={{0,6},{1,7},{2,4},{3,5},{4,2},{5,3},{6,0},{7,1},{8,14},{9,15},{10,... | collective-permute-start | bytes 147464 | tf_op jit(solution)/shard_map/ppermute | solution.py:493
  58.4 3.9 %back_bottom.1 = (bf16[2560,256]{1,0:T(8,128)(2,1)}, f32[8,128]{1,0:T(8,128)S(1)}) custom-call(bf16[90112,256]{1,0:T(8,128)(2,1)} %get-tuple-element.56.refs_0_, bf16[1120,256]{1,0:T(8,128)(2,1)S(1)} %collective-permute-done.4.refs_1_, bf16[3,3,256,256]{3,2,1,0:T(8,128)(2,1)S(1)} %copy-done, ...), custom_call_target="tpu_custom_call", output_to_operand_aliasing={{0}: (3, {})} | custom-call | flops 1509949440 | bytes 4374528 | tf_op jit(solution)/shard_map/back_bottom/pallas_call | solution.py:50
  63.4 1.5 %collective-permute-start.14 = (bf16[96,256]{1,0:T(8,128)(2,1)S(1)}, bf16[96,256]{1,0:T(8,128)(2,1)S(1)}, u32[]{:S(2)}, u32[]{:S(2)}) collective-permute-start(bf16[96,256]{1,0:T(8,128)(2,1)S(1)} %get-tuple-element.74.refs_1_), channel_id=1, source_target_pairs={{24,0},{16,8},{8,16},{0,24},{25,1},{17,9},{9,17},{1,25},{26,2},{18... | collective-permute-start | bytes 147464 | tf_op jit(solution)/shard_map/ppermute | solution.py:505
  64.9 1.2 %collective-permute-start.13 = (bf16[96,256]{1,0:T(8,128)(2,1)S(1)}, bf16[96,256]{1,0:T(8,128)(2,1)S(1)}, u32[]{:S(2)}, u32[]{:S(2)}) collective-permute-start(bf16[96,256]{1,0:T(8,128)(2,1)S(1)} %get-tuple-element.74.refs_1_), channel_id=1, source_target_pairs={{16,0},{24,8},{0,16},{8,24},{17,1},{25,9},{1,17},{9,25},{18,2},{26... | collective-permute-start | bytes 147464 | tf_op jit(solution)/shard_map/ppermute | solution.py:505
  66.9 1.5 %collective-permute-done.14.refs_4_ = bf16[96,256]{1,0:T(8,128)(2,1)S(1)} collective-permute-done((bf16[96,256]{1,0:T(8,128)(2,1)S(1)}, bf16[96,256]{1,0:T(8,128)(2,1)S(1)}, u32[]{:S(2)}, u32[]{:S(2)}) %collective-permute-start.14) | collective-permute-done | bytes 49184 | tf_op jit(solution)/shard_map/ppermute | solution.py:505
  69.0 1.2 %collective-permute-done.12.refs_2_ = bf16[96,256]{1,0:T(8,128)(2,1)S(1)} collective-permute-done((bf16[96,256]{1,0:T(8,128)(2,1)S(1)}, bf16[96,256]{1,0:T(8,128)(2,1)S(1)}, u32[]{:S(2)}, u32[]{:S(2)}) %collective-permute-start.12) | collective-permute-done | bytes 49184 | tf_op jit(solution)/shard_map/ppermute | solution.py:505
  (27 shorter events, 5.8 us)
Async XLA Ops:
  0.6 4.1 %copy-start.1 = (bf16[1,1,16,160,256]{4,3,2,1,0:T(8,128)(2,1)S(1)}, bf16[1,1,16,160,256]{4,3,2,1,0:T(8,128)(2,1)}, u32[]{:S(2)}) copy-start(bf16[1,1,16,160,256]{4,3,2,1,0:T(8,128)(2,1)} %param.4) | copy-start | bytes 3932164
  0.6 10.1 %copy-start = (bf16[3,3,256,256]{3,2,1,0:T(8,128)(2,1)S(1)}, bf16[3,3,256,256]{3,2,1,0:T(8,128)(2,1)}, u32[]{:S(2)}) copy-start(bf16[3,3,256,256]{3,2,1,0:T(8,128)(2,1)} %refs_2_.1) | copy-start | bytes 3538948
  0.6 4.9 %collective-permute-start = (bf16[2560,256]{1,0:T(8,128)(2,1)}, bf16[2560,256]{1,0:T(8,128)(2,1)}, u32[]{:S(2)}, u32[]{:S(2)}) collective-permute-start(bf16[2560,256]{1,0:T(8,128)(2,1)} %bitcast.12), channel_id=1, source_target_pairs={{0,1},{1,0},{2,3},{3,2},{4,5},{5,4},{6,7},{7,6},{8,9},{9,8},{10,11... | collective-permute-start | bytes 3932168 | tf_op jit(solution)/shard_map/ppermute | solution.py:420
  3.4 21.6 %collective-permute-start.1 = (bf16[1440,256]{1,0:T(8,128)(2,1)}, bf16[1440,256]{1,0:T(8,128)(2,1)S(1)}, u32[]{:S(2)}, u32[]{:S(2)}) collective-permute-start(bf16[1440,256]{1,0:T(8,128)(2,1)} %bitcast.4), channel_id=1, source_target_pairs={{2,0},{3,1},{4,2},{5,3},{6,4},{7,5},{10,8},{11,9},{12,10},{13,11},... | collective-permute-start | bytes 2211848 | tf_op jit(solution)/shard_map/ppermute | solution.py:421
  5.6 19.9 %collective-permute-start.3 = (bf16[1280,256]{1,0:T(8,128)(2,1)}, bf16[1280,256]{1,0:T(8,128)(2,1)S(1)}, u32[]{:S(2)}, u32[]{:S(2)}) collective-permute-start(bf16[1280,256]{1,0:T(8,128)(2,1)} %bitcast.16), channel_id=1, source_target_pairs={{0,2},{1,3},{2,4},{3,5},{4,6},{5,7},{8,10},{9,11},{10,12},{11,13},... | collective-permute-start | bytes 1966088 | tf_op jit(solution)/shard_map/ppermute | solution.py:423
  10.7 1.3 %copy-start.2 = (bf16[1,1,16,160,256]{4,3,2,1,0:T(8,128)(2,1)S(1)}, bf16[1,1,16,160,256]{4,3,2,1,0:T(8,128)(2,1)}, u32[]{:S(2)}) copy-start(bf16[1,1,16,160,256]{4,3,2,1,0:T(8,128)(2,1)} %param.5) | copy-start | bytes 3932164
  12.0 1.0 %copy-start.3 = (bf16[3,256,256]{2,1,0:T(8,128)(2,1)S(1)}, bf16[3,256,256]{2,1,0:T(8,128)(2,1)}, u32[]{:S(2)}) copy-start(bf16[3,256,256]{2,1,0:T(8,128)(2,1)} %refs_7_.1) | copy-start | bytes 1179652
  25.0 5.3 %collective-permute-start.2 = (bf16[1440,256]{1,0:T(8,128)(2,1)S(1)}, bf16[1440,256]{1,0:T(8,128)(2,1)S(1)}, u32[]{:S(2)}, u32[]{:S(2)}) collective-permute-start(bf16[1440,256]{1,0:T(8,128)(2,1)S(1)} %collective-permute-done.1.refs_6_), channel_id=1, source_target_pairs={{0,1},{1,0},{2,3},{3,2},{4,5},{5,4},{6,7},{7,6},{8,9},{9,8},{10,11... | collective-permute-start | bytes 2211848 | tf_op jit(solution)/shard_map/ppermute | solution.py:441
  25.5 4.9 %copy-start.4 = (bf16[3,256,256]{2,1,0:T(8,128)(2,1)S(1)}, bf16[3,256,256]{2,1,0:T(8,128)(2,1)}, u32[]{:S(2)}) copy-start(bf16[3,256,256]{2,1,0:T(8,128)(2,1)} %refs_7_.1) | copy-start | bytes 1179652
  35.7 2.6 %collective-permute-start.5 = (bf16[4,384,256]{2,1,0:T(8,128)(2,1)}, bf16[4,384,256]{2,1,0:T(8,128)(2,1)S(1)}, u32[]{:S(2)}, u32[]{:S(2)}) collective-permute-start(bf16[4,384,256]{2,1,0:T(8,128)(2,1)} %get-tuple-element.59), channel_id=1, source_target_pairs={{0,1},{1,0},{2,3},{3,2},{4,5},{5,4},{6,7},{7,6},{8,9},{9,8},{10,11... | collective-permute-start | bytes 2359304 | tf_op jit(solution)/shard_map/ppermute | solution.py:473
  35.8 22.6 %collective-permute-start.4 = (bf16[1120,256]{1,0:T(8,128)(2,1)}, bf16[1120,256]{1,0:T(8,128)(2,1)S(1)}, u32[]{:S(2)}, u32[]{:S(2)}) collective-permute-start(bf16[1120,256]{1,0:T(8,128)(2,1)} %get-tuple-element.57), channel_id=1, source_target_pairs={{2,0},{3,1},{4,2},{5,3},{6,4},{7,5},{10,8},{11,9},{12,10},{13,11},... | collective-permute-start | bytes 1720328 | tf_op jit(solution)/shard_map/ppermute | solution.py:481
  39.7 7.8 %collective-permute-start.6 = (bf16[4,96,256]{2,1,0:T(8,128)(2,1)S(1)}, bf16[4,96,256]{2,1,0:T(8,128)(2,1)S(1)}, u32[]{:S(2)}, u32[]{:S(2)}) collective-permute-start(bf16[4,96,256]{2,1,0:T(8,128)(2,1)S(1)} %get-tuple-element.63), channel_id=1, source_target_pairs={{0,8},{8,0},{16,24},{24,16},{1,9},{9,1},{17,25},{25,17},{2,10},{10... | collective-permute-start | bytes 589832 | tf_op jit(solution)/shard_map/ppermute | solution.py:480
  41.4 10.9 %collective-permute-start.7 = (bf16[4,96,256]{2,1,0:T(8,128)(2,1)S(1)}, bf16[4,96,256]{2,1,0:T(8,128)(2,1)S(1)}, u32[]{:S(2)}, u32[]{:S(2)}) collective-permute-start(bf16[4,96,256]{2,1,0:T(8,128)(2,1)S(1)} %get-tuple-element.64), channel_id=1, source_target_pairs={{0,16},{8,24},{16,0},{24,8},{1,17},{9,25},{17,1},{25,9},{2,18},{10... | collective-permute-start | bytes 589832 | tf_op jit(solution)/shard_map/ppermute | solution.py:480
  42.9 9.4 %collective-permute-start.8 = (bf16[4,96,256]{2,1,0:T(8,128)(2,1)S(1)}, bf16[4,96,256]{2,1,0:T(8,128)(2,1)S(1)}, u32[]{:S(2)}, u32[]{:S(2)}) collective-permute-start(bf16[4,96,256]{2,1,0:T(8,128)(2,1)S(1)} %get-tuple-element.65), channel_id=1, source_target_pairs={{0,24},{8,16},{16,8},{24,0},{1,25},{9,17},{17,9},{25,1},{2,26},{10... | collective-permute-start | bytes 589832 | tf_op jit(solution)/shard_map/ppermute | solution.py:480
  53.1 9.2 %collective-permute-start.9 = (bf16[96,256]{1,0:T(8,128)(2,1)S(1)}, bf16[96,256]{1,0:T(8,128)(2,1)S(1)}, u32[]{:S(2)}, u32[]{:S(2)}) collective-permute-start(bf16[96,256]{1,0:T(8,128)(2,1)S(1)} %get-tuple-element.70), channel_id=1, source_target_pairs={{0,6},{1,7},{2,4},{3,5},{4,2},{5,3},{6,0},{7,1},{8,14},{9,15},{10,... | collective-permute-start | bytes 147464 | tf_op jit(solution)/shard_map/ppermute | solution.py:493
  57.8 5.0 %collective-permute-start.10 = (bf16[96,256]{1,0:T(8,128)(2,1)S(1)}, bf16[96,256]{1,0:T(8,128)(2,1)S(1)}, u32[]{:S(2)}, u32[]{:S(2)}) collective-permute-start(bf16[96,256]{1,0:T(8,128)(2,1)S(1)} %get-tuple-element.71), channel_id=1, source_target_pairs={{0,4},{1,5},{2,6},{3,7},{4,0},{5,1},{6,2},{7,3},{8,12},{9,13},{10,... | collective-permute-start | bytes 147464 | tf_op jit(solution)/shard_map/ppermute | solution.py:493
  57.8 5.0 %collective-permute-start.11 = (bf16[96,256]{1,0:T(8,128)(2,1)S(1)}, bf16[96,256]{1,0:T(8,128)(2,1)S(1)}, u32[]{:S(2)}, u32[]{:S(2)}) collective-permute-start(bf16[96,256]{1,0:T(8,128)(2,1)S(1)} %get-tuple-element.72), channel_id=1, source_target_pairs={{0,2},{1,3},{2,0},{3,1},{4,6},{5,7},{6,4},{7,5},{8,10},{9,11},{10,... | collective-permute-start | bytes 147464 | tf_op jit(solution)/shard_map/ppermute | solution.py:493
  63.4 5.0 %collective-permute-start.14 = (bf16[96,256]{1,0:T(8,128)(2,1)S(1)}, bf16[96,256]{1,0:T(8,128)(2,1)S(1)}, u32[]{:S(2)}, u32[]{:S(2)}) collective-permute-start(bf16[96,256]{1,0:T(8,128)(2,1)S(1)} %get-tuple-element.74.refs_1_), channel_id=1, source_target_pairs={{24,0},{16,8},{8,16},{0,24},{25,1},{17,9},{9,17},{1,25},{26,2},{18... | collective-permute-start | bytes 147464 | tf_op jit(solution)/shard_map/ppermute | solution.py:505
  64.9 4.1 %collective-permute-start.13 = (bf16[96,256]{1,0:T(8,128)(2,1)S(1)}, bf16[96,256]{1,0:T(8,128)(2,1)S(1)}, u32[]{:S(2)}, u32[]{:S(2)}) collective-permute-start(bf16[96,256]{1,0:T(8,128)(2,1)S(1)} %get-tuple-element.74.refs_1_), channel_id=1, source_target_pairs={{16,0},{24,8},{0,16},{8,24},{17,1},{25,9},{1,17},{9,25},{18,2},{26... | collective-permute-start | bytes 147464 | tf_op jit(solution)/shard_map/ppermute | solution.py:505
  66.1 4.1 %collective-permute-start.12 = (bf16[96,256]{1,0:T(8,128)(2,1)S(1)}, bf16[96,256]{1,0:T(8,128)(2,1)S(1)}, u32[]{:S(2)}, u32[]{:S(2)}) collective-permute-start(bf16[96,256]{1,0:T(8,128)(2,1)S(1)} %get-tuple-element.74.refs_1_), channel_id=1, source_target_pairs={{8,0},{0,8},{24,16},{16,24},{9,1},{1,9},{25,17},{17,25},{10,2},{2,... | collective-permute-start | bytes 147464 | tf_op jit(solution)/shard_map/ppermute | solution.py:505

commit v7 on v6

--- a/solution.py
+++ b/solution.py
@@ -45,13 +45,12 @@
     def body(*refs):
         rest = refs[n_in + len(after) :]
         kernel(*refs[:n_in], *rest[:n_out], *rest[n_out + 1 :])
-        rest[n_out][...] = jnp.zeros(TOKEN.shape, TOKEN.dtype)
 
     return pl.pallas_call(
         body,
         out_shape=[*outs, TOKEN],
-        in_specs=[SPACE[c] for c in ins] + [SPACE["v"]] * len(after),
-        out_specs=[SPACE[c] for c in results] + [SPACE["v"]],
+        in_specs=[SPACE[c] for c in ins] + [SPACE["h"]] * len(after),
+        out_specs=[SPACE[c] for c in results] + [SPACE["h"]],
         scratch_shapes=[*(pltpu.VMEM(s.shape, s.dtype) for s in scratch), *([pltpu.SemaphoreType.DMA((copies,))] if copies else [])],
         input_output_aliases={} if alias is None else alias,
         compiler_params=pltpu.CompilerParams(vmem_limit_bytes=limit),
@@ -361,15 +360,12 @@
 
 
 def level_kernel(size, where, own, *refs):
-    got = refs[: -size - 2]
-    mine, *sends = refs[-size - 2 : -2]
-    got_v, sems = refs[-2:]
+    got = refs[:-size]
+    mine, *sends = refs[-size:]
     level = where[0]
-    copies = Copies(sems)
-    wait_all(copies.start(*((g, got_v.at[k]) for k, g in enumerate(got))))
 
     def total(i):
-        return sum((got_v[k, i].astype(F32) for k in range(len(got))), own[i])
+        return sum((g[i].astype(F32) for g in got), own[i])
 
     mine[...] = total(level)
     for k, out in enumerate(sends, 1):
@@ -485,9 +481,9 @@
     )
     level_piece = (rs + rt, chans)
     own, *sends, token = call(
-        functools.partial(level_kernel, levels), "level", "sv" + "h" * (dp - 1) + " " + "v" * levels, mac // 8,
+        functools.partial(level_kernel, levels), "level", "sv" + "v" * (dp - 1) + " " + "v" * levels, mac // 8,
         [level, own, *got], [like(F32, *level_piece)] + [like(BF16, *level_piece)] * (levels - 1),
-        [like(BF16, dp - 1, *piece)], copies=dp - 1, after=[token],
+        after=[token],
     )
     got = [
         lax.ppermute(s, "seq", [(i, 2 * peer(i // 2, k, levels) + i % 2) for i in range(seq)])

time: 71.3 us -> 69.4 us (0.973)
  Pallas kernels: 29.2 us -> 27.3 us
    pallas_call x9, Pallas kernels: 29.2 us -> 27.3 us  [call(): pl.pallas_call(body, out_shape=[*outs, TOKEN], in_specs=[SPACE[c] for c i...]
  transfers between devices with their start and end apart: 15 -> 15, of which waited for: 9 -> 9; matrix products, arithmetic and copies ran while one was open for 4% -> 5% of each run, Pallas kernels for 32% -> 32%
where the time goes in v7:
time: 69.4 us; the launch traced here: 69.1 us
  Pallas kernels  27.3 us (39%)
  starting transfers between devices  20.9 us (30%)
  waiting for transfers between devices  14.6 us (21%)
  local copies, waits for them, and re-layouts  5.44 us (8%)
  between operations  0.8 us (1%)
    pallas_call x9, Pallas kernels, call(): pl.pallas_call(body, out_shape=[*outs, TOKEN], in_specs=[SPACE[c] for c i...  27.3 us
    ppermute x3, waiting for transfers between devices, shards(): lax.ppermute(s, 'dp', [(i, peer(i, k, dp)) for i in range(dp)])  5.31 us
    ppermute x3, starting transfers between devices, shards(): lax.ppermute(s, 'seq', [(i, 2 * peer(i // 2, k, levels) + i % 2) for i in...  5.29 us
    ppermute x1, starting transfers between devices, shards(): above = lax.ppermute(above, 'seq', up)  5.09 us
    ppermute x1, waiting for transfers between devices, shards(): far = lax.ppermute(cot[:upper * width], 'seq', down)  4.25 us
    ppermute x3, starting transfers between devices, shards(): lax.ppermute(small, 'dp', [(peer(i, k, dp), i) for i in range(dp)])  3.55 us
    ppermute x3, starting transfers between devices, shards(): lax.ppermute(s, 'dp', [(i, peer(i, k, dp)) for i in range(dp)])  3.55 us
    ppermute x3, waiting for transfers between devices, shards(): lax.ppermute(small, 'dp', [(peer(i, k, dp), i) for i in range(dp)])  3.29 us
  transfers between devices with their start and end apart: 15, of which 9 were waited for; matrix products, arithmetic and copies ran while one was open for 5% of the time, Pallas kernels for 32%

profile of v7, /device:TPU:0, one launch (start us, length us, event | category | flops | bytes accessed | tf_op | source)
XLA Modules:
  0.0 69.1 jit_solution(11668058233954131691)
XLA Ops:
  1.2 2.2 %slice.14 = bf16[1,1,9,160,256]{4,3,2,1,0:T(8,128)(2,1)} slice(bf16[1,1,16,160,256]{4,3,2,1,0:T(8,128)(2,1)} %param.5), slice={[0:1], [0:1], [0:9], [0:160], [0:256]} | slice | bytes 1474560 | tf_op jit(solution)/shard_map/slice | solution.py:417
  3.4 1.3 %collective-permute-start.1 = (bf16[1440,256]{1,0:T(8,128)(2,1)}, bf16[1440,256]{1,0:T(8,128)(2,1)S(1)}, u32[]{:S(2)}, u32[]{:S(2)}) collective-permute-start(bf16[1440,256]{1,0:T(8,128)(2,1)} %bitcast.4), channel_id=1, source_target_pairs={{2,0},{3,1},{4,2},{5,3},{6,4},{7,5},{10,8},{11,9},{12,10},{13,11},... | collective-permute-start | bytes 2211848 | tf_op jit(solution)/shard_map/ppermute | solution.py:417
  4.7 0.9 %slice.12 = bf16[1,1,8,160,256]{4,3,2,1,0:T(8,128)(2,1)} slice(bf16[1,1,16,160,256]{4,3,2,1,0:T(8,128)(2,1)S(1)} %copy-done.1), slice={[0:1], [0:1], [8:16], [0:160], [0:256]} | slice | bytes 1310720 | tf_op jit(solution)/shard_map/slice | solution.py:418
  5.6 5.1 %collective-permute-start.3 = (bf16[1280,256]{1,0:T(8,128)(2,1)}, bf16[1280,256]{1,0:T(8,128)(2,1)S(1)}, u32[]{:S(2)}, u32[]{:S(2)}) collective-permute-start(bf16[1280,256]{1,0:T(8,128)(2,1)} %bitcast.16), channel_id=1, source_target_pairs={{0,2},{1,3},{2,4},{3,5},{4,6},{5,7},{8,10},{9,11},{10,12},{11,13},... | collective-permute-start | bytes 1966088 | tf_op jit(solution)/shard_map/ppermute | solution.py:419
  10.7 1.3 %copy-done.2 = bf16[1,1,16,160,256]{4,3,2,1,0:T(8,128)(2,1)S(1)} copy-done((bf16[1,1,16,160,256]{4,3,2,1,0:T(8,128)(2,1)S(1)}, bf16[1,1,16,160,256]{4,3,2,1,0:T(8,128)(2,1)}, u32[]{:S(2)}) %copy-start.2) | copy-done | bytes 1310744
  12.0 1.0 %copy-done.3 = bf16[3,256,256]{2,1,0:T(8,128)(2,1)S(1)} copy-done((bf16[3,256,256]{2,1,0:T(8,128)(2,1)S(1)}, bf16[3,256,256]{2,1,0:T(8,128)(2,1)}, u32[]{:S(2)}) %copy-start.3) | copy-done | bytes 393240
  13.0 7.7 %local.1 = (bf16[1440,256]{1,0:T(8,128)(2,1)S(1)}, f32[1440,256]{1,0:T(8,128)S(1)}, f32[1440,256]{1,0:T(8,128)S(1)}, f32[1120,256]{1,0:T(8,128)S(1)}, f32[9,256,...) custom-call(s32[1]{0:T(128)} %bitcast.refs_0_, ...), custom_call_target="tpu_custom_call" | custom-call | flops 5704253440 | bytes 14663684 | tf_op jit(solution)/shard_map/local/pallas_call | solution.py:49
  20.8 4.2 %collective-permute-done.1.refs_6_ = bf16[1440,256]{1,0:T(8,128)(2,1)S(1)} collective-permute-done((bf16[1440,256]{1,0:T(8,128)(2,1)}, bf16[1440,256]{1,0:T(8,128)(2,1)S(1)}, u32[]{:S(2)}, u32[]{:S(2)}) %collective-permute-start.1) | collective-permute-done | bytes 737312 | tf_op jit(solution)/shard_map/ppermute | solution.py:417
  25.5 4.9 %remote.1 = (f32[9,256,256]{2,1,0:T(8,128)S(1)}, f32[3,256,256]{2,1,0:T(8,128)S(1)}, bf16[1120,256]{1,0:T(8,128)(2,1)}, f32[8,128]{1,0:T(8,128)S(1)}) custom-call(s32[1]{0:T(128)} %bitcast.refs_0_, bf16[1280,256]{1,0:T(8,128)(2,1)S(1)} %collective-permute-done.3.refs_1_, bf16[2560,256]{1,0:T(8,128)(2,1)S(1)} %bitcast.14, ...), custom_call_target="tpu_custom_call" | custom-call | flops 2684354560 | bytes 12468228 | tf_op jit(solution)/shard_map/remote/pallas_call | solution.py:49
  30.4 4.7 %own.1 = (bf16[90112,256]{1,0:T(8,128)(2,1)}, f32[45056,256]{1,0:T(8,128)}, bf16[4,384,256]{2,1,0:T(8,128)(2,1)}, f32[8,128]{1,0:T(8,128)}) custom-call(s32[1]{0:T(128)} %bitcast.refs_0_, bf16[2560,256]{1,0:T(8,128)(2,1)S(1)} %bitcast.11, bf16[1440,256]{1,0:T(8,128)(2,1)S(1)} %get-tuple-element.41.refs_2_, ...), custom_call_target="tpu_custom_call", output_to_operand_aliasing={{0}: (10, {})} | custom-call | flops 2684354560 | bytes 10797060 | tf_op jit(solution)/shard_map/own/pallas_call | solution.py:49
  35.2 1.5 %collective-permute-start.4 = (bf16[1120,256]{1,0:T(8,128)(2,1)}, bf16[1120,256]{1,0:T(8,128)(2,1)S(1)}, u32[]{:S(2)}, u32[]{:S(2)}) collective-permute-start(bf16[1120,256]{1,0:T(8,128)(2,1)} %get-tuple-element.57), channel_id=1, source_target_pairs={{2,0},{3,1},{4,2},{5,3},{6,4},{7,5},{10,8},{11,9},{12,10},{13,11},... | collective-permute-start | bytes 1720328 | tf_op jit(solution)/shard_map/ppermute | solution.py:477
  36.7 0.9 %collective-permute-done.5.refs_2_ = bf16[4,384,256]{2,1,0:T(8,128)(2,1)S(1)} collective-permute-done((bf16[4,384,256]{2,1,0:T(8,128)(2,1)}, bf16[4,384,256]{2,1,0:T(8,128)(2,1)S(1)}, u32[]{:S(2)}, u32[]{:S(2)}) %collective-permute-start.5) | collective-permute-done | bytes 786464 | tf_op jit(solution)/shard_map/ppermute | solution.py:469
  37.6 1.4 %split.1 = (f32[4,96,256]{2,1,0:T(8,128)S(1)}, bf16[4,96,256]{2,1,0:T(8,128)(2,1)S(1)}, bf16[4,96,256]{2,1,0:T(8,128)(2,1)S(1)}, bf16[4,96,256]{2,1,0:T(8,128)(2,1)S(1)}, f32[8,128]{1,0:T(8,128)S(1)}) custom-call(s32[1]{0:T(128)} %bitcast.5.refs_0_, f32[45056,256]{1,0:T(8,128)} %get-tuple-element.58.refs_1_, ...), custom_call_target="tpu_custom_call" | custom-call | flops 20971520 | bytes 1769476 | tf_op jit(solution)/shard_map/split/pallas_call | solution.py:49
  39.1 1.7 %collective-permute-start.6 = (bf16[4,96,256]{2,1,0:T(8,128)(2,1)S(1)}, bf16[4,96,256]{2,1,0:T(8,128)(2,1)S(1)}, u32[]{:S(2)}, u32[]{:S(2)}) collective-permute-start(bf16[4,96,256]{2,1,0:T(8,128)(2,1)S(1)} %get-tuple-element.63), channel_id=1, source_target_pairs={{0,8},{8,0},{16,24},{24,16},{1,9},{9,1},{17,25},{25,17},{2,10},{10... | collective-permute-start | bytes 589832 | tf_op jit(solution)/shard_map/ppermute | solution.py:476
  40.8 1.5 %collective-permute-start.7 = (bf16[4,96,256]{2,1,0:T(8,128)(2,1)S(1)}, bf16[4,96,256]{2,1,0:T(8,128)(2,1)S(1)}, u32[]{:S(2)}, u32[]{:S(2)}) collective-permute-start(bf16[4,96,256]{2,1,0:T(8,128)(2,1)S(1)} %get-tuple-element.64), channel_id=1, source_target_pairs={{0,16},{8,24},{16,0},{24,8},{1,17},{9,25},{17,1},{25,9},{2,18},{10... | collective-permute-start | bytes 589832 | tf_op jit(solution)/shard_map/ppermute | solution.py:476
  42.6 3.7 %back_top.1 = (bf16[2560,256]{1,0:T(8,128)(2,1)}, f32[8,128]{1,0:T(8,128)S(1)}) custom-call(bf16[90112,256]{1,0:T(8,128)(2,1)} %get-tuple-element.56.refs_0_, bf16[3,3,256,256]{3,2,1,0:T(8,128)(2,1)S(1)} %copy-done, f32[8,128]{1,0:T(8,128)S(1)} %get-tuple-element.60.refs_2_), custom_call_target="tpu_custom_call" | custom-call | flops 1509949440 | bytes 2490368 | tf_op jit(solution)/shard_map/back_top/pallas_call | solution.py:49
  46.9 4.8 %collective-permute-done.7.refs_3_ = bf16[4,96,256]{2,1,0:T(8,128)(2,1)S(1)} collective-permute-done((bf16[4,96,256]{2,1,0:T(8,128)(2,1)S(1)}, bf16[4,96,256]{2,1,0:T(8,128)(2,1)S(1)}, u32[]{:S(2)}, u32[]{:S(2)}) %collective-permute-start.7) | collective-permute-done | bytes 196640 | tf_op jit(solution)/shard_map/ppermute | solution.py:476
  51.8 4.7 %collective-permute-start.9 = (bf16[96,256]{1,0:T(8,128)(2,1)S(1)}, bf16[96,256]{1,0:T(8,128)(2,1)S(1)}, u32[]{:S(2)}, u32[]{:S(2)}) collective-permute-start(bf16[96,256]{1,0:T(8,128)(2,1)S(1)} %get-tuple-element.70), channel_id=1, source_target_pairs={{0,6},{1,7},{2,4},{3,5},{4,2},{5,3},{6,0},{7,1},{8,14},{9,15},{10,... | collective-permute-start | bytes 147464 | tf_op jit(solution)/shard_map/ppermute | solution.py:489
  57.1 3.9 %back_bottom.1 = (bf16[2560,256]{1,0:T(8,128)(2,1)}, f32[8,128]{1,0:T(8,128)S(1)}) custom-call(bf16[90112,256]{1,0:T(8,128)(2,1)} %get-tuple-element.56.refs_0_, bf16[1120,256]{1,0:T(8,128)(2,1)S(1)} %collective-permute-done.4.refs_1_, bf16[3,3,256,256]{3,2,1,0:T(8,128)(2,1)S(1)} %copy-done, ...), custom_call_target="tpu_custom_call", output_to_operand_aliasing={{0}: (3, {})} | custom-call | flops 1509949440 | bytes 4374528 | tf_op jit(solution)/shard_map/back_bottom/pallas_call | solution.py:49
  61.4 1.6 %collective-permute-start.14 = (bf16[96,256]{1,0:T(8,128)(2,1)S(1)}, bf16[96,256]{1,0:T(8,128)(2,1)S(1)}, u32[]{:S(2)}, u32[]{:S(2)}) collective-permute-start(bf16[96,256]{1,0:T(8,128)(2,1)S(1)} %get-tuple-element.74.refs_1_), channel_id=1, source_target_pairs={{24,0},{16,8},{8,16},{0,24},{25,1},{17,9},{9,17},{1,25},{26,2},{18... | collective-permute-start | bytes 147464 | tf_op jit(solution)/shard_map/ppermute | solution.py:501
  63.0 1.2 %collective-permute-start.13 = (bf16[96,256]{1,0:T(8,128)(2,1)S(1)}, bf16[96,256]{1,0:T(8,128)(2,1)S(1)}, u32[]{:S(2)}, u32[]{:S(2)}) collective-permute-start(bf16[96,256]{1,0:T(8,128)(2,1)S(1)} %get-tuple-element.74.refs_1_), channel_id=1, source_target_pairs={{16,0},{24,8},{0,16},{8,24},{17,1},{25,9},{1,17},{9,25},{18,2},{26... | collective-permute-start | bytes 147464 | tf_op jit(solution)/shard_map/ppermute | solution.py:501
  64.2 0.8 %collective-permute-start.12 = (bf16[96,256]{1,0:T(8,128)(2,1)S(1)}, bf16[96,256]{1,0:T(8,128)(2,1)S(1)}, u32[]{:S(2)}, u32[]{:S(2)}) collective-permute-start(bf16[96,256]{1,0:T(8,128)(2,1)S(1)} %get-tuple-element.74.refs_1_), channel_id=1, source_target_pairs={{8,0},{0,8},{24,16},{16,24},{9,1},{1,9},{25,17},{17,25},{10,2},{2,... | collective-permute-start | bytes 147464 | tf_op jit(solution)/shard_map/ppermute | solution.py:501
  65.0 1.5 %collective-permute-done.14.refs_4_ = bf16[96,256]{1,0:T(8,128)(2,1)S(1)} collective-permute-done((bf16[96,256]{1,0:T(8,128)(2,1)S(1)}, bf16[96,256]{1,0:T(8,128)(2,1)S(1)}, u32[]{:S(2)}, u32[]{:S(2)}) %collective-permute-start.14) | collective-permute-done | bytes 49184 | tf_op jit(solution)/shard_map/ppermute | solution.py:501
  67.1 1.2 %collective-permute-done.12.refs_2_ = bf16[96,256]{1,0:T(8,128)(2,1)S(1)} collective-permute-done((bf16[96,256]{1,0:T(8,128)(2,1)S(1)}, bf16[96,256]{1,0:T(8,128)(2,1)S(1)}, u32[]{:S(2)}, u32[]{:S(2)}) %collective-permute-start.12) | collective-permute-done | bytes 49184 | tf_op jit(solution)/shard_map/ppermute | solution.py:501
  (27 shorter events, 4.5 us)
Async XLA Ops:
  0.6 4.1 %copy-start.1 = (bf16[1,1,16,160,256]{4,3,2,1,0:T(8,128)(2,1)S(1)}, bf16[1,1,16,160,256]{4,3,2,1,0:T(8,128)(2,1)}, u32[]{:S(2)}) copy-start(bf16[1,1,16,160,256]{4,3,2,1,0:T(8,128)(2,1)} %param.4) | copy-start | bytes 3932164
  0.6 10.1 %copy-start = (bf16[3,3,256,256]{3,2,1,0:T(8,128)(2,1)S(1)}, bf16[3,3,256,256]{3,2,1,0:T(8,128)(2,1)}, u32[]{:S(2)}) copy-start(bf16[3,3,256,256]{3,2,1,0:T(8,128)(2,1)} %refs_2_.1) | copy-start | bytes 3538948
  0.6 4.9 %collective-permute-start = (bf16[2560,256]{1,0:T(8,128)(2,1)}, bf16[2560,256]{1,0:T(8,128)(2,1)}, u32[]{:S(2)}, u32[]{:S(2)}) collective-permute-start(bf16[2560,256]{1,0:T(8,128)(2,1)} %bitcast.12), channel_id=1, source_target_pairs={{0,1},{1,0},{2,3},{3,2},{4,5},{5,4},{6,7},{7,6},{8,9},{9,8},{10,11... | collective-permute-start | bytes 3932168 | tf_op jit(solution)/shard_map/ppermute | solution.py:416
  3.4 21.6 %collective-permute-start.1 = (bf16[1440,256]{1,0:T(8,128)(2,1)}, bf16[1440,256]{1,0:T(8,128)(2,1)S(1)}, u32[]{:S(2)}, u32[]{:S(2)}) collective-permute-start(bf16[1440,256]{1,0:T(8,128)(2,1)} %bitcast.4), channel_id=1, source_target_pairs={{2,0},{3,1},{4,2},{5,3},{6,4},{7,5},{10,8},{11,9},{12,10},{13,11},... | collective-permute-start | bytes 2211848 | tf_op jit(solution)/shard_map/ppermute | solution.py:417
  5.6 19.9 %collective-permute-start.3 = (bf16[1280,256]{1,0:T(8,128)(2,1)}, bf16[1280,256]{1,0:T(8,128)(2,1)S(1)}, u32[]{:S(2)}, u32[]{:S(2)}) collective-permute-start(bf16[1280,256]{1,0:T(8,128)(2,1)} %bitcast.16), channel_id=1, source_target_pairs={{0,2},{1,3},{2,4},{3,5},{4,6},{5,7},{8,10},{9,11},{10,12},{11,13},... | collective-permute-start | bytes 1966088 | tf_op jit(solution)/shard_map/ppermute | solution.py:419
  10.7 1.3 %copy-start.2 = (bf16[1,1,16,160,256]{4,3,2,1,0:T(8,128)(2,1)S(1)}, bf16[1,1,16,160,256]{4,3,2,1,0:T(8,128)(2,1)}, u32[]{:S(2)}) copy-start(bf16[1,1,16,160,256]{4,3,2,1,0:T(8,128)(2,1)} %param.5) | copy-start | bytes 3932164
  12.0 1.0 %copy-start.3 = (bf16[3,256,256]{2,1,0:T(8,128)(2,1)S(1)}, bf16[3,256,256]{2,1,0:T(8,128)(2,1)}, u32[]{:S(2)}) copy-start(bf16[3,256,256]{2,1,0:T(8,128)(2,1)} %refs_7_.1) | copy-start | bytes 1179652
  25.0 5.3 %collective-permute-start.2 = (bf16[1440,256]{1,0:T(8,128)(2,1)S(1)}, bf16[1440,256]{1,0:T(8,128)(2,1)S(1)}, u32[]{:S(2)}, u32[]{:S(2)}) collective-permute-start(bf16[1440,256]{1,0:T(8,128)(2,1)S(1)} %collective-permute-done.1.refs_6_), channel_id=1, source_target_pairs={{0,1},{1,0},{2,3},{3,2},{4,5},{5,4},{6,7},{7,6},{8,9},{9,8},{10,11... | collective-permute-start | bytes 2211848 | tf_op jit(solution)/shard_map/ppermute | solution.py:437
  25.5 4.9 %copy-start.4 = (bf16[3,256,256]{2,1,0:T(8,128)(2,1)S(1)}, bf16[3,256,256]{2,1,0:T(8,128)(2,1)}, u32[]{:S(2)}) copy-start(bf16[3,256,256]{2,1,0:T(8,128)(2,1)} %refs_7_.1) | copy-start | bytes 1179652
  35.1 2.6 %collective-permute-start.5 = (bf16[4,384,256]{2,1,0:T(8,128)(2,1)}, bf16[4,384,256]{2,1,0:T(8,128)(2,1)S(1)}, u32[]{:S(2)}, u32[]{:S(2)}) collective-permute-start(bf16[4,384,256]{2,1,0:T(8,128)(2,1)} %get-tuple-element.59), channel_id=1, source_target_pairs={{0,1},{1,0},{2,3},{3,2},{4,5},{5,4},{6,7},{7,6},{8,9},{9,8},{10,11... | collective-permute-start | bytes 2359304 | tf_op jit(solution)/shard_map/ppermute | solution.py:469
  35.2 21.8 %collective-permute-start.4 = (bf16[1120,256]{1,0:T(8,128)(2,1)}, bf16[1120,256]{1,0:T(8,128)(2,1)S(1)}, u32[]{:S(2)}, u32[]{:S(2)}) collective-permute-start(bf16[1120,256]{1,0:T(8,128)(2,1)} %get-tuple-element.57), channel_id=1, source_target_pairs={{2,0},{3,1},{4,2},{5,3},{6,4},{7,5},{10,8},{11,9},{12,10},{13,11},... | collective-permute-start | bytes 1720328 | tf_op jit(solution)/shard_map/ppermute | solution.py:477
  39.1 7.8 %collective-permute-start.6 = (bf16[4,96,256]{2,1,0:T(8,128)(2,1)S(1)}, bf16[4,96,256]{2,1,0:T(8,128)(2,1)S(1)}, u32[]{:S(2)}, u32[]{:S(2)}) collective-permute-start(bf16[4,96,256]{2,1,0:T(8,128)(2,1)S(1)} %get-tuple-element.63), channel_id=1, source_target_pairs={{0,8},{8,0},{16,24},{24,16},{1,9},{9,1},{17,25},{25,17},{2,10},{10... | collective-permute-start | bytes 589832 | tf_op jit(solution)/shard_map/ppermute | solution.py:476
  40.8 10.9 %collective-permute-start.7 = (bf16[4,96,256]{2,1,0:T(8,128)(2,1)S(1)}, bf16[4,96,256]{2,1,0:T(8,128)(2,1)S(1)}, u32[]{:S(2)}, u32[]{:S(2)}) collective-permute-start(bf16[4,96,256]{2,1,0:T(8,128)(2,1)S(1)} %get-tuple-element.64), channel_id=1, source_target_pairs={{0,16},{8,24},{16,0},{24,8},{1,17},{9,25},{17,1},{25,9},{2,18},{10... | collective-permute-start | bytes 589832 | tf_op jit(solution)/shard_map/ppermute | solution.py:476
  42.3 9.4 %collective-permute-start.8 = (bf16[4,96,256]{2,1,0:T(8,128)(2,1)S(1)}, bf16[4,96,256]{2,1,0:T(8,128)(2,1)S(1)}, u32[]{:S(2)}, u32[]{:S(2)}) collective-permute-start(bf16[4,96,256]{2,1,0:T(8,128)(2,1)S(1)} %get-tuple-element.65), channel_id=1, source_target_pairs={{0,24},{8,16},{16,8},{24,0},{1,25},{9,17},{17,9},{25,1},{2,26},{10... | collective-permute-start | bytes 589832 | tf_op jit(solution)/shard_map/ppermute | solution.py:476
  51.8 9.2 %collective-permute-start.9 = (bf16[96,256]{1,0:T(8,128)(2,1)S(1)}, bf16[96,256]{1,0:T(8,128)(2,1)S(1)}, u32[]{:S(2)}, u32[]{:S(2)}) collective-permute-start(bf16[96,256]{1,0:T(8,128)(2,1)S(1)} %get-tuple-element.70), channel_id=1, source_target_pairs={{0,6},{1,7},{2,4},{3,5},{4,2},{5,3},{6,0},{7,1},{8,14},{9,15},{10,... | collective-permute-start | bytes 147464 | tf_op jit(solution)/shard_map/ppermute | solution.py:489
  56.4 5.0 %collective-permute-start.10 = (bf16[96,256]{1,0:T(8,128)(2,1)S(1)}, bf16[96,256]{1,0:T(8,128)(2,1)S(1)}, u32[]{:S(2)}, u32[]{:S(2)}) collective-permute-start(bf16[96,256]{1,0:T(8,128)(2,1)S(1)} %get-tuple-element.71), channel_id=1, source_target_pairs={{0,4},{1,5},{2,6},{3,7},{4,0},{5,1},{6,2},{7,3},{8,12},{9,13},{10,... | collective-permute-start | bytes 147464 | tf_op jit(solution)/shard_map/ppermute | solution.py:489
  56.4 5.0 %collective-permute-start.11 = (bf16[96,256]{1,0:T(8,128)(2,1)S(1)}, bf16[96,256]{1,0:T(8,128)(2,1)S(1)}, u32[]{:S(2)}, u32[]{:S(2)}) collective-permute-start(bf16[96,256]{1,0:T(8,128)(2,1)S(1)} %get-tuple-element.72), channel_id=1, source_target_pairs={{0,2},{1,3},{2,0},{3,1},{4,6},{5,7},{6,4},{7,5},{8,10},{9,11},{10,... | collective-permute-start | bytes 147464 | tf_op jit(solution)/shard_map/ppermute | solution.py:489
  61.4 5.1 %collective-permute-start.14 = (bf16[96,256]{1,0:T(8,128)(2,1)S(1)}, bf16[96,256]{1,0:T(8,128)(2,1)S(1)}, u32[]{:S(2)}, u32[]{:S(2)}) collective-permute-start(bf16[96,256]{1,0:T(8,128)(2,1)S(1)} %get-tuple-element.74.refs_1_), channel_id=1, source_target_pairs={{24,0},{16,8},{8,16},{0,24},{25,1},{17,9},{9,17},{1,25},{26,2},{18... | collective-permute-start | bytes 147464 | tf_op jit(solution)/shard_map/ppermute | solution.py:501
  63.0 4.1 %collective-permute-start.13 = (bf16[96,256]{1,0:T(8,128)(2,1)S(1)}, bf16[96,256]{1,0:T(8,128)(2,1)S(1)}, u32[]{:S(2)}, u32[]{:S(2)}) collective-permute-start(bf16[96,256]{1,0:T(8,128)(2,1)S(1)} %get-tuple-element.74.refs_1_), channel_id=1, source_target_pairs={{16,0},{24,8},{0,16},{8,24},{17,1},{25,9},{1,17},{9,25},{18,2},{26... | collective-permute-start | bytes 147464 | tf_op jit(solution)/shard_map/ppermute | solution.py:501
  64.2 4.1 %collective-permute-start.12 = (bf16[96,256]{1,0:T(8,128)(2,1)S(1)}, bf16[96,256]{1,0:T(8,128)(2,1)S(1)}, u32[]{:S(2)}, u32[]{:S(2)}) collective-permute-start(bf16[96,256]{1,0:T(8,128)(2,1)S(1)} %get-tuple-element.74.refs_1_), channel_id=1, source_target_pairs={{8,0},{0,8},{24,16},{16,24},{9,1},{1,9},{25,17},{17,25},{10,2},{2,... | collective-permute-start | bytes 147464 | tf_op jit(solution)/shard_map/ppermute | solution.py:501

commit v8 on v7

--- a/solution.py
+++ b/solution.py
@@ -487,7 +487,7 @@
     )
     got = [
         lax.ppermute(s, "seq", [(i, 2 * peer(i // 2, k, levels) + i % 2) for i in range(seq)])
-        for k, s in reversed(list(enumerate(sends, 1)))
+        for k, s in sorted(enumerate(sends, 1), key=lambda pair: (pair[0] < levels // 2, pair[0]))
     ]
     back, token = call(
         functools.partial(back_bottom_kernel, rows, width), "back_bottom", "hhhh h", 9 * mac,

time: 69.4 us -> 69.3 us (level)
  no operation moved by 1% of the time
where the time goes in v8:
time: 69.3 us; the launch traced here: 68.9 us
  Pallas kernels  27.3 us (39%)
  starting transfers between devices  20.8 us (30%)
  waiting for transfers between devices  14.6 us (21%)
  local copies, waits for them, and re-layouts  5.44 us (8%)
  between operations  0.8 us (1%)
    pallas_call x9, Pallas kernels, call(): pl.pallas_call(body, out_shape=[*outs, TOKEN], in_specs=[SPACE[c] for c i...  27.3 us
    ppermute x3, waiting for transfers between devices, shards(): lax.ppermute(s, 'dp', [(i, peer(i, k, dp)) for i in range(dp)])  5.31 us
    ppermute x3, starting transfers between devices, shards(): lax.ppermute(s, 'seq', [(i, 2 * peer(i // 2, k, levels) + i % 2) for i in...  5.22 us
    ppermute x1, starting transfers between devices, shards(): above = lax.ppermute(above, 'seq', up)  5.09 us
    ppermute x1, waiting for transfers between devices, shards(): far = lax.ppermute(cot[:upper * width], 'seq', down)  4.25 us
    ppermute x3, starting transfers between devices, shards(): lax.ppermute(small, 'dp', [(peer(i, k, dp), i) for i in range(dp)])  3.55 us
    ppermute x3, starting transfers between devices, shards(): lax.ppermute(s, 'dp', [(i, peer(i, k, dp)) for i in range(dp)])  3.55 us
    ppermute x3, waiting for transfers between devices, shards(): lax.ppermute(small, 'dp', [(peer(i, k, dp), i) for i in range(dp)])  3.29 us
  transfers between devices with their start and end apart: 15, of which 9 were waited for; matrix products, arithmetic and copies ran while one was open for 5% of the time, Pallas kernels for 32%

profile of v8, /device:TPU:0, one launch (start us, length us, event | category | flops | bytes accessed | tf_op | source)
XLA Modules:
  0.0 68.9 jit_solution(1763386230283627983)
XLA Ops:
  1.2 2.2 %slice.14 = bf16[1,1,9,160,256]{4,3,2,1,0:T(8,128)(2,1)} slice(bf16[1,1,16,160,256]{4,3,2,1,0:T(8,128)(2,1)} %param.5), slice={[0:1], [0:1], [0:9], [0:160], [0:256]} | slice | bytes 1474560 | tf_op jit(solution)/shard_map/slice | solution.py:417
  3.4 1.3 %collective-permute-start.1 = (bf16[1440,256]{1,0:T(8,128)(2,1)}, bf16[1440,256]{1,0:T(8,128)(2,1)S(1)}, u32[]{:S(2)}, u32[]{:S(2)}) collective-permute-start(bf16[1440,256]{1,0:T(8,128)(2,1)} %bitcast.4), channel_id=1, source_target_pairs={{2,0},{3,1},{4,2},{5,3},{6,4},{7,5},{10,8},{11,9},{12,10},{13,11},... | collective-permute-start | bytes 2211848 | tf_op jit(solution)/shard_map/ppermute | solution.py:417
  4.7 0.9 %slice.12 = bf16[1,1,8,160,256]{4,3,2,1,0:T(8,128)(2,1)} slice(bf16[1,1,16,160,256]{4,3,2,1,0:T(8,128)(2,1)S(1)} %copy-done.1), slice={[0:1], [0:1], [8:16], [0:160], [0:256]} | slice | bytes 1310720 | tf_op jit(solution)/shard_map/slice | solution.py:418
  5.6 5.1 %collective-permute-start.3 = (bf16[1280,256]{1,0:T(8,128)(2,1)}, bf16[1280,256]{1,0:T(8,128)(2,1)S(1)}, u32[]{:S(2)}, u32[]{:S(2)}) collective-permute-start(bf16[1280,256]{1,0:T(8,128)(2,1)} %bitcast.16), channel_id=1, source_target_pairs={{0,2},{1,3},{2,4},{3,5},{4,6},{5,7},{8,10},{9,11},{10,12},{11,13},... | collective-permute-start | bytes 1966088 | tf_op jit(solution)/shard_map/ppermute | solution.py:419
  10.7 1.3 %copy-done.2 = bf16[1,1,16,160,256]{4,3,2,1,0:T(8,128)(2,1)S(1)} copy-done((bf16[1,1,16,160,256]{4,3,2,1,0:T(8,128)(2,1)S(1)}, bf16[1,1,16,160,256]{4,3,2,1,0:T(8,128)(2,1)}, u32[]{:S(2)}) %copy-start.2) | copy-done | bytes 1310744
  12.0 1.0 %copy-done.3 = bf16[3,256,256]{2,1,0:T(8,128)(2,1)S(1)} copy-done((bf16[3,256,256]{2,1,0:T(8,128)(2,1)S(1)}, bf16[3,256,256]{2,1,0:T(8,128)(2,1)}, u32[]{:S(2)}) %copy-start.3) | copy-done | bytes 393240
  13.0 7.7 %local.1 = (bf16[1440,256]{1,0:T(8,128)(2,1)S(1)}, f32[1440,256]{1,0:T(8,128)S(1)}, f32[1440,256]{1,0:T(8,128)S(1)}, f32[1120,256]{1,0:T(8,128)S(1)}, f32[9,256,...) custom-call(s32[1]{0:T(128)} %bitcast.refs_0_, ...), custom_call_target="tpu_custom_call" | custom-call | flops 5704253440 | bytes 14663684 | tf_op jit(solution)/shard_map/local/pallas_call | solution.py:49
  20.8 4.2 %collective-permute-done.1.refs_6_ = bf16[1440,256]{1,0:T(8,128)(2,1)S(1)} collective-permute-done((bf16[1440,256]{1,0:T(8,128)(2,1)}, bf16[1440,256]{1,0:T(8,128)(2,1)S(1)}, u32[]{:S(2)}, u32[]{:S(2)}) %collective-permute-start.1) | collective-permute-done | bytes 737312 | tf_op jit(solution)/shard_map/ppermute | solution.py:417
  25.5 4.9 %remote.1 = (f32[9,256,256]{2,1,0:T(8,128)S(1)}, f32[3,256,256]{2,1,0:T(8,128)S(1)}, bf16[1120,256]{1,0:T(8,128)(2,1)}, f32[8,128]{1,0:T(8,128)S(1)}) custom-call(s32[1]{0:T(128)} %bitcast.refs_0_, bf16[1280,256]{1,0:T(8,128)(2,1)S(1)} %collective-permute-done.3.refs_1_, bf16[2560,256]{1,0:T(8,128)(2,1)S(1)} %bitcast.14, ...), custom_call_target="tpu_custom_call" | custom-call | flops 2684354560 | bytes 12468228 | tf_op jit(solution)/shard_map/remote/pallas_call | solution.py:49
  30.4 4.7 %own.1 = (bf16[90112,256]{1,0:T(8,128)(2,1)}, f32[45056,256]{1,0:T(8,128)}, bf16[4,384,256]{2,1,0:T(8,128)(2,1)}, f32[8,128]{1,0:T(8,128)}) custom-call(s32[1]{0:T(128)} %bitcast.refs_0_, bf16[2560,256]{1,0:T(8,128)(2,1)S(1)} %bitcast.11, bf16[1440,256]{1,0:T(8,128)(2,1)S(1)} %get-tuple-element.41.refs_2_, ...), custom_call_target="tpu_custom_call", output_to_operand_aliasing={{0}: (10, {})} | custom-call | flops 2684354560 | bytes 10797060 | tf_op jit(solution)/shard_map/own/pallas_call | solution.py:49
  35.2 1.5 %collective-permute-start.4 = (bf16[1120,256]{1,0:T(8,128)(2,1)}, bf16[1120,256]{1,0:T(8,128)(2,1)S(1)}, u32[]{:S(2)}, u32[]{:S(2)}) collective-permute-start(bf16[1120,256]{1,0:T(8,128)(2,1)} %get-tuple-element.57), channel_id=1, source_target_pairs={{2,0},{3,1},{4,2},{5,3},{6,4},{7,5},{10,8},{11,9},{12,10},{13,11},... | collective-permute-start | bytes 1720328 | tf_op jit(solution)/shard_map/ppermute | solution.py:477
  36.7 0.9 %collective-permute-done.5.refs_2_ = bf16[4,384,256]{2,1,0:T(8,128)(2,1)S(1)} collective-permute-done((bf16[4,384,256]{2,1,0:T(8,128)(2,1)}, bf16[4,384,256]{2,1,0:T(8,128)(2,1)S(1)}, u32[]{:S(2)}, u32[]{:S(2)}) %collective-permute-start.5) | collective-permute-done | bytes 786464 | tf_op jit(solution)/shard_map/ppermute | solution.py:469
  37.6 1.4 %split.1 = (f32[4,96,256]{2,1,0:T(8,128)S(1)}, bf16[4,96,256]{2,1,0:T(8,128)(2,1)S(1)}, bf16[4,96,256]{2,1,0:T(8,128)(2,1)S(1)}, bf16[4,96,256]{2,1,0:T(8,128)(2,1)S(1)}, f32[8,128]{1,0:T(8,128)S(1)}) custom-call(s32[1]{0:T(128)} %bitcast.5.refs_0_, f32[45056,256]{1,0:T(8,128)} %get-tuple-element.58.refs_1_, ...), custom_call_target="tpu_custom_call" | custom-call | flops 20971520 | bytes 1769476 | tf_op jit(solution)/shard_map/split/pallas_call | solution.py:49
  39.1 1.7 %collective-permute-start.6 = (bf16[4,96,256]{2,1,0:T(8,128)(2,1)S(1)}, bf16[4,96,256]{2,1,0:T(8,128)(2,1)S(1)}, u32[]{:S(2)}, u32[]{:S(2)}) collective-permute-start(bf16[4,96,256]{2,1,0:T(8,128)(2,1)S(1)} %get-tuple-element.63), channel_id=1, source_target_pairs={{0,8},{8,0},{16,24},{24,16},{1,9},{9,1},{17,25},{25,17},{2,10},{10... | collective-permute-start | bytes 589832 | tf_op jit(solution)/shard_map/ppermute | solution.py:476
  40.8 1.5 %collective-permute-start.7 = (bf16[4,96,256]{2,1,0:T(8,128)(2,1)S(1)}, bf16[4,96,256]{2,1,0:T(8,128)(2,1)S(1)}, u32[]{:S(2)}, u32[]{:S(2)}) collective-permute-start(bf16[4,96,256]{2,1,0:T(8,128)(2,1)S(1)} %get-tuple-element.64), channel_id=1, source_target_pairs={{0,16},{8,24},{16,0},{24,8},{1,17},{9,25},{17,1},{25,9},{2,18},{10... | collective-permute-start | bytes 589832 | tf_op jit(solution)/shard_map/ppermute | solution.py:476
  42.6 3.7 %back_top.1 = (bf16[2560,256]{1,0:T(8,128)(2,1)}, f32[8,128]{1,0:T(8,128)S(1)}) custom-call(bf16[90112,256]{1,0:T(8,128)(2,1)} %get-tuple-element.56.refs_0_, bf16[3,3,256,256]{3,2,1,0:T(8,128)(2,1)S(1)} %copy-done, f32[8,128]{1,0:T(8,128)S(1)} %get-tuple-element.60.refs_2_), custom_call_target="tpu_custom_call" | custom-call | flops 1509949440 | bytes 2490368 | tf_op jit(solution)/shard_map/back_top/pallas_call | solution.py:49
  46.9 4.8 %collective-permute-done.7.refs_3_ = bf16[4,96,256]{2,1,0:T(8,128)(2,1)S(1)} collective-permute-done((bf16[4,96,256]{2,1,0:T(8,128)(2,1)S(1)}, bf16[4,96,256]{2,1,0:T(8,128)(2,1)S(1)}, u32[]{:S(2)}, u32[]{:S(2)}) %collective-permute-start.7) | collective-permute-done | bytes 196640 | tf_op jit(solution)/shard_map/ppermute | solution.py:476
  51.8 3.6 %collective-permute-start.9 = (bf16[96,256]{1,0:T(8,128)(2,1)S(1)}, bf16[96,256]{1,0:T(8,128)(2,1)S(1)}, u32[]{:S(2)}, u32[]{:S(2)}) collective-permute-start(bf16[96,256]{1,0:T(8,128)(2,1)S(1)} %get-tuple-element.70), channel_id=1, source_target_pairs={{0,4},{1,5},{2,6},{3,7},{4,0},{5,1},{6,2},{7,3},{8,12},{9,13},{10,... | collective-permute-start | bytes 147464 | tf_op jit(solution)/shard_map/ppermute | solution.py:489
  55.4 1.2 %collective-permute-start.10 = (bf16[96,256]{1,0:T(8,128)(2,1)S(1)}, bf16[96,256]{1,0:T(8,128)(2,1)S(1)}, u32[]{:S(2)}, u32[]{:S(2)}) collective-permute-start(bf16[96,256]{1,0:T(8,128)(2,1)S(1)} %get-tuple-element.71), channel_id=1, source_target_pairs={{0,6},{1,7},{2,4},{3,5},{4,2},{5,3},{6,0},{7,1},{8,14},{9,15},{10,... | collective-permute-start | bytes 147464 | tf_op jit(solution)/shard_map/ppermute | solution.py:489
  57.0 3.9 %back_bottom.1 = (bf16[2560,256]{1,0:T(8,128)(2,1)}, f32[8,128]{1,0:T(8,128)S(1)}) custom-call(bf16[90112,256]{1,0:T(8,128)(2,1)} %get-tuple-element.56.refs_0_, bf16[1120,256]{1,0:T(8,128)(2,1)S(1)} %collective-permute-done.4.refs_1_, bf16[3,3,256,256]{3,2,1,0:T(8,128)(2,1)S(1)} %copy-done, ...), custom_call_target="tpu_custom_call", output_to_operand_aliasing={{0}: (3, {})} | custom-call | flops 1509949440 | bytes 4374528 | tf_op jit(solution)/shard_map/back_bottom/pallas_call | solution.py:49
  61.3 1.6 %collective-permute-start.14 = (bf16[96,256]{1,0:T(8,128)(2,1)S(1)}, bf16[96,256]{1,0:T(8,128)(2,1)S(1)}, u32[]{:S(2)}, u32[]{:S(2)}) collective-permute-start(bf16[96,256]{1,0:T(8,128)(2,1)S(1)} %get-tuple-element.74.refs_1_), channel_id=1, source_target_pairs={{24,0},{16,8},{8,16},{0,24},{25,1},{17,9},{9,17},{1,25},{26,2},{18... | collective-permute-start | bytes 147464 | tf_op jit(solution)/shard_map/ppermute | solution.py:501
  62.8 1.2 %collective-permute-start.13 = (bf16[96,256]{1,0:T(8,128)(2,1)S(1)}, bf16[96,256]{1,0:T(8,128)(2,1)S(1)}, u32[]{:S(2)}, u32[]{:S(2)}) collective-permute-start(bf16[96,256]{1,0:T(8,128)(2,1)S(1)} %get-tuple-element.74.refs_1_), channel_id=1, source_target_pairs={{16,0},{24,8},{0,16},{8,24},{17,1},{25,9},{1,17},{9,25},{18,2},{26... | collective-permute-start | bytes 147464 | tf_op jit(solution)/shard_map/ppermute | solution.py:501
  64.8 1.5 %collective-permute-done.14.refs_4_ = bf16[96,256]{1,0:T(8,128)(2,1)S(1)} collective-permute-done((bf16[96,256]{1,0:T(8,128)(2,1)S(1)}, bf16[96,256]{1,0:T(8,128)(2,1)S(1)}, u32[]{:S(2)}, u32[]{:S(2)}) %collective-permute-start.14) | collective-permute-done | bytes 49184 | tf_op jit(solution)/shard_map/ppermute | solution.py:501
  66.9 1.2 %collective-permute-done.12.refs_2_ = bf16[96,256]{1,0:T(8,128)(2,1)S(1)} collective-permute-done((bf16[96,256]{1,0:T(8,128)(2,1)S(1)}, bf16[96,256]{1,0:T(8,128)(2,1)S(1)}, u32[]{:S(2)}, u32[]{:S(2)}) %collective-permute-start.12) | collective-permute-done | bytes 49184 | tf_op jit(solution)/shard_map/ppermute | solution.py:501
  (27 shorter events, 5.0 us)
Async XLA Ops:
  0.6 4.1 %copy-start.1 = (bf16[1,1,16,160,256]{4,3,2,1,0:T(8,128)(2,1)S(1)}, bf16[1,1,16,160,256]{4,3,2,1,0:T(8,128)(2,1)}, u32[]{:S(2)}) copy-start(bf16[1,1,16,160,256]{4,3,2,1,0:T(8,128)(2,1)} %param.4) | copy-start | bytes 3932164
  0.6 10.1 %copy-start = (bf16[3,3,256,256]{3,2,1,0:T(8,128)(2,1)S(1)}, bf16[3,3,256,256]{3,2,1,0:T(8,128)(2,1)}, u32[]{:S(2)}) copy-start(bf16[3,3,256,256]{3,2,1,0:T(8,128)(2,1)} %refs_2_.1) | copy-start | bytes 3538948
  0.6 4.9 %collective-permute-start = (bf16[2560,256]{1,0:T(8,128)(2,1)}, bf16[2560,256]{1,0:T(8,128)(2,1)}, u32[]{:S(2)}, u32[]{:S(2)}) collective-permute-start(bf16[2560,256]{1,0:T(8,128)(2,1)} %bitcast.12), channel_id=1, source_target_pairs={{0,1},{1,0},{2,3},{3,2},{4,5},{5,4},{6,7},{7,6},{8,9},{9,8},{10,11... | collective-permute-start | bytes 3932168 | tf_op jit(solution)/shard_map/ppermute | solution.py:416
  3.4 21.6 %collective-permute-start.1 = (bf16[1440,256]{1,0:T(8,128)(2,1)}, bf16[1440,256]{1,0:T(8,128)(2,1)S(1)}, u32[]{:S(2)}, u32[]{:S(2)}) collective-permute-start(bf16[1440,256]{1,0:T(8,128)(2,1)} %bitcast.4), channel_id=1, source_target_pairs={{2,0},{3,1},{4,2},{5,3},{6,4},{7,5},{10,8},{11,9},{12,10},{13,11},... | collective-permute-start | bytes 2211848 | tf_op jit(solution)/shard_map/ppermute | solution.py:417
  5.6 19.9 %collective-permute-start.3 = (bf16[1280,256]{1,0:T(8,128)(2,1)}, bf16[1280,256]{1,0:T(8,128)(2,1)S(1)}, u32[]{:S(2)}, u32[]{:S(2)}) collective-permute-start(bf16[1280,256]{1,0:T(8,128)(2,1)} %bitcast.16), channel_id=1, source_target_pairs={{0,2},{1,3},{2,4},{3,5},{4,6},{5,7},{8,10},{9,11},{10,12},{11,13},... | collective-permute-start | bytes 1966088 | tf_op jit(solution)/shard_map/ppermute | solution.py:419
  10.7 1.3 %copy-start.2 = (bf16[1,1,16,160,256]{4,3,2,1,0:T(8,128)(2,1)S(1)}, bf16[1,1,16,160,256]{4,3,2,1,0:T(8,128)(2,1)}, u32[]{:S(2)}) copy-start(bf16[1,1,16,160,256]{4,3,2,1,0:T(8,128)(2,1)} %param.5) | copy-start | bytes 3932164
  12.0 1.0 %copy-start.3 = (bf16[3,256,256]{2,1,0:T(8,128)(2,1)S(1)}, bf16[3,256,256]{2,1,0:T(8,128)(2,1)}, u32[]{:S(2)}) copy-start(bf16[3,256,256]{2,1,0:T(8,128)(2,1)} %refs_7_.1) | copy-start | bytes 1179652
  25.0 5.3 %collective-permute-start.2 = (bf16[1440,256]{1,0:T(8,128)(2,1)S(1)}, bf16[1440,256]{1,0:T(8,128)(2,1)S(1)}, u32[]{:S(2)}, u32[]{:S(2)}) collective-permute-start(bf16[1440,256]{1,0:T(8,128)(2,1)S(1)} %collective-permute-done.1.refs_6_), channel_id=1, source_target_pairs={{0,1},{1,0},{2,3},{3,2},{4,5},{5,4},{6,7},{7,6},{8,9},{9,8},{10,11... | collective-permute-start | bytes 2211848 | tf_op jit(solution)/shard_map/ppermute | solution.py:437
  25.5 4.9 %copy-start.4 = (bf16[3,256,256]{2,1,0:T(8,128)(2,1)S(1)}, bf16[3,256,256]{2,1,0:T(8,128)(2,1)}, u32[]{:S(2)}) copy-start(bf16[3,256,256]{2,1,0:T(8,128)(2,1)} %refs_7_.1) | copy-start | bytes 1179652
  35.1 2.6 %collective-permute-start.5 = (bf16[4,384,256]{2,1,0:T(8,128)(2,1)}, bf16[4,384,256]{2,1,0:T(8,128)(2,1)S(1)}, u32[]{:S(2)}, u32[]{:S(2)}) collective-permute-start(bf16[4,384,256]{2,1,0:T(8,128)(2,1)} %get-tuple-element.59), channel_id=1, source_target_pairs={{0,1},{1,0},{2,3},{3,2},{4,5},{5,4},{6,7},{7,6},{8,9},{9,8},{10,11... | collective-permute-start | bytes 2359304 | tf_op jit(solution)/shard_map/ppermute | solution.py:469
  35.2 21.8 %collective-permute-start.4 = (bf16[1120,256]{1,0:T(8,128)(2,1)}, bf16[1120,256]{1,0:T(8,128)(2,1)S(1)}, u32[]{:S(2)}, u32[]{:S(2)}) collective-permute-start(bf16[1120,256]{1,0:T(8,128)(2,1)} %get-tuple-element.57), channel_id=1, source_target_pairs={{2,0},{3,1},{4,2},{5,3},{6,4},{7,5},{10,8},{11,9},{12,10},{13,11},... | collective-permute-start | bytes 1720328 | tf_op jit(solution)/shard_map/ppermute | solution.py:477
  39.1 7.8 %collective-permute-start.6 = (bf16[4,96,256]{2,1,0:T(8,128)(2,1)S(1)}, bf16[4,96,256]{2,1,0:T(8,128)(2,1)S(1)}, u32[]{:S(2)}, u32[]{:S(2)}) collective-permute-start(bf16[4,96,256]{2,1,0:T(8,128)(2,1)S(1)} %get-tuple-element.63), channel_id=1, source_target_pairs={{0,8},{8,0},{16,24},{24,16},{1,9},{9,1},{17,25},{25,17},{2,10},{10... | collective-permute-start | bytes 589832 | tf_op jit(solution)/shard_map/ppermute | solution.py:476
  40.8 10.9 %collective-permute-start.7 = (bf16[4,96,256]{2,1,0:T(8,128)(2,1)S(1)}, bf16[4,96,256]{2,1,0:T(8,128)(2,1)S(1)}, u32[]{:S(2)}, u32[]{:S(2)}) collective-permute-start(bf16[4,96,256]{2,1,0:T(8,128)(2,1)S(1)} %get-tuple-element.64), channel_id=1, source_target_pairs={{0,16},{8,24},{16,0},{24,8},{1,17},{9,25},{17,1},{25,9},{2,18},{10... | collective-permute-start | bytes 589832 | tf_op jit(solution)/shard_map/ppermute | solution.py:476
  42.3 9.4 %collective-permute-start.8 = (bf16[4,96,256]{2,1,0:T(8,128)(2,1)S(1)}, bf16[4,96,256]{2,1,0:T(8,128)(2,1)S(1)}, u32[]{:S(2)}, u32[]{:S(2)}) collective-permute-start(bf16[4,96,256]{2,1,0:T(8,128)(2,1)S(1)} %get-tuple-element.65), channel_id=1, source_target_pairs={{0,24},{8,16},{16,8},{24,0},{1,25},{9,17},{17,9},{25,1},{2,26},{10... | collective-permute-start | bytes 589832 | tf_op jit(solution)/shard_map/ppermute | solution.py:476
  51.8 9.1 %collective-permute-start.9 = (bf16[96,256]{1,0:T(8,128)(2,1)S(1)}, bf16[96,256]{1,0:T(8,128)(2,1)S(1)}, u32[]{:S(2)}, u32[]{:S(2)}) collective-permute-start(bf16[96,256]{1,0:T(8,128)(2,1)S(1)} %get-tuple-element.70), channel_id=1, source_target_pairs={{0,4},{1,5},{2,6},{3,7},{4,0},{5,1},{6,2},{7,3},{8,12},{9,13},{10,... | collective-permute-start | bytes 147464 | tf_op jit(solution)/shard_map/ppermute | solution.py:489
  55.4 5.9 %collective-permute-start.10 = (bf16[96,256]{1,0:T(8,128)(2,1)S(1)}, bf16[96,256]{1,0:T(8,128)(2,1)S(1)}, u32[]{:S(2)}, u32[]{:S(2)}) collective-permute-start(bf16[96,256]{1,0:T(8,128)(2,1)S(1)} %get-tuple-element.71), channel_id=1, source_target_pairs={{0,6},{1,7},{2,4},{3,5},{4,2},{5,3},{6,0},{7,1},{8,14},{9,15},{10,... | collective-permute-start | bytes 147464 | tf_op jit(solution)/shard_map/ppermute | solution.py:489
  56.6 4.7 %collective-permute-start.11 = (bf16[96,256]{1,0:T(8,128)(2,1)S(1)}, bf16[96,256]{1,0:T(8,128)(2,1)S(1)}, u32[]{:S(2)}, u32[]{:S(2)}) collective-permute-start(bf16[96,256]{1,0:T(8,128)(2,1)S(1)} %get-tuple-element.72), channel_id=1, source_target_pairs={{0,2},{1,3},{2,0},{3,1},{4,6},{5,7},{6,4},{7,5},{8,10},{9,11},{10,... | collective-permute-start | bytes 147464 | tf_op jit(solution)/shard_map/ppermute | solution.py:489
  61.3 5.1 %collective-permute-start.14 = (bf16[96,256]{1,0:T(8,128)(2,1)S(1)}, bf16[96,256]{1,0:T(8,128)(2,1)S(1)}, u32[]{:S(2)}, u32[]{:S(2)}) collective-permute-start(bf16[96,256]{1,0:T(8,128)(2,1)S(1)} %get-tuple-element.74.refs_1_), channel_id=1, source_target_pairs={{24,0},{16,8},{8,16},{0,24},{25,1},{17,9},{9,17},{1,25},{26,2},{18... | collective-permute-start | bytes 147464 | tf_op jit(solution)/shard_map/ppermute | solution.py:501
  62.8 4.1 %collective-permute-start.13 = (bf16[96,256]{1,0:T(8,128)(2,1)S(1)}, bf16[96,256]{1,0:T(8,128)(2,1)S(1)}, u32[]{:S(2)}, u32[]{:S(2)}) collective-permute-start(bf16[96,256]{1,0:T(8,128)(2,1)S(1)} %get-tuple-element.74.refs_1_), channel_id=1, source_target_pairs={{16,0},{24,8},{0,16},{8,24},{17,1},{25,9},{1,17},{9,25},{18,2},{26... | collective-permute-start | bytes 147464 | tf_op jit(solution)/shard_map/ppermute | solution.py:501
  64.0 4.1 %collective-permute-start.12 = (bf16[96,256]{1,0:T(8,128)(2,1)S(1)}, bf16[96,256]{1,0:T(8,128)(2,1)S(1)}, u32[]{:S(2)}, u32[]{:S(2)}) collective-permute-start(bf16[96,256]{1,0:T(8,128)(2,1)S(1)} %get-tuple-element.74.refs_1_), channel_id=1, source_target_pairs={{8,0},{0,8},{24,16},{16,24},{9,1},{1,9},{25,17},{17,25},{10,2},{2,... | collective-permute-start | bytes 147464 | tf_op jit(solution)/shard_map/ppermute | solution.py:501
